TPU v7x, 128 devices: a whole 4x4x4 slice. The times are simulated.
128 devices in a mesh: blk: 16 (over y, z_lo, core), head: 8 (over z_hi, x).
Axes of the slice: x: 4, y: 4, z: 4 (z_hi: 2, z_lo: 2; z = z_hi * 2 + z_lo), core: 2. Of those that a mesh axis runs over, the one named last changes fastest.
Arguments:
- queries: bfloat16 [10240, 1024], P(('blk', 'head')), may hold values from -96 to 96
- keys: bfloat16 [10240, 1024], P(('blk', 'head')), may hold values from -18 to 18
- values: bfloat16 [10240, 1024], P(('blk', 'head')), may hold values from -6 to 6
- out_grad: bfloat16 [10240, 1024], P(('blk', 'head')), may hold values from -6 to 6
- doc_ids: int32 [10240], P('blk'), may hold values from 0 to 63, never falling along the last dimension, each value on 1 to 7680 neighbouring positions
Outputs:
- grad_queries: bfloat16 [10240, 1024], P(('blk', 'head'))
- grad_keys: bfloat16 [10240, 1024], P(('blk', 'head'))
- grad_values: bfloat16 [10240, 1024], P(('blk', 'head'))
Inputs may be any that keep to these rules, and one draw needn't show every extreme that they name: doc_ids never falls along the window; each document holds 1 to 7680 frames and one holds exactly 7680.
All inputs are finite; a program needn't handle non-finite values.
Results may differ from a plain program's by a relative error of at most 0.0085.
Values may be sent and summed in bfloat16 or wider, within the bound.
No kernel may reach another device: no remote copies, remote signals or barrier semaphores. Data moves between devices by JAX's collectives and lax.ppermute only.
A program may use at most 64 MiB of HBM per device.

v0:
```python
import math

import jax
import jax.numpy as jnp
from jax import lax
from jax.sharding import PartitionSpec as P

HD = 64


masked_score = -1e30


def passed_along(array, axis, by):
    count = lax.axis_size(axis)
    return lax.ppermute(array, axis, [(i, (i + by) % count) for i in range(count)])


def tile_grads(
    query_part, grad_part, query_docs, log_total, row_dot, key_part, value_part, key_docs
):
    score_scale = 1.0 / math.sqrt(HD)
    scores = (
        jnp.einsum("qhd,khd->hqk", query_part, key_part, preferred_element_type=jnp.float32)
        * score_scale
    )
    prob_grad = jnp.einsum(
        "qhd,khd->hqk", grad_part, value_part, preferred_element_type=jnp.float32
    )
    same_doc = (query_docs[:, None] == key_docs[None, :])[None]
    probs = jnp.where(same_doc, jnp.exp(scores - log_total[:, :, None]), 0.0)
    rounded_probs = probs.astype(jnp.bfloat16)
    grad_value = jnp.einsum(
        "hqk,qhd->khd", rounded_probs, grad_part, preferred_element_type=jnp.float32
    )
    score_grad = (score_scale * probs * (prob_grad - row_dot[:, :, None])).astype(jnp.bfloat16)
    grad_query = jnp.einsum(
        "hqk,khd->qhd", score_grad, key_part, preferred_element_type=jnp.float32
    )
    grad_key = jnp.einsum(
        "hqk,qhd->khd", score_grad, query_part, preferred_element_type=jnp.float32
    )
    return (grad_query, grad_key, grad_value)


def guarded_grads(
    query_part, grad_part, query_docs, log_total, row_dot, key_part, value_part, key_docs
):
    return tile_grads(
        query_part, grad_part, query_docs, log_total, row_dot, key_part, value_part, key_docs
    )


def body(queries, keys, values, out_grad, doc_ids):
    query_loc, key_loc, value_loc, grad_loc = (
        lax.all_to_all(queries, "head", split_axis=1, concat_axis=0, tiled=True),
        lax.all_to_all(keys, "head", split_axis=1, concat_axis=0, tiled=True),
        lax.all_to_all(values, "head", split_axis=1, concat_axis=0, tiled=True),
        lax.all_to_all(out_grad, "head", split_axis=1, concat_axis=0, tiled=True),
    )
    row_count = query_loc.shape[0]
    head_count = query_loc.shape[1] // HD
    query_three = query_loc.reshape(row_count, head_count, HD)
    key_three = key_loc.reshape(row_count, head_count, HD)
    value_three = value_loc.reshape(row_count, head_count, HD)
    grad_three = grad_loc.reshape(row_count, head_count, HD)
    score_scale = 1.0 / math.sqrt(HD)
    turns = lax.axis_size("blk")

    def update_stats(totals, tile_set):
        key_part, value_part, key_docs = tile_set
        run_max, run_sum, run_dot = totals
        scores = (
            jnp.einsum("qhd,khd->hqk", query_three, key_part, preferred_element_type=jnp.float32)
            * score_scale
        )
        prob_grad = jnp.einsum(
            "qhd,khd->hqk", grad_three, value_part, preferred_element_type=jnp.float32
        )
        same_doc = (doc_ids[:, None] == key_docs[None, :])[None]
        new_max = jnp.maximum(run_max, jnp.max(jnp.where(same_doc, scores, masked_score), axis=2))
        rescale = jnp.exp(run_max - new_max)
        weights = jnp.where(same_doc, jnp.exp(scores - new_max[:, :, None]), 0.0)
        return (
            (
                new_max,
                run_sum * rescale + jnp.sum(weights, axis=2),
                run_dot * rescale + jnp.sum(weights * prob_grad, axis=2),
            ),
            None,
        )

    initial = (
        jnp.full((head_count, row_count), masked_score, jnp.float32),
        jnp.zeros((head_count, row_count), jnp.float32),
        jnp.zeros((head_count, row_count), jnp.float32),
    )
    totals = initial
    key_part = lax.all_gather(key_three, "blk", axis=0, tiled=True)
    value_part = lax.all_gather(value_three, "blk", axis=0, tiled=True)
    key_docs = lax.all_gather(doc_ids, "blk", axis=0, tiled=True)
    length = key_part.shape[0]
    block_count = length // row_count
    blocks = (
        key_part.reshape(block_count, row_count, head_count, HD),
        value_part.reshape(block_count, row_count, head_count, HD),
        key_docs.reshape(block_count, row_count),
    )
    totals, unused = lax.scan(update_stats, totals, blocks)
    run_max, run_sum, run_dot = totals
    log_total = run_max + jnp.log(run_sum)
    row_dot = run_dot / run_sum
    zero_grads = jnp.zeros((row_count, head_count, HD), jnp.float32)

    def key_turn(turn, cycle_state):
        key_now, value_now, docs_now, grad_key, grad_value, grad_query = cycle_state
        partials = guarded_grads(
            query_three, grad_three, doc_ids, log_total, row_dot, key_now, value_now, docs_now
        )
        grad_query = grad_query + partials[0]
        grad_key = grad_key + partials[1]
        grad_value = grad_value + partials[2]
        key_now, value_now, docs_now, grad_key, grad_value = (
            passed_along(key_now.astype(jnp.float32), "blk", 1).astype(key_now.dtype),
            passed_along(value_now.astype(jnp.float32), "blk", 1).astype(value_now.dtype),
            passed_along(docs_now, "blk", 1),
            passed_along(grad_key, "blk", 1),
            passed_along(grad_value, "blk", 1),
        )
        return (key_now, value_now, docs_now, grad_key, grad_value, grad_query)

    final_state = lax.fori_loop(
        0, turns, key_turn, (key_three, value_three, doc_ids, zero_grads, zero_grads, zero_grads)
    )
    grad_key, grad_value, grad_query = (final_state[3], final_state[4], final_state[5])
    width_local = head_count * HD
    grad_queries, grad_keys, grad_values = (
        lax.all_to_all(
            grad_query.astype(jnp.bfloat16).reshape(row_count, width_local),
            "head",
            split_axis=0,
            concat_axis=1,
            tiled=True,
        ),
        lax.all_to_all(
            grad_key.astype(jnp.bfloat16).reshape(row_count, width_local),
            "head",
            split_axis=0,
            concat_axis=1,
            tiled=True,
        ),
        lax.all_to_all(
            grad_value.astype(jnp.bfloat16).reshape(row_count, width_local),
            "head",
            split_axis=0,
            concat_axis=1,
            tiled=True,
        ),
    )
    return (grad_queries, grad_keys, grad_values)


def solution(mesh):
    return jax.shard_map(
        body,
        mesh=mesh,
        in_specs=(
            P(("blk", "head"), None),
            P(("blk", "head"), None),
            P(("blk", "head"), None),
            P(("blk", "head"), None),
            P("blk"),
        ),
        out_specs=(P(("blk", "head"), None), P(("blk", "head"), None), P(("blk", "head"), None)),
        check_vma=False,
    )
```

profile of v0, /device:TPU:0, one launch (start us, length us, event | category | flops | bytes accessed | tf_op | source)
XLA Modules:
  0.0 617.3 jit_solution(4967280005436181591)
XLA Ops:
  8.1 15.8 %all_to_all.121 = bf16[80,8,128]{2,0,1:T(8,128)(2,1)S(1)} all-to-all(bf16[80,8,128]{2,0,1:T(8,128)(2,1)S(1)} %copy_bitcast_fusion.7), channel_id=1, replica_groups=mesh['blk'=16,'head'=8] {'head'}, dimensions={1} | all-to-all | bytes 327680 | tf_op jit(solution)/shard_map/all_to_all | solution.py:58
  26.0 10.8 %all_to_all.122 = bf16[80,8,128]{2,0,1:T(8,128)(2,1)S(1)} all-to-all(bf16[80,8,128]{2,0,1:T(8,128)(2,1)S(1)} %copy_bitcast_fusion.8), channel_id=1, replica_groups=mesh['blk'=16,'head'=8] {'head'}, dimensions={1} | all-to-all | bytes 327680 | tf_op jit(solution)/shard_map/all_to_all | solution.py:57
  38.6 3.4 all-to-all-start.2
  42.7 7.5 %all-to-all-done.2 = bf16[80,8,128]{2,0,1:T(8,128)(2,1)S(1)} async-done(((bf16[80,8,128]{2,0,1:T(8,128)(2,1)}), bf16[80,8,128]{2,0,1:T(8,128)(2,1)S(1)}, u32[]{:S(2)}, u32[]{:S(2)}) %all-to-all-start.2) | async-done | bytes 163872 | tf_op jit(solution)/shard_map/all_to_all | solution.py:56
  50.2 3.4 all-to-all-start.3
  53.6 19.6 %all-gather = s32[16,1,640]{2,1,0:T(1,128)S(1)} all-gather(s32[1,1,640]{2,1,0:T(1,128)S(1)} %reshape.123), channel_id=1, replica_groups=mesh['blk'=16,'head'=8] {'blk'}, dimensions={0}, use_global_device_ids=true | all-gather | bytes 43520 | tf_op jit(solution)/shard_map/all_gather | solution.py:101
  75.4 3.7 copy.80
  79.0 16.9 %all-gather.4.cloned.1.call-done = bf16[10240,2,64]{0,2,1:T(8,128)(2,1)} async-done(((bf16[640,2,64]{0,2,1:T(8,128)(2,1)}), bf16[10240,2,64]{0,2,1:T(8,128)(2,1)}) %all-gather.4.cloned.1.call-update) | async-done | bytes 2621456 | tf_op jit(solution)/shard_map/all_gather | solution.py:99
  95.9 3.7 copy.81
  99.6 112.0 %while.36 = (s32[]{:T(128)}, f32[2,640]{1,0:T(2,128)S(1)}, f32[2,640]{1,0:T(2,128)S(1)}, f32[2,640]{1,0:T(2,128)S(1)}, s32[640]{0:T(1024)S(1)}, /*index=5*/s32[1...) while((s32[]{:T(128)}, f32[2,640]{1,0:T(2,128)S(1)}, ...), condition=%wide.region_4.5_spmd.clone, body=%wide.region_0.4_spmd.clone.sunk | while | flops 219964160 | bytes 16159960 | solution.py:109
  212.4 356.7 %while.37 = (s32[]{:T(128)}, bf16[640,2,64]{0,2,1:T(8,128)(2,1)}, bf16[640,2,64]{0,2,1:T(8,128)(2,1)}, s32[640]{0:T(1024)S(1)}, f32[640,2,64]{0,2,1:T(8,128)S(1)...) while((s32[]{:T(128)}, bf16[640,2,64]{0,2,1:T(8,128)(2,1)}, ...), condition=%wide.region_6.7_spmd.clone, body=%wide.region_5.6_spmd.clone.sunk | while | flops 534036480 | bytes 28954108 | solution.py:132
  225.0 8.9 %collective-permute-done.2 = s32[640]{0:T(1024)S(1)} collective-permute-done((s32[640]{0:T(1024)S(1)}, s32[640]{0:T(1024)S(1)}, u32[]{:S(2)}, u32[]{:S(2)}) %collective-permute-start.2) | collective-permute-done | bytes 2592 | tf_op jit(solution)/shard_map/while/body/eval_jaxpr/ppermute | solution.py:16
  240.5 2.8 fusion.91
  245.9 10.3 %collective-permute-done.2 = s32[640]{0:T(1024)S(1)} collective-permute-done((s32[640]{0:T(1024)S(1)}, s32[640]{0:T(1024)S(1)}, u32[]{:S(2)}, u32[]{:S(2)}) %collective-permute-start.2) | collective-permute-done | bytes 2592 | tf_op jit(solution)/shard_map/while/body/eval_jaxpr/ppermute | solution.py:16
  262.7 2.8 fusion.91
  266.9 11.5 %collective-permute-done.2 = s32[640]{0:T(1024)S(1)} collective-permute-done((s32[640]{0:T(1024)S(1)}, s32[640]{0:T(1024)S(1)}, u32[]{:S(2)}, u32[]{:S(2)}) %collective-permute-start.2) | collective-permute-done | bytes 2592 | tf_op jit(solution)/shard_map/while/body/eval_jaxpr/ppermute | solution.py:16
  284.9 2.8 fusion.91
  288.5 12.1 %collective-permute-done.2 = s32[640]{0:T(1024)S(1)} collective-permute-done((s32[640]{0:T(1024)S(1)}, s32[640]{0:T(1024)S(1)}, u32[]{:S(2)}, u32[]{:S(2)}) %collective-permute-start.2) | collective-permute-done | bytes 2592 | tf_op jit(solution)/shard_map/while/body/eval_jaxpr/ppermute | solution.py:16
  307.2 2.8 fusion.91
  310.7 12.1 %collective-permute-done.2 = s32[640]{0:T(1024)S(1)} collective-permute-done((s32[640]{0:T(1024)S(1)}, s32[640]{0:T(1024)S(1)}, u32[]{:S(2)}, u32[]{:S(2)}) %collective-permute-start.2) | collective-permute-done | bytes 2592 | tf_op jit(solution)/shard_map/while/body/eval_jaxpr/ppermute | solution.py:16
  329.4 2.8 fusion.91
  333.0 12.1 %collective-permute-done.2 = s32[640]{0:T(1024)S(1)} collective-permute-done((s32[640]{0:T(1024)S(1)}, s32[640]{0:T(1024)S(1)}, u32[]{:S(2)}, u32[]{:S(2)}) %collective-permute-start.2) | collective-permute-done | bytes 2592 | tf_op jit(solution)/shard_map/while/body/eval_jaxpr/ppermute | solution.py:16
  351.6 2.8 fusion.91
  355.2 12.1 %collective-permute-done.2 = s32[640]{0:T(1024)S(1)} collective-permute-done((s32[640]{0:T(1024)S(1)}, s32[640]{0:T(1024)S(1)}, u32[]{:S(2)}, u32[]{:S(2)}) %collective-permute-start.2) | collective-permute-done | bytes 2592 | tf_op jit(solution)/shard_map/while/body/eval_jaxpr/ppermute | solution.py:16
  373.9 2.8 fusion.91
  377.4 12.1 %collective-permute-done.2 = s32[640]{0:T(1024)S(1)} collective-permute-done((s32[640]{0:T(1024)S(1)}, s32[640]{0:T(1024)S(1)}, u32[]{:S(2)}, u32[]{:S(2)}) %collective-permute-start.2) | collective-permute-done | bytes 2592 | tf_op jit(solution)/shard_map/while/body/eval_jaxpr/ppermute | solution.py:16
  396.1 2.8 fusion.91
  399.6 12.1 %collective-permute-done.2 = s32[640]{0:T(1024)S(1)} collective-permute-done((s32[640]{0:T(1024)S(1)}, s32[640]{0:T(1024)S(1)}, u32[]{:S(2)}, u32[]{:S(2)}) %collective-permute-start.2) | collective-permute-done | bytes 2592 | tf_op jit(solution)/shard_map/while/body/eval_jaxpr/ppermute | solution.py:16
  418.3 2.8 fusion.91
  421.9 12.1 %collective-permute-done.2 = s32[640]{0:T(1024)S(1)} collective-permute-done((s32[640]{0:T(1024)S(1)}, s32[640]{0:T(1024)S(1)}, u32[]{:S(2)}, u32[]{:S(2)}) %collective-permute-start.2) | collective-permute-done | bytes 2592 | tf_op jit(solution)/shard_map/while/body/eval_jaxpr/ppermute | solution.py:16
  440.5 2.8 fusion.91
  444.1 12.1 %collective-permute-done.2 = s32[640]{0:T(1024)S(1)} collective-permute-done((s32[640]{0:T(1024)S(1)}, s32[640]{0:T(1024)S(1)}, u32[]{:S(2)}, u32[]{:S(2)}) %collective-permute-start.2) | collective-permute-done | bytes 2592 | tf_op jit(solution)/shard_map/while/body/eval_jaxpr/ppermute | solution.py:16
  462.8 2.8 fusion.91
  466.3 12.1 %collective-permute-done.2 = s32[640]{0:T(1024)S(1)} collective-permute-done((s32[640]{0:T(1024)S(1)}, s32[640]{0:T(1024)S(1)}, u32[]{:S(2)}, u32[]{:S(2)}) %collective-permute-start.2) | collective-permute-done | bytes 2592 | tf_op jit(solution)/shard_map/while/body/eval_jaxpr/ppermute | solution.py:16
  485.0 2.8 fusion.91
  488.6 12.1 %collective-permute-done.2 = s32[640]{0:T(1024)S(1)} collective-permute-done((s32[640]{0:T(1024)S(1)}, s32[640]{0:T(1024)S(1)}, u32[]{:S(2)}, u32[]{:S(2)}) %collective-permute-start.2) | collective-permute-done | bytes 2592 | tf_op jit(solution)/shard_map/while/body/eval_jaxpr/ppermute | solution.py:16
  507.2 2.8 fusion.91
  510.8 12.1 %collective-permute-done.2 = s32[640]{0:T(1024)S(1)} collective-permute-done((s32[640]{0:T(1024)S(1)}, s32[640]{0:T(1024)S(1)}, u32[]{:S(2)}, u32[]{:S(2)}) %collective-permute-start.2) | collective-permute-done | bytes 2592 | tf_op jit(solution)/shard_map/while/body/eval_jaxpr/ppermute | solution.py:16
  529.4 2.8 fusion.91
  533.0 12.1 %collective-permute-done.2 = s32[640]{0:T(1024)S(1)} collective-permute-done((s32[640]{0:T(1024)S(1)}, s32[640]{0:T(1024)S(1)}, u32[]{:S(2)}, u32[]{:S(2)}) %collective-permute-start.2) | collective-permute-done | bytes 2592 | tf_op jit(solution)/shard_map/while/body/eval_jaxpr/ppermute | solution.py:16
  551.7 2.8 fusion.91
  555.2 13.2 %collective-permute-done.2 = s32[640]{0:T(1024)S(1)} collective-permute-done((s32[640]{0:T(1024)S(1)}, s32[640]{0:T(1024)S(1)}, u32[]{:S(2)}, u32[]{:S(2)}) %collective-permute-start.2) | collective-permute-done | bytes 2592 | tf_op jit(solution)/shard_map/while/body/eval_jaxpr/ppermute | solution.py:16
  571.2 7.1 %all-to-all-start.6 = ((bf16[8,80,128]{2,1,0:T(8,128)(2,1)}), bf16[8,80,128]{2,1,0:T(8,128)(2,1)S(1)}, u32[]{:S(2)}, u32[]{:S(2)}) async-start(bf16[8,80,128]{2,1,0:T(8,128)(2,1)} %copy.58), calls=%async_computation.6 | async-start | bytes 327680 | tf_op jit(solution)/shard_map/all_to_all | solution.py:152
  581.6 5.0 all-to-all-done.6
  586.6 3.4 all-to-all-start.5
  590.7 7.5 %all-to-all-done.5 = bf16[8,80,128]{2,1,0:T(8,128)(2,1)S(1)} async-done(((bf16[8,80,128]{2,1,0:T(8,128)(2,1)}), bf16[8,80,128]{2,1,0:T(8,128)(2,1)S(1)}, u32[]{:S(2)}, u32[]{:S(2)}) %all-to-all-start.5) | async-done | bytes 163872 | tf_op jit(solution)/shard_map/all_to_all | solution.py:145
  598.2 3.4 all-to-all-start.4
  602.2 7.5 %all-to-all-done.4 = bf16[8,80,128]{2,1,0:T(8,128)(2,1)S(1)} async-done(((bf16[8,80,128]{2,1,0:T(8,128)(2,1)}), bf16[8,80,128]{2,1,0:T(8,128)(2,1)S(1)}, u32[]{:S(2)}, u32[]{:S(2)}) %all-to-all-start.4) | async-done | bytes 163872 | tf_op jit(solution)/shard_map/all_to_all | solution.py:138
  (737 shorter events, 250.0 us)
Async XLA Ops:
  7.2 68.2 %all-gather.6.cloned.1.call-start = ((), (), s32[]{:S(2)}) async-start(), calls=%async_computation.8 | async-start | bytes 2785280 | tf_op jit(solution)/shard_map/all_gather | solution.py:100
  25.0 71.0 %all-gather.4.cloned.1.call-start = ((), (), s32[]{:S(2)}) async-start(), calls=%async_computation.7 | async-start | bytes 2785280 | tf_op jit(solution)/shard_map/all_gather | solution.py:99
  50.2 24.1 %all-to-all-start.3 = ((bf16[80,8,128]{2,0,1:T(8,128)(2,1)}), bf16[80,8,128]{2,0,1:T(8,128)(2,1)S(1)}, u32[]{:S(2)}, u32[]{:S(2)}) async-start(bf16[80,8,128]{2,0,1:T(8,128)(2,1)} %copy_bitcast_fusion.5), calls=%async_computation.3 | async-start | bytes 327680 | tf_op jit(solution)/shard_map/all_to_all | solution.py:59
  218.2 15.8 %collective-permute-start.3 = (f32[640,2,64]{0,2,1:T(8,128)S(1)}, f32[640,2,64]{0,2,1:T(8,128)S(1)}, u32[]{:S(2)}, u32[]{:S(2)}) collective-permute-start(f32[640,2,64]{0,2,1:T(8,128)S(1)} %fusion.90), channel_id=1, source_target_pairs={{0,8},{8,16},{16,24},{24,32},{32,40},{40,48},{48,56},{56,64},{64,7... | collective-permute-start | bytes 983048 | tf_op jit(solution)/shard_map/while/body/eval_jaxpr/ppermute | solution.py:16
  240.4 15.8 %collective-permute-start.3 = (f32[640,2,64]{0,2,1:T(8,128)S(1)}, f32[640,2,64]{0,2,1:T(8,128)S(1)}, u32[]{:S(2)}, u32[]{:S(2)}) collective-permute-start(f32[640,2,64]{0,2,1:T(8,128)S(1)} %fusion.90), channel_id=1, source_target_pairs={{0,8},{8,16},{16,24},{24,32},{32,40},{40,48},{48,56},{56,64},{64,7... | collective-permute-start | bytes 983048 | tf_op jit(solution)/shard_map/while/body/eval_jaxpr/ppermute | solution.py:16
  243.3 12.9 %collective-permute-start.4 = (f32[640,2,64]{0,2,1:T(8,128)}, f32[640,2,64]{0,2,1:T(8,128)}, u32[]{:S(2)}, u32[]{:S(2)}) collective-permute-start(f32[640,2,64]{0,2,1:T(8,128)} %fusion.91), channel_id=1, source_target_pairs={{0,8},{8,16},{16,24},{24,32},{32,40},{40,48},{48,56},{56,64},{64,7... | collective-permute-start | bytes 983048 | tf_op jit(solution)/shard_map/while/body/eval_jaxpr/ppermute | solution.py:16
  262.6 15.8 %collective-permute-start.3 = (f32[640,2,64]{0,2,1:T(8,128)S(1)}, f32[640,2,64]{0,2,1:T(8,128)S(1)}, u32[]{:S(2)}, u32[]{:S(2)}) collective-permute-start(f32[640,2,64]{0,2,1:T(8,128)S(1)} %fusion.90), channel_id=1, source_target_pairs={{0,8},{8,16},{16,24},{24,32},{32,40},{40,48},{48,56},{56,64},{64,7... | collective-permute-start | bytes 983048 | tf_op jit(solution)/shard_map/while/body/eval_jaxpr/ppermute | solution.py:16
  265.5 12.9 %collective-permute-start.4 = (f32[640,2,64]{0,2,1:T(8,128)}, f32[640,2,64]{0,2,1:T(8,128)}, u32[]{:S(2)}, u32[]{:S(2)}) collective-permute-start(f32[640,2,64]{0,2,1:T(8,128)} %fusion.91), channel_id=1, source_target_pairs={{0,8},{8,16},{16,24},{24,32},{32,40},{40,48},{48,56},{56,64},{64,7... | collective-permute-start | bytes 983048 | tf_op jit(solution)/shard_map/while/body/eval_jaxpr/ppermute | solution.py:16
  265.5 12.9 %collective-permute-start = (bf16[640,2,64]{0,2,1:T(8,128)(2,1)S(1)}, bf16[640,2,64]{0,2,1:T(8,128)(2,1)S(1)}, u32[]{:S(2)}, u32[]{:S(2)}) collective-permute-start(bf16[640,2,64]{0,2,1:T(8,128)(2,1)S(1)} %copy.103), channel_id=1, source_target_pairs={{0,8},{8,16},{16,24},{24,32},{32,40},{40,48},{48,56},{56,64},{64,7... | collective-permute-start | bytes 491528 | tf_op jit(solution)/shard_map/while/body/eval_jaxpr/ppermute | solution.py:16
  265.5 12.9 %collective-permute-start.1 = (bf16[640,2,64]{0,2,1:T(8,128)(2,1)S(1)}, bf16[640,2,64]{0,2,1:T(8,128)(2,1)S(1)}, u32[]{:S(2)}, u32[]{:S(2)}) collective-permute-start(bf16[640,2,64]{0,2,1:T(8,128)(2,1)S(1)} %copy.104), channel_id=1, source_target_pairs={{0,8},{8,16},{16,24},{24,32},{32,40},{40,48},{48,56},{56,64},{64,7... | collective-permute-start | bytes 491528 | tf_op jit(solution)/shard_map/while/body/eval_jaxpr/ppermute | solution.py:16
  284.9 15.8 %collective-permute-start.3 = (f32[640,2,64]{0,2,1:T(8,128)S(1)}, f32[640,2,64]{0,2,1:T(8,128)S(1)}, u32[]{:S(2)}, u32[]{:S(2)}) collective-permute-start(f32[640,2,64]{0,2,1:T(8,128)S(1)} %fusion.90), channel_id=1, source_target_pairs={{0,8},{8,16},{16,24},{24,32},{32,40},{40,48},{48,56},{56,64},{64,7... | collective-permute-start | bytes 983048 | tf_op jit(solution)/shard_map/while/body/eval_jaxpr/ppermute | solution.py:16
  287.7 12.9 %collective-permute-start.4 = (f32[640,2,64]{0,2,1:T(8,128)}, f32[640,2,64]{0,2,1:T(8,128)}, u32[]{:S(2)}, u32[]{:S(2)}) collective-permute-start(f32[640,2,64]{0,2,1:T(8,128)} %fusion.91), channel_id=1, source_target_pairs={{0,8},{8,16},{16,24},{24,32},{32,40},{40,48},{48,56},{56,64},{64,7... | collective-permute-start | bytes 983048 | tf_op jit(solution)/shard_map/while/body/eval_jaxpr/ppermute | solution.py:16
  287.7 12.9 %collective-permute-start.1 = (bf16[640,2,64]{0,2,1:T(8,128)(2,1)S(1)}, bf16[640,2,64]{0,2,1:T(8,128)(2,1)S(1)}, u32[]{:S(2)}, u32[]{:S(2)}) collective-permute-start(bf16[640,2,64]{0,2,1:T(8,128)(2,1)S(1)} %copy.104), channel_id=1, source_target_pairs={{0,8},{8,16},{16,24},{24,32},{32,40},{40,48},{48,56},{56,64},{64,7... | collective-permute-start | bytes 491528 | tf_op jit(solution)/shard_map/while/body/eval_jaxpr/ppermute | solution.py:16
  307.1 15.8 %collective-permute-start.3 = (f32[640,2,64]{0,2,1:T(8,128)S(1)}, f32[640,2,64]{0,2,1:T(8,128)S(1)}, u32[]{:S(2)}, u32[]{:S(2)}) collective-permute-start(f32[640,2,64]{0,2,1:T(8,128)S(1)} %fusion.90), channel_id=1, source_target_pairs={{0,8},{8,16},{16,24},{24,32},{32,40},{40,48},{48,56},{56,64},{64,7... | collective-permute-start | bytes 983048 | tf_op jit(solution)/shard_map/while/body/eval_jaxpr/ppermute | solution.py:16
  309.9 12.9 %collective-permute-start.4 = (f32[640,2,64]{0,2,1:T(8,128)}, f32[640,2,64]{0,2,1:T(8,128)}, u32[]{:S(2)}, u32[]{:S(2)}) collective-permute-start(f32[640,2,64]{0,2,1:T(8,128)} %fusion.91), channel_id=1, source_target_pairs={{0,8},{8,16},{16,24},{24,32},{32,40},{40,48},{48,56},{56,64},{64,7... | collective-permute-start | bytes 983048 | tf_op jit(solution)/shard_map/while/body/eval_jaxpr/ppermute | solution.py:16
  329.3 15.8 %collective-permute-start.3 = (f32[640,2,64]{0,2,1:T(8,128)S(1)}, f32[640,2,64]{0,2,1:T(8,128)S(1)}, u32[]{:S(2)}, u32[]{:S(2)}) collective-permute-start(f32[640,2,64]{0,2,1:T(8,128)S(1)} %fusion.90), channel_id=1, source_target_pairs={{0,8},{8,16},{16,24},{24,32},{32,40},{40,48},{48,56},{56,64},{64,7... | collective-permute-start | bytes 983048 | tf_op jit(solution)/shard_map/while/body/eval_jaxpr/ppermute | solution.py:16
  332.2 12.9 %collective-permute-start.4 = (f32[640,2,64]{0,2,1:T(8,128)}, f32[640,2,64]{0,2,1:T(8,128)}, u32[]{:S(2)}, u32[]{:S(2)}) collective-permute-start(f32[640,2,64]{0,2,1:T(8,128)} %fusion.91), channel_id=1, source_target_pairs={{0,8},{8,16},{16,24},{24,32},{32,40},{40,48},{48,56},{56,64},{64,7... | collective-permute-start | bytes 983048 | tf_op jit(solution)/shard_map/while/body/eval_jaxpr/ppermute | solution.py:16
  332.2 12.9 %collective-permute-start.1 = (bf16[640,2,64]{0,2,1:T(8,128)(2,1)S(1)}, bf16[640,2,64]{0,2,1:T(8,128)(2,1)S(1)}, u32[]{:S(2)}, u32[]{:S(2)}) collective-permute-start(bf16[640,2,64]{0,2,1:T(8,128)(2,1)S(1)} %copy.104), channel_id=1, source_target_pairs={{0,8},{8,16},{16,24},{24,32},{32,40},{40,48},{48,56},{56,64},{64,7... | collective-permute-start | bytes 491528 | tf_op jit(solution)/shard_map/while/body/eval_jaxpr/ppermute | solution.py:16
  351.5 15.8 %collective-permute-start.3 = (f32[640,2,64]{0,2,1:T(8,128)S(1)}, f32[640,2,64]{0,2,1:T(8,128)S(1)}, u32[]{:S(2)}, u32[]{:S(2)}) collective-permute-start(f32[640,2,64]{0,2,1:T(8,128)S(1)} %fusion.90), channel_id=1, source_target_pairs={{0,8},{8,16},{16,24},{24,32},{32,40},{40,48},{48,56},{56,64},{64,7... | collective-permute-start | bytes 983048 | tf_op jit(solution)/shard_map/while/body/eval_jaxpr/ppermute | solution.py:16
  354.4 12.9 %collective-permute-start.4 = (f32[640,2,64]{0,2,1:T(8,128)}, f32[640,2,64]{0,2,1:T(8,128)}, u32[]{:S(2)}, u32[]{:S(2)}) collective-permute-start(f32[640,2,64]{0,2,1:T(8,128)} %fusion.91), channel_id=1, source_target_pairs={{0,8},{8,16},{16,24},{24,32},{32,40},{40,48},{48,56},{56,64},{64,7... | collective-permute-start | bytes 983048 | tf_op jit(solution)/shard_map/while/body/eval_jaxpr/ppermute | solution.py:16
  354.4 12.9 %collective-permute-start.1 = (bf16[640,2,64]{0,2,1:T(8,128)(2,1)S(1)}, bf16[640,2,64]{0,2,1:T(8,128)(2,1)S(1)}, u32[]{:S(2)}, u32[]{:S(2)}) collective-permute-start(bf16[640,2,64]{0,2,1:T(8,128)(2,1)S(1)} %copy.104), channel_id=1, source_target_pairs={{0,8},{8,16},{16,24},{24,32},{32,40},{40,48},{48,56},{56,64},{64,7... | collective-permute-start | bytes 491528 | tf_op jit(solution)/shard_map/while/body/eval_jaxpr/ppermute | solution.py:16
  373.8 15.8 %collective-permute-start.3 = (f32[640,2,64]{0,2,1:T(8,128)S(1)}, f32[640,2,64]{0,2,1:T(8,128)S(1)}, u32[]{:S(2)}, u32[]{:S(2)}) collective-permute-start(f32[640,2,64]{0,2,1:T(8,128)S(1)} %fusion.90), channel_id=1, source_target_pairs={{0,8},{8,16},{16,24},{24,32},{32,40},{40,48},{48,56},{56,64},{64,7... | collective-permute-start | bytes 983048 | tf_op jit(solution)/shard_map/while/body/eval_jaxpr/ppermute | solution.py:16
  376.6 12.9 %collective-permute-start.4 = (f32[640,2,64]{0,2,1:T(8,128)}, f32[640,2,64]{0,2,1:T(8,128)}, u32[]{:S(2)}, u32[]{:S(2)}) collective-permute-start(f32[640,2,64]{0,2,1:T(8,128)} %fusion.91), channel_id=1, source_target_pairs={{0,8},{8,16},{16,24},{24,32},{32,40},{40,48},{48,56},{56,64},{64,7... | collective-permute-start | bytes 983048 | tf_op jit(solution)/shard_map/while/body/eval_jaxpr/ppermute | solution.py:16
  396.0 15.8 %collective-permute-start.3 = (f32[640,2,64]{0,2,1:T(8,128)S(1)}, f32[640,2,64]{0,2,1:T(8,128)S(1)}, u32[]{:S(2)}, u32[]{:S(2)}) collective-permute-start(f32[640,2,64]{0,2,1:T(8,128)S(1)} %fusion.90), channel_id=1, source_target_pairs={{0,8},{8,16},{16,24},{24,32},{32,40},{40,48},{48,56},{56,64},{64,7... | collective-permute-start | bytes 983048 | tf_op jit(solution)/shard_map/while/body/eval_jaxpr/ppermute | solution.py:16
  398.8 12.9 %collective-permute-start.4 = (f32[640,2,64]{0,2,1:T(8,128)}, f32[640,2,64]{0,2,1:T(8,128)}, u32[]{:S(2)}, u32[]{:S(2)}) collective-permute-start(f32[640,2,64]{0,2,1:T(8,128)} %fusion.91), channel_id=1, source_target_pairs={{0,8},{8,16},{16,24},{24,32},{32,40},{40,48},{48,56},{56,64},{64,7... | collective-permute-start | bytes 983048 | tf_op jit(solution)/shard_map/while/body/eval_jaxpr/ppermute | solution.py:16
  398.8 12.9 %collective-permute-start.1 = (bf16[640,2,64]{0,2,1:T(8,128)(2,1)S(1)}, bf16[640,2,64]{0,2,1:T(8,128)(2,1)S(1)}, u32[]{:S(2)}, u32[]{:S(2)}) collective-permute-start(bf16[640,2,64]{0,2,1:T(8,128)(2,1)S(1)} %copy.104), channel_id=1, source_target_pairs={{0,8},{8,16},{16,24},{24,32},{32,40},{40,48},{48,56},{56,64},{64,7... | collective-permute-start | bytes 491528 | tf_op jit(solution)/shard_map/while/body/eval_jaxpr/ppermute | solution.py:16
  418.2 15.8 %collective-permute-start.3 = (f32[640,2,64]{0,2,1:T(8,128)S(1)}, f32[640,2,64]{0,2,1:T(8,128)S(1)}, u32[]{:S(2)}, u32[]{:S(2)}) collective-permute-start(f32[640,2,64]{0,2,1:T(8,128)S(1)} %fusion.90), channel_id=1, source_target_pairs={{0,8},{8,16},{16,24},{24,32},{32,40},{40,48},{48,56},{56,64},{64,7... | collective-permute-start | bytes 983048 | tf_op jit(solution)/shard_map/while/body/eval_jaxpr/ppermute | solution.py:16
  421.1 12.9 %collective-permute-start.4 = (f32[640,2,64]{0,2,1:T(8,128)}, f32[640,2,64]{0,2,1:T(8,128)}, u32[]{:S(2)}, u32[]{:S(2)}) collective-permute-start(f32[640,2,64]{0,2,1:T(8,128)} %fusion.91), channel_id=1, source_target_pairs={{0,8},{8,16},{16,24},{24,32},{32,40},{40,48},{48,56},{56,64},{64,7... | collective-permute-start | bytes 983048 | tf_op jit(solution)/shard_map/while/body/eval_jaxpr/ppermute | solution.py:16
  421.1 12.9 %collective-permute-start.1 = (bf16[640,2,64]{0,2,1:T(8,128)(2,1)S(1)}, bf16[640,2,64]{0,2,1:T(8,128)(2,1)S(1)}, u32[]{:S(2)}, u32[]{:S(2)}) collective-permute-start(bf16[640,2,64]{0,2,1:T(8,128)(2,1)S(1)} %copy.104), channel_id=1, source_target_pairs={{0,8},{8,16},{16,24},{24,32},{32,40},{40,48},{48,56},{56,64},{64,7... | collective-permute-start | bytes 491528 | tf_op jit(solution)/shard_map/while/body/eval_jaxpr/ppermute | solution.py:16
  440.4 15.8 %collective-permute-start.3 = (f32[640,2,64]{0,2,1:T(8,128)S(1)}, f32[640,2,64]{0,2,1:T(8,128)S(1)}, u32[]{:S(2)}, u32[]{:S(2)}) collective-permute-start(f32[640,2,64]{0,2,1:T(8,128)S(1)} %fusion.90), channel_id=1, source_target_pairs={{0,8},{8,16},{16,24},{24,32},{32,40},{40,48},{48,56},{56,64},{64,7... | collective-permute-start | bytes 983048 | tf_op jit(solution)/shard_map/while/body/eval_jaxpr/ppermute | solution.py:16
  443.3 12.9 %collective-permute-start.4 = (f32[640,2,64]{0,2,1:T(8,128)}, f32[640,2,64]{0,2,1:T(8,128)}, u32[]{:S(2)}, u32[]{:S(2)}) collective-permute-start(f32[640,2,64]{0,2,1:T(8,128)} %fusion.91), channel_id=1, source_target_pairs={{0,8},{8,16},{16,24},{24,32},{32,40},{40,48},{48,56},{56,64},{64,7... | collective-permute-start | bytes 983048 | tf_op jit(solution)/shard_map/while/body/eval_jaxpr/ppermute | solution.py:16
  462.7 15.8 %collective-permute-start.3 = (f32[640,2,64]{0,2,1:T(8,128)S(1)}, f32[640,2,64]{0,2,1:T(8,128)S(1)}, u32[]{:S(2)}, u32[]{:S(2)}) collective-permute-start(f32[640,2,64]{0,2,1:T(8,128)S(1)} %fusion.90), channel_id=1, source_target_pairs={{0,8},{8,16},{16,24},{24,32},{32,40},{40,48},{48,56},{56,64},{64,7... | collective-permute-start | bytes 983048 | tf_op jit(solution)/shard_map/while/body/eval_jaxpr/ppermute | solution.py:16
  465.5 12.9 %collective-permute-start.4 = (f32[640,2,64]{0,2,1:T(8,128)}, f32[640,2,64]{0,2,1:T(8,128)}, u32[]{:S(2)}, u32[]{:S(2)}) collective-permute-start(f32[640,2,64]{0,2,1:T(8,128)} %fusion.91), channel_id=1, source_target_pairs={{0,8},{8,16},{16,24},{24,32},{32,40},{40,48},{48,56},{56,64},{64,7... | collective-permute-start | bytes 983048 | tf_op jit(solution)/shard_map/while/body/eval_jaxpr/ppermute | solution.py:16
  465.5 12.9 %collective-permute-start.1 = (bf16[640,2,64]{0,2,1:T(8,128)(2,1)S(1)}, bf16[640,2,64]{0,2,1:T(8,128)(2,1)S(1)}, u32[]{:S(2)}, u32[]{:S(2)}) collective-permute-start(bf16[640,2,64]{0,2,1:T(8,128)(2,1)S(1)} %copy.104), channel_id=1, source_target_pairs={{0,8},{8,16},{16,24},{24,32},{32,40},{40,48},{48,56},{56,64},{64,7... | collective-permute-start | bytes 491528 | tf_op jit(solution)/shard_map/while/body/eval_jaxpr/ppermute | solution.py:16
  484.9 15.8 %collective-permute-start.3 = (f32[640,2,64]{0,2,1:T(8,128)S(1)}, f32[640,2,64]{0,2,1:T(8,128)S(1)}, u32[]{:S(2)}, u32[]{:S(2)}) collective-permute-start(f32[640,2,64]{0,2,1:T(8,128)S(1)} %fusion.90), channel_id=1, source_target_pairs={{0,8},{8,16},{16,24},{24,32},{32,40},{40,48},{48,56},{56,64},{64,7... | collective-permute-start | bytes 983048 | tf_op jit(solution)/shard_map/while/body/eval_jaxpr/ppermute | solution.py:16
  487.7 12.9 %collective-permute-start.4 = (f32[640,2,64]{0,2,1:T(8,128)}, f32[640,2,64]{0,2,1:T(8,128)}, u32[]{:S(2)}, u32[]{:S(2)}) collective-permute-start(f32[640,2,64]{0,2,1:T(8,128)} %fusion.91), channel_id=1, source_target_pairs={{0,8},{8,16},{16,24},{24,32},{32,40},{40,48},{48,56},{56,64},{64,7... | collective-permute-start | bytes 983048 | tf_op jit(solution)/shard_map/while/body/eval_jaxpr/ppermute | solution.py:16
  487.8 12.9 %collective-permute-start.1 = (bf16[640,2,64]{0,2,1:T(8,128)(2,1)S(1)}, bf16[640,2,64]{0,2,1:T(8,128)(2,1)S(1)}, u32[]{:S(2)}, u32[]{:S(2)}) collective-permute-start(bf16[640,2,64]{0,2,1:T(8,128)(2,1)S(1)} %copy.104), channel_id=1, source_target_pairs={{0,8},{8,16},{16,24},{24,32},{32,40},{40,48},{48,56},{56,64},{64,7... | collective-permute-start | bytes 491528 | tf_op jit(solution)/shard_map/while/body/eval_jaxpr/ppermute | solution.py:16
  507.1 15.8 %collective-permute-start.3 = (f32[640,2,64]{0,2,1:T(8,128)S(1)}, f32[640,2,64]{0,2,1:T(8,128)S(1)}, u32[]{:S(2)}, u32[]{:S(2)}) collective-permute-start(f32[640,2,64]{0,2,1:T(8,128)S(1)} %fusion.90), channel_id=1, source_target_pairs={{0,8},{8,16},{16,24},{24,32},{32,40},{40,48},{48,56},{56,64},{64,7... | collective-permute-start | bytes 983048 | tf_op jit(solution)/shard_map/while/body/eval_jaxpr/ppermute | solution.py:16
  510.0 12.9 %collective-permute-start.4 = (f32[640,2,64]{0,2,1:T(8,128)}, f32[640,2,64]{0,2,1:T(8,128)}, u32[]{:S(2)}, u32[]{:S(2)}) collective-permute-start(f32[640,2,64]{0,2,1:T(8,128)} %fusion.91), channel_id=1, source_target_pairs={{0,8},{8,16},{16,24},{24,32},{32,40},{40,48},{48,56},{56,64},{64,7... | collective-permute-start | bytes 983048 | tf_op jit(solution)/shard_map/while/body/eval_jaxpr/ppermute | solution.py:16
  529.4 15.8 %collective-permute-start.3 = (f32[640,2,64]{0,2,1:T(8,128)S(1)}, f32[640,2,64]{0,2,1:T(8,128)S(1)}, u32[]{:S(2)}, u32[]{:S(2)}) collective-permute-start(f32[640,2,64]{0,2,1:T(8,128)S(1)} %fusion.90), channel_id=1, source_target_pairs={{0,8},{8,16},{16,24},{24,32},{32,40},{40,48},{48,56},{56,64},{64,7... | collective-permute-start | bytes 983048 | tf_op jit(solution)/shard_map/while/body/eval_jaxpr/ppermute | solution.py:16
  532.2 12.9 %collective-permute-start.4 = (f32[640,2,64]{0,2,1:T(8,128)}, f32[640,2,64]{0,2,1:T(8,128)}, u32[]{:S(2)}, u32[]{:S(2)}) collective-permute-start(f32[640,2,64]{0,2,1:T(8,128)} %fusion.91), channel_id=1, source_target_pairs={{0,8},{8,16},{16,24},{24,32},{32,40},{40,48},{48,56},{56,64},{64,7... | collective-permute-start | bytes 983048 | tf_op jit(solution)/shard_map/while/body/eval_jaxpr/ppermute | solution.py:16
  532.2 12.9 %collective-permute-start.1 = (bf16[640,2,64]{0,2,1:T(8,128)(2,1)S(1)}, bf16[640,2,64]{0,2,1:T(8,128)(2,1)S(1)}, u32[]{:S(2)}, u32[]{:S(2)}) collective-permute-start(bf16[640,2,64]{0,2,1:T(8,128)(2,1)S(1)} %copy.104), channel_id=1, source_target_pairs={{0,8},{8,16},{16,24},{24,32},{32,40},{40,48},{48,56},{56,64},{64,7... | collective-permute-start | bytes 491528 | tf_op jit(solution)/shard_map/while/body/eval_jaxpr/ppermute | solution.py:16
  551.6 16.8 %collective-permute-start.3 = (f32[640,2,64]{0,2,1:T(8,128)S(1)}, f32[640,2,64]{0,2,1:T(8,128)S(1)}, u32[]{:S(2)}, u32[]{:S(2)}) collective-permute-start(f32[640,2,64]{0,2,1:T(8,128)S(1)} %fusion.90), channel_id=1, source_target_pairs={{0,8},{8,16},{16,24},{24,32},{32,40},{40,48},{48,56},{56,64},{64,7... | collective-permute-start | bytes 983048 | tf_op jit(solution)/shard_map/while/body/eval_jaxpr/ppermute | solution.py:16
  554.4 14.0 %collective-permute-start.4 = (f32[640,2,64]{0,2,1:T(8,128)}, f32[640,2,64]{0,2,1:T(8,128)}, u32[]{:S(2)}, u32[]{:S(2)}) collective-permute-start(f32[640,2,64]{0,2,1:T(8,128)} %fusion.91), channel_id=1, source_target_pairs={{0,8},{8,16},{16,24},{24,32},{32,40},{40,48},{48,56},{56,64},{64,7... | collective-permute-start | bytes 983048 | tf_op jit(solution)/shard_map/while/body/eval_jaxpr/ppermute | solution.py:16
  554.4 14.0 %collective-permute-start = (bf16[640,2,64]{0,2,1:T(8,128)(2,1)S(1)}, bf16[640,2,64]{0,2,1:T(8,128)(2,1)S(1)}, u32[]{:S(2)}, u32[]{:S(2)}) collective-permute-start(bf16[640,2,64]{0,2,1:T(8,128)(2,1)S(1)} %copy.103), channel_id=1, source_target_pairs={{0,8},{8,16},{16,24},{24,32},{32,40},{40,48},{48,56},{56,64},{64,7... | collective-permute-start | bytes 491528 | tf_op jit(solution)/shard_map/while/body/eval_jaxpr/ppermute | solution.py:16
  554.4 14.0 %collective-permute-start.1 = (bf16[640,2,64]{0,2,1:T(8,128)(2,1)S(1)}, bf16[640,2,64]{0,2,1:T(8,128)(2,1)S(1)}, u32[]{:S(2)}, u32[]{:S(2)}) collective-permute-start(bf16[640,2,64]{0,2,1:T(8,128)(2,1)S(1)} %copy.104), channel_id=1, source_target_pairs={{0,8},{8,16},{16,24},{24,32},{32,40},{40,48},{48,56},{56,64},{64,7... | collective-permute-start | bytes 491528 | tf_op jit(solution)/shard_map/while/body/eval_jaxpr/ppermute | solution.py:16
  554.4 13.9 %collective-permute-start.2 = (s32[640]{0:T(1024)S(1)}, s32[640]{0:T(1024)S(1)}, u32[]{:S(2)}, u32[]{:S(2)}) collective-permute-start(s32[640]{0:T(1024)S(1)} %copy.105), channel_id=1, source_target_pairs={{0,8},{8,16},{16,24},{24,32},{32,40},{40,48},{48,56},{56,64},{64,7... | collective-permute-start | bytes 7688 | tf_op jit(solution)/shard_map/while/body/eval_jaxpr/ppermute | solution.py:16
  571.2 15.3 %all-to-all-start.6 = ((bf16[8,80,128]{2,1,0:T(8,128)(2,1)}), bf16[8,80,128]{2,1,0:T(8,128)(2,1)S(1)}, u32[]{:S(2)}, u32[]{:S(2)}) async-start(bf16[8,80,128]{2,1,0:T(8,128)(2,1)} %copy.58), calls=%async_computation.6 | async-start | bytes 327680 | tf_op jit(solution)/shard_map/all_to_all | solution.py:152
  (187 other events, 1031.3 us)
Sparse Core Ops, SparseCore 0:
  25.1 33.1 all-gather.5
  60.5 35.3 all-gather.3
where the time goes:
time: 621 us; the launch traced here: 617 us
  waiting for transfers between devices  234 us (38%)
  matrix products  175 us (28%)
  local copies, waits for them, and re-layouts  74.6 us (12%)
  blocking collectives  46.2 us (7%)
  other arithmetic  41.1 us (7%)
  starting transfers between devices  28.9 us (5%)
  between operations  14.3 us (2%)
    ppermute x80, waiting for transfers between devices, passed_along(): lax.ppermute(array, axis, [(i, (i + by) % count) for i in range(count)])  189 us
    while x352, local copies, waits for them, and re-layouts  53.3 us
    dot_general x16, matrix products, tile_grads(): jnp.einsum('hqk,qhd->khd', rounded_probs, grad_part, preferred_element_ty...  44.2 us
    dot_general x16, matrix products, update_stats(): jnp.einsum('qhd,khd->hqk', grad_three, value_part, preferred_element_type...  34.2 us
    dot_general x16, matrix products, update_stats(): jnp.einsum('qhd,khd->hqk', query_three, key_part, preferred_element_type=...  29.2 us
    reduce_sum x16, other arithmetic, update_stats(): jnp.sum(weights, axis=2)  29.1 us
    dot_general x16, matrix products, tile_grads(): jnp.einsum('qhd,khd->hqk', grad_part, value_part, preferred_element_type=...  25.3 us
    dot_general x16, matrix products, tile_grads(): jnp.einsum('qhd,khd->hqk', query_part, key_part, preferred_element_type=j...  24.7 us
  transfers between devices with their start and end apart: 87, of which 21 were waited for; matrix products, arithmetic and copies ran while one was open for 11% of the time, Pallas kernels for 0%

commit v1 on v0

v1 whole, which is shorter than its diff:
```python
import functools
import math

import jax
import jax.numpy as jnp
from jax import lax
from jax.experimental import pallas as pl
from jax.experimental.pallas import tpu as pltpu
from jax.sharding import Mesh
from jax.sharding import PartitionSpec as P

BF = jnp.bfloat16
F32 = jnp.float32
HD = 64
HEADS = 16
ROWS = 80
LONG = 7680
NQ, NK = 5120, 2560
LQ, LK = LONG // 2, LONG // 4
RQ, RK = NQ - LQ, NK - LK
SCALE = 1.0 / math.sqrt(HD)
LOG2_SCALE = SCALE * math.log2(math.e)
NEG = -1e30
BLK = ("y", "zl", "c")
VMEM_LIMIT = 56 << 20


def dot_nt(a, b):
    return lax.dot_general(a, b, (((1,), (1,)), ((), ())), preferred_element_type=F32)


def dot_nn(a, b):
    return lax.dot_general(a, b, (((1,), (0,)), ((), ())), preferred_element_type=F32)


def lane_of(x):
    return lax.broadcasted_iota(jnp.int32, x.shape, x.ndim - 1)


def row_of(x):
    return lax.broadcasted_iota(jnp.int32, x.shape, 0)


def swap_halves(x):
    return pltpu.roll(x, HD, 1)


def vmem_call(kernel, out_shape, scratch=(), smem=0, n_in=0, flops=0, nbytes=0, name=None):
    vm = pl.BlockSpec(memory_space=pltpu.VMEM)
    sm = pl.BlockSpec(memory_space=pltpu.SMEM)
    return pl.pallas_call(
        kernel,
        out_shape=out_shape,
        in_specs=[sm] * smem + [vm] * n_in,
        out_specs=[vm] * len(out_shape),
        scratch_shapes=list(scratch),
        compiler_params=pltpu.CompilerParams(vmem_limit_bytes=VMEM_LIMIT),
        cost_estimate=pl.CostEstimate(flops=flops, bytes_accessed=nbytes, transcendentals=0),
        name=name,
    )


def pack_kernel(q_ref, k_ref, v_ref, g_ref, qg_ref, kv_ref):
    for pair in range(HEADS // 2):
        cols = slice(pair * 128, pair * 128 + 128)
        for a_ref, b_ref, out_ref, copies in ((q_ref, g_ref, qg_ref, 4), (k_ref, v_ref, kv_ref, 2)):
            a = a_ref[:, cols].astype(F32)
            b = b_ref[:, cols].astype(F32)
            low = lane_of(a) < HD
            even = jnp.where(low, a, swap_halves(b)).astype(BF)
            odd = jnp.where(low, swap_halves(a), b).astype(BF)
            for c in range(copies):
                out_ref[2 * pair * copies + c] = even
                out_ref[(2 * pair + 1) * copies + c] = odd


def gather_rows(src_ref, dst_ref, base, off, rows, main):
    def move(i, _):
        at = lax.rem(base + i * 16, rows)
        dst_ref[pl.ds(pl.multiple_of(i * 16, 16), 16), :] = src_ref[
            pl.ds(pl.multiple_of(at, 16), 16), :
        ]
        return 0

    lax.fori_loop(0, rows // 16, move, 0, unroll=8)
    first = dst_ref[0:16, :]
    last = dst_ref[main : main + 16, :]
    early = row_of(first) < off
    dst_ref[0:16, :] = jnp.where(early, last, first)
    dst_ref[main : main + 16, :] = jnp.where(early, first, last)


def halves(x):
    zero = jnp.zeros_like(x)
    low = lane_of(x) < HD
    return jnp.where(low, x, zero), jnp.where(low, zero, x)


def columns_of(doc_row):
    return jnp.broadcast_to(doc_row, (128, doc_row.shape[1])).T


def same_doc(doc_cols, doc_row):
    wide = jnp.concatenate([doc_cols] * (doc_row.shape[1] // 128), axis=1)
    return wide == doc_row


def totals_kernel(
    at_ref, qg_in, kv_in, qdoc_ref, kdoc_ref, lse_ref, dot_ref, qg_ref, kv_ref, kvt_ref, vet_ref, kcol_ref
):
    gather_rows(qg_in, qg_ref, at_ref[0], at_ref[1], NQ, LQ)
    gather_rows(kv_in, kv_ref, at_ref[2], at_ref[3], NK, LK)
    kvt = kv_ref[...].astype(F32).T
    kvt_ref[...] = kvt.astype(BF)
    vet_ref[...] = jnp.where(row_of(kvt) < HD, 1.0, kvt).astype(BF)
    kcol_ref[...] = columns_of(kdoc_ref[...])

    def tile(rows, width, keys, step, doc_row):
        qg = qg_ref[rows, :]
        q0, _ = halves(qg)
        starts = list(range(keys[0], keys[1], step))
        scores, tops, outs = {}, [], []

        def finish(at):
            s = scores.pop(at)
            mask = None
            if doc_row is not None:
                mask = same_doc(kcol_ref[at - LK : at - LK + step, :], doc_row)
                s = jnp.where(mask, s, NEG)
            top = jnp.max(s, axis=0, keepdims=True) * LOG2_SCALE
            p = jnp.exp2(s * LOG2_SCALE - top)
            if mask is not None:
                p = jnp.where(mask, p, 0.0)
            outs.append(dot_nn(vet_ref[:, at : at + step], p.astype(BF)))
            tops.append(top)

        for n, at in enumerate(starts):
            scores[at] = dot_nt(kv_ref[at : at + step, :], q0)
            if n:
                finish(starts[n - 1])
        finish(starts[-1])
        top = functools.reduce(jnp.maximum, tops)
        out = sum(o * jnp.exp2(t - top) for o, t in zip(outs, tops))
        total = out[0:1, :]
        grad_t = qg.astype(F32).T
        dot = jnp.sum(out[HD:, :] * grad_t[HD:, :], axis=0, keepdims=True)
        if doc_row is not None:
            empty = total <= 0.0
            total = jnp.where(empty, 1.0, total)
            top = jnp.where(empty, NEG, top)
        lse_ref[:, rows] = top + jnp.log2(total)
        dot_ref[:, rows] = dot / total

    wide = 768

    def long_tile(t, _):
        tile(pl.ds(pl.multiple_of(t * wide, wide), wide), wide, (0, LK), 384, None)
        return 0

    lax.fori_loop(0, LQ // wide, long_tile, 0)

    def rest_tile(t, _):
        rows = pl.ds(pl.multiple_of(LQ + t * 640, 128), 640)
        docs = qdoc_ref[:, pl.ds(pl.multiple_of(t * 640, 128), 640)]
        tile(rows, 640, (LK, NK), 320, docs)
        return 0

    lax.fori_loop(0, RQ // 640, rest_tile, 0)


def grads_kernel(
    at_ref, qg_ref, kv_ref, kvt_ref, qdoc_ref, kdoc_ref, s0, s1, s2, s3,
    dq_out, dkv_out, lse_ref, dot_ref, kcol_ref, dq_ref, dkv_ref,
):
    lses = [s[0:1, :] for s in (s0, s1, s2, s3)]
    dots = [s[1:2, :] for s in (s0, s1, s2, s3)]
    top = functools.reduce(jnp.maximum, lses)
    shares = [jnp.exp2(one - top) for one in lses]
    total = sum(shares)
    lse_ref[...] = top + jnp.log2(total)
    dot_ref[...] = sum(w * d for w, d in zip(shares, dots)) / total
    kcol_ref[...] = columns_of(kdoc_ref[...])
    dkv_ref[...] = jnp.zeros_like(dkv_ref)

    def tile(rows, keys, step, doc_row):
        q0, g0 = halves(qg_ref[rows, :])
        lse = lse_ref[:, rows]
        dot = dot_ref[:, rows]
        both = jnp.concatenate([g0, q0], axis=0)
        acc = None
        for at in range(keys[0], keys[1], step):
            kv = kv_ref[at : at + step, :]
            p = jnp.exp2(dot_nt(kv, q0) * LOG2_SCALE - lse)
            if doc_row is not None:
                p = jnp.where(same_doc(kcol_ref[at - LK : at - LK + step, :], doc_row), p, 0.0)
            ds = (p * (dot_nt(kv, g0) - dot)).astype(BF)
            dkv_ref[at : at + step, :] += dot_nn(jnp.concatenate([p.astype(BF), ds], axis=1), both)
            part = dot_nn(kvt_ref[0:HD, at : at + step], ds)
            acc = part if acc is None else acc + part
        acc = acc * SCALE
        dq_ref[rows, :] = jnp.concatenate([acc, acc], axis=0).T

    wide = 768

    def long_tile(t, _):
        tile(pl.ds(pl.multiple_of(t * wide, wide), wide), (0, LK), 384, None)
        return 0

    lax.fori_loop(0, LQ // wide, long_tile, 0)

    def rest_tile(t, _):
        rows = pl.ds(pl.multiple_of(LQ + t * 640, 128), 640)
        docs = qdoc_ref[:, pl.ds(pl.multiple_of(t * 640, 128), 640)]
        tile(rows, (LK, NK), 320, docs)
        return 0

    lax.fori_loop(0, RQ // 640, rest_tile, 0)

    def swap_back(ref, off, main):
        first = ref[0:16, :]
        last = ref[main : main + 16, :]
        early = row_of(first) < off
        ref[0:16, :] = jnp.where(early, last, first)
        ref[main : main + 16, :] = jnp.where(early, first, last)

    swap_back(dq_ref, at_ref[1], LQ)
    swap_back(dkv_ref, at_ref[3], LK)
    base_q, base_k = at_ref[0], at_ref[2]

    def sixteen(ref, at, base, rows):
        spot = lax.rem(at + rows - base, rows)
        return ref[pl.ds(pl.multiple_of(spot, 16), 16), :]

    def store_dq(c, _):
        groups = [sixteen(dq_ref, c * ROWS + 16 * n, base_q, NQ) for n in range(5)]
        low = lane_of(groups[0]) < HD
        dq_out[c, 0:16, :] = jnp.where(low, groups[0], groups[1]).astype(BF)
        dq_out[c, 16:32, :] = jnp.where(low, groups[2], groups[3]).astype(BF)
        dq_out[c, 32:48, :] = groups[4].astype(BF)
        return 0

    lax.fori_loop(0, NQ // ROWS, store_dq, 0, unroll=2)

    def store_dkv(c, _):
        for n in range(5):
            one = sixteen(dkv_ref, c * ROWS + 16 * n, base_k, NK)
            dkv_out[c, 16 * n : 16 * n + 16, :] = jnp.where(
                lane_of(one) < HD, one * SCALE, one
            ).astype(BF)
        return 0

    lax.fori_loop(0, NK // ROWS, store_dkv, 0, unroll=2)


def join_kernel(dq_ref, dkv_ref, q_out, k_out, v_out):
    for pair in range(HEADS // 2):
        cols = slice(pair * 128, pair * 128 + 128)
        even, odd = 2 * pair, 2 * pair + 1

        def total(ref, h, copies):
            return sum(ref[h * copies + c].astype(F32) for c in range(copies))

        a, b = total(dq_ref, even, 4), total(dq_ref, odd, 4)
        a_swap, b_swap = swap_halves(a), swap_halves(b)
        low = lane_of(a[0:16]) < HD
        for n in range(5):
            part = slice(16 * (n // 2), 16 * (n // 2) + 16)
            if n % 2 == 0:
                rows = jnp.where(low, a[part], b_swap[part])
            else:
                rows = jnp.where(low, a_swap[part], b[part])
            q_out[16 * n : 16 * n + 16, cols] = rows.astype(BF)
        a, b = total(dkv_ref, even, 2), total(dkv_ref, odd, 2)
        low = lane_of(a) < HD
        k_out[:, cols] = jnp.where(low, a, swap_halves(b)).astype(BF)
        v_out[:, cols] = jnp.where(low, swap_halves(a), b).astype(BF)


def doc_plan(docs, rows, main, long_doc):
    start = jnp.sum((docs < long_doc).astype(jnp.int32))
    off = lax.rem(start, 16)
    base = start - off
    turned = lax.dynamic_slice(jnp.concatenate([docs, docs]), (base,), (rows,))
    early = jnp.arange(16) < off
    rest = jnp.concatenate(
        [jnp.where(early, turned[:16], turned[main : main + 16]), turned[main + 16 :]]
    )
    return base, off, rest.astype(F32).reshape(1, rows - main)


def body(queries, keys, values, out_grad, doc_ids):
    shape = jax.ShapeDtypeStruct
    all_docs = lax.all_gather(doc_ids, BLK, axis=0, tiled=True)
    qg, kv = vmem_call(
        pack_kernel,
        [shape((64, ROWS, 128), BF), shape((32, ROWS, 128), BF)],
        n_in=4,
        name="pack",
    )(queries, keys, values, out_grad)
    kv = lax.all_to_all(kv, BLK + ("zh",), 0, 0, tiled=True).reshape(NK, 128)
    qg = lax.all_to_all(qg, BLK + ("x",), 0, 0, tiled=True).reshape(NQ, 128)

    docs = all_docs.reshape(16, 2, 4, ROWS)
    long_doc = all_docs[all_docs.shape[0] // 2]
    zh, x = lax.axis_index("zh"), lax.axis_index("x")
    q_docs = lax.dynamic_index_in_dim(docs, zh, 1, keepdims=False).reshape(NQ)
    k_docs = lax.dynamic_index_in_dim(docs, x, 2, keepdims=False).reshape(NK)
    base_q, off_q, rest_q = doc_plan(q_docs, NQ, LQ, long_doc)
    base_k, off_k, rest_k = doc_plan(k_docs, NK, LK, long_doc)
    at = jnp.stack([base_q, off_q, base_k, off_k])

    lse, dot, qg, kv, kvt = vmem_call(
        totals_kernel,
        [
            shape((1, NQ), F32),
            shape((1, NQ), F32),
            shape((NQ, 128), BF),
            shape((NK, 128), BF),
            shape((128, NK), BF),
        ],
        scratch=[pltpu.VMEM((128, NK), BF), pltpu.VMEM((RK, 128), F32)],
        smem=1,
        n_in=4,
        name="totals",
    )(at, qg, kv, rest_q, rest_k)
    stats = jnp.concatenate([lse, dot], axis=0)
    others = [
        lax.ppermute(stats, "x", [(i, (i + n) % 4) for i in range(4)]) for n in (1, 2, 3)
    ]
    dq, dkv = vmem_call(
        grads_kernel,
        [shape((64, 48, 128), BF), shape((32, ROWS, 128), BF)],
        scratch=[
            pltpu.VMEM((1, NQ), F32),
            pltpu.VMEM((1, NQ), F32),
            pltpu.VMEM((RK, 128), F32),
            pltpu.VMEM((NQ, 128), F32),
            pltpu.VMEM((NK, 128), F32),
        ],
        smem=1,
        n_in=9,
        name="grads",
    )(at, qg, kv, kvt, rest_q, rest_k, stats, *others)
    dkv = lax.all_to_all(dkv, BLK + ("zh",), 0, 0, tiled=True)
    dq = lax.all_to_all(dq, BLK + ("x",), 0, 0, tiled=True)
    return tuple(
        vmem_call(join_kernel, [shape((ROWS, HEADS * HD), BF)] * 3, n_in=2, name="join")(dq, dkv)
    )


def solution(mesh):
    fine = Mesh(mesh.devices.reshape(4, 2, 2, 2, 4), BLK + ("zh", "x"))
    rows = P(BLK + ("zh", "x"), None)
    return jax.shard_map(
        body,
        mesh=fine,
        in_specs=(rows, rows, rows, rows, P(BLK)),
        out_specs=(rows, rows, rows),
        check_vma=False,
    )
```

time: 621 us -> 167 us (0.27)
  waiting for transfers between devices: 234 us -> 4.32 us
  matrix products: 175 us -> 0 us
  local copies, waits for them, and re-layouts: 74.6 us -> 2.66 us
  Pallas kernels: 0 us -> 49.4 us
  blocking collectives: 46.2 us -> 84.9 us
  other arithmetic: 41.1 us -> 5.62 us
  starting transfers between devices: 28.9 us -> 13.4 us
  between operations: 14.3 us -> 5.91 us
    ppermute x80 -> x3, waiting for transfers between devices: 189 us -> 4.32 us  [body(): lax.ppermute(stats, 'x', [(i, (i + n) % 4) for i in range(4)])]
    dot_general x112 -> x0, matrix products: 175 us -> none  [the longest x16 44.2 us: tile_grads(): jnp.einsum('hqk,qhd->khd', rounded_probs, grad_part, preferred_element_ty...]
    while x352 -> x0, local copies, waits for them, and re-layouts: 53.3 us -> none
    pallas_call x0 -> x4, Pallas kernels: none -> 49.4 us  [the longest x1 27.2 us: body(): vmem_call(grads_kernel, [shape((64, 48, 128), BF), shape((32, ROWS, 128),...]
    all_to_all x2 -> x3, blocking collectives: 26.6 us -> 60.8 us  [the longest x1 22.3 us: body(): kv = lax.all_to_all(kv, BLK + ('zh',), 0, 0, tiled=True).reshape(NK, 128)]
    reduce_sum x16 -> x1, other arithmetic: 29.1 us -> 1.3 us  [doc_plan(): start = jnp.sum((docs < long_doc).astype(jnp.int32))]
    all_to_all x5 -> x1, waiting for transfers between devices: 27.5 us -> 0.01 us  [body(): qg = lax.all_to_all(qg, BLK + ('x',), 0, 0, tiled=True).reshape(NQ, 128)]
    all_gather x2 -> x0, waiting for transfers between devices: 16.9 us -> none  [the longest x1 16.9 us: body(): key_part = lax.all_gather(key_three, 'blk', axis=0, tiled=True)]
  transfers between devices with their start and end apart: 87 -> 4, of which waited for: 21 -> 3; matrix products, arithmetic and copies ran while one was open for 11% -> 3% of each run, Pallas kernels for 0% -> 0%
where the time goes in v1:
time: 167 us; the launch traced here: 166 us
  blocking collectives  84.9 us (51%)
  Pallas kernels  49.4 us (30%)
  starting transfers between devices  13.4 us (8%)
  between operations  5.91 us (4%)
  other arithmetic  5.62 us (3%)
  waiting for transfers between devices  4.32 us (3%)
  local copies, waits for them, and re-layouts  2.66 us (2%)
    pallas_call x1, Pallas kernels, body(): vmem_call(grads_kernel, [shape((64, 48, 128), BF), shape((32, ROWS, 128),...  27.2 us
    all_gather x1, blocking collectives, body(): all_docs = lax.all_gather(doc_ids, BLK, axis=0, tiled=True)  24.1 us
    all_to_all x1, blocking collectives, body(): kv = lax.all_to_all(kv, BLK + ('zh',), 0, 0, tiled=True).reshape(NK, 128)  22.3 us
    all_to_all x1, blocking collectives, body(): dq = lax.all_to_all(dq, BLK + ('x',), 0, 0, tiled=True)  20 us
    all_to_all x1, blocking collectives, body(): dkv = lax.all_to_all(dkv, BLK + ('zh',), 0, 0, tiled=True)  18.5 us
    pallas_call x1, Pallas kernels, body(): vmem_call(totals_kernel, [shape((1, NQ), F32), shape((1, NQ), F32), shape...  17.1 us
    ppermute x3, starting transfers between devices, body(): lax.ppermute(stats, 'x', [(i, (i + n) % 4) for i in range(4)])  7.72 us
    all_to_all x1, starting transfers between devices, body(): qg = lax.all_to_all(qg, BLK + ('x',), 0, 0, tiled=True).reshape(NQ, 128)  5.67 us
  transfers between devices with their start and end apart: 4, of which 3 were waited for; matrix products, arithmetic and copies ran while one was open for 3% of the time, Pallas kernels for 0%

profile of v1, /device:TPU:0, one launch (start us, length us, event | category | flops | bytes accessed | tf_op | source)
XLA Modules:
  0.0 166.2 jit_solution(8633957831811867170)
XLA Ops:
  0.6 2.7 %pack.1 = (bf16[64,80,128]{2,1,0:T(8,128)(2,1)}, bf16[32,80,128]{2,1,0:T(8,128)(2,1)}) custom-call(bf16[80,1024]{1,0:T(8,128)(2,1)} %q_ref.1, bf16[80,1024]{1,0:T(8,128)(2,1)} %k_ref.1, bf16[80,1024]{1,0:T(8,128)(2,1)} %v_ref.1, bf16[80,1024]{1,0:T(8,128)(2,1)} %g_ref.1), custom_call_target="tpu_custom_call" | custom-call | tf_op jit(solution)/shard_map/pack/pallas_call | solution.py:294
  3.4 22.3 %all_to_all.20 = bf16[32,80,128]{2,1,0:T(8,128)(2,1)} all-to-all(bf16[32,80,128]{2,1,0:T(8,128)(2,1)} %get-tuple-element.13), channel_id=1, replica_groups=mesh['y'=4,'zl'=2,'c'=2,'zh'=2,'x'=4] {'y','zl','c','zh'}, dimensions={0} | all-to-all | bytes 1310720 | tf_op jit(solution)/shard_map/all_to_all | solution.py:300
  25.7 0.0 copy-start.6
  25.7 5.7 %all-to-all-start = ((bf16[64,80,128]{2,1,0:T(8,128)(2,1)}), bf16[64,80,128]{2,1,0:T(8,128)(2,1)S(1)}, u32[]{:S(2)}, u32[]{:S(2)}) async-start(bf16[64,80,128]{2,1,0:T(8,128)(2,1)} %get-tuple-element.12), calls=%async_computation | async-start | bytes 2621440 | tf_op jit(solution)/shard_map/all_to_all | solution.py:301
  31.3 0.0 copy-done.6
  31.4 24.1 %all-gather = s32[16,1,640]{2,1,0:T(1,128)S(1)} all-gather(s32[1,1,640]{2,1,0:T(1,128)S(1)} %reshape.88), channel_id=1, replica_groups=mesh['y'=4,'zl'=2,'c'=2,'zh'=2,'x'=4] {'y','zl','c'}, dimensions={0}, use_global_device_ids=true | all-gather | bytes 43520 | tf_op jit(solution)/shard_map/all_gather | solution.py:293
  55.5 0.1 reduce.2
  55.6 0.5 slice.28
  56.1 0.1 reshape.83
  56.2 1.3 dynamic-slice_reduce_fusion
  58.8 1.3 convert_reduce_fusion
  64.0 0.1 reshape.86
  64.1 0.1 reshape.87
  64.2 0.1 fusion.2
  64.3 0.1 slice.34
  64.4 0.1 fusion
  64.5 0.1 slice.31
  64.6 0.6 pad_add_fusion.at_ref
  65.1 0.7 add_convert_fusion.1.kdoc_ref
  65.8 0.7 add_convert_fusion.qdoc_ref
  66.5 0.0 all-to-all-done
  66.5 0.0 copy-start
  66.5 1.1 copy-done
  67.6 17.1 %totals.1 = (f32[1,5120]{1,0:T(1,128)}, f32[1,5120]{1,0:T(1,128)}, bf16[5120,128]{1,0:T(8,128)(2,1)}, bf16[2560,128]{1,0:T(8,128)(2,1)}, bf16[128,2560]{1,0:T(8,128)(2,1)}) custom-call(s32[4]{0:T(128)} %pad_add_fusion.at_ref, bf16[5120,128]{1,0:T(8,128)(2,1)} %bitcast.12, bf16[2560,128]{1,0:T(8,128)(2,1)} %bitcast.13, f32[1,1280]{1,0:T(1,128)} %add_convert_fusion.qdoc_ref, ...), custom_call_target="tpu_custom_call" | custom-call | tf_op jit(solution)/shard_map/totals/pallas_call | solution.py:312
  84.6 0.8 pad_maximum_fusion.s0
  85.4 0.0 copy-start.2
  85.4 6.2 %collective-permute-start.2 = (f32[2,5120]{1,0:T(2,128)S(1)}, f32[2,5120]{1,0:T(2,128)S(1)}, u32[]{:S(2)}, u32[]{:S(2)}) collective-permute-start(f32[2,5120]{1,0:T(2,128)S(1)} %pad_maximum_fusion.s0), channel_id=1, source_target_pairs={{0,3},{1,0},{2,1},{3,2},{4,7},{5,4},{6,5},{7,6},{8,11},{9,8},{10,9... | collective-permute-start | bytes 122888 | tf_op jit(solution)/shard_map/ppermute | solution.py:328
  91.7 0.2 collective-permute-start.1
  91.8 1.3 collective-permute-start
  93.2 0.5 collective-permute-done.2.s3
  93.7 0.0 copy-start.3
  93.7 3.6 %collective-permute-done.1.s2 = f32[2,5120]{1,0:T(2,128)S(1)} collective-permute-done((f32[2,5120]{1,0:T(2,128)S(1)}, f32[2,5120]{1,0:T(2,128)S(1)}, u32[]{:S(2)}, u32[]{:S(2)}) %collective-permute-start.1) | collective-permute-done | bytes 40992 | tf_op jit(solution)/shard_map/ppermute | solution.py:328
  97.2 0.0 copy-start.4
  97.2 0.2 collective-permute-done.s1
  97.5 0.0 copy-start.5
  97.5 0.0 copy-done.2
  97.5 0.0 copy-done.3
  97.5 0.4 copy-done.4
  97.8 0.3 copy-done.5
  98.1 27.2 %grads.1 = (bf16[64,48,128]{2,1,0:T(8,128)(2,1)}, bf16[32,80,128]{2,1,0:T(8,128)(2,1)}) custom-call(s32[4]{0:T(128)} %pad_add_fusion.at_ref, bf16[5120,128]{1,0:T(8,128)(2,1)} %get-tuple-element.14.qg_ref, bf16[2560,128]{1,0:T(8,128)(2,1)} %get-tuple-element.15.kv_ref, bf16[128,2560]{1,0:T(8,128)(2,1)} %get-tuple-element.16.kvt_ref, ...), custom_call_target="tpu_custom_call" | custom-call | tf_op jit(solution)/shard_map/grads/pallas_call | solution.py:330
  125.3 0.0 copy-start.1
  125.3 18.5 %all_to_all.21.dkv_ref = bf16[32,80,128]{2,1,0:T(8,128)(2,1)} all-to-all(bf16[32,80,128]{2,1,0:T(8,128)(2,1)} %get-tuple-element.20), channel_id=1, replica_groups=mesh['y'=4,'zl'=2,'c'=2,'zh'=2,'x'=4] {'y','zl','c','zh'}, dimensions={0} | all-to-all | bytes 1310720 | tf_op jit(solution)/shard_map/all_to_all | solution.py:344
  143.8 0.0 copy-done.1
  143.8 20.0 %all_to_all.22.dq_ref = bf16[64,48,128]{2,1,0:T(8,128)(2,1)} all-to-all(bf16[64,48,128]{2,1,0:T(8,128)(2,1)S(1)} %copy-done.1), channel_id=1, replica_groups=mesh['y'=4,'zl'=2,'c'=2,'zh'=2,'x'=4] {'y','zl','c','x'}, dimensions={0} | all-to-all | bytes 1572864 | tf_op jit(solution)/shard_map/all_to_all | solution.py:345
  163.8 2.4 %join.1 = (bf16[80,1024]{1,0:T(8,128)(2,1)}, bf16[80,1024]{1,0:T(8,128)(2,1)}, bf16[80,1024]{1,0:T(8,128)(2,1)}) custom-call(bf16[64,48,128]{2,1,0:T(8,128)(2,1)} %all_to_all.22.dq_ref, bf16[32,80,128]{2,1,0:T(8,128)(2,1)} %all_to_all.21.dkv_ref), custom_call_target="tpu_custom_call" | custom-call | tf_op jit(solution)/shard_map/join/pallas_call | solution.py:347
  (5 shorter events, 0.0 us)
Async XLA Ops:
  25.7 5.7 %copy-start.6 = (s32[640]{0:T(1024)S(1)}, s32[640]{0:T(1024)}, u32[]{:S(2)}) copy-start(s32[640]{0:T(1024)} %param.9) | copy-start | bytes 7684
  25.7 40.9 %all-to-all-start = ((bf16[64,80,128]{2,1,0:T(8,128)(2,1)}), bf16[64,80,128]{2,1,0:T(8,128)(2,1)S(1)}, u32[]{:S(2)}, u32[]{:S(2)}) async-start(bf16[64,80,128]{2,1,0:T(8,128)(2,1)} %get-tuple-element.12), calls=%async_computation | async-start | bytes 2621440 | tf_op jit(solution)/shard_map/all_to_all | solution.py:301
  66.5 1.1 copy-start
  85.4 12.1 %copy-start.2 = (f32[2,5120]{1,0:T(2,128)}, f32[2,5120]{1,0:T(2,128)S(1)}, u32[]{:S(2)}) copy-start(f32[2,5120]{1,0:T(2,128)S(1)} %pad_maximum_fusion.s0) | copy-start | bytes 122884
  85.4 8.2 %collective-permute-start.2 = (f32[2,5120]{1,0:T(2,128)S(1)}, f32[2,5120]{1,0:T(2,128)S(1)}, u32[]{:S(2)}, u32[]{:S(2)}) collective-permute-start(f32[2,5120]{1,0:T(2,128)S(1)} %pad_maximum_fusion.s0), channel_id=1, source_target_pairs={{0,3},{1,0},{2,1},{3,2},{4,7},{5,4},{6,5},{7,6},{8,11},{9,8},{10,9... | collective-permute-start | bytes 122888 | tf_op jit(solution)/shard_map/ppermute | solution.py:328
  91.7 5.6 %collective-permute-start.1 = (f32[2,5120]{1,0:T(2,128)S(1)}, f32[2,5120]{1,0:T(2,128)S(1)}, u32[]{:S(2)}, u32[]{:S(2)}) collective-permute-start(f32[2,5120]{1,0:T(2,128)S(1)} %pad_maximum_fusion.s0), channel_id=1, source_target_pairs={{0,2},{1,3},{2,0},{3,1},{4,6},{5,7},{6,4},{7,5},{8,10},{9,11},{10,... | collective-permute-start | bytes 122888 | tf_op jit(solution)/shard_map/ppermute | solution.py:328
  91.8 5.7 %collective-permute-start = (f32[2,5120]{1,0:T(2,128)S(1)}, f32[2,5120]{1,0:T(2,128)S(1)}, u32[]{:S(2)}, u32[]{:S(2)}) collective-permute-start(f32[2,5120]{1,0:T(2,128)S(1)} %pad_maximum_fusion.s0), channel_id=1, source_target_pairs={{0,1},{1,2},{2,3},{3,0},{4,5},{5,6},{6,7},{7,4},{8,9},{9,10},{10,1... | collective-permute-start | bytes 122888 | tf_op jit(solution)/shard_map/ppermute | solution.py:328
  93.7 3.8 %copy-start.3 = (f32[2,5120]{1,0:T(2,128)}, f32[2,5120]{1,0:T(2,128)S(1)}, u32[]{:S(2)}) copy-start(f32[2,5120]{1,0:T(2,128)S(1)} %collective-permute-done.2.s3) | copy-start | bytes 122884
  97.2 0.6 copy-start.4
  97.5 0.6 copy-start.5
  125.3 18.5 %copy-start.1 = (bf16[64,48,128]{2,1,0:T(8,128)(2,1)S(1)}, bf16[64,48,128]{2,1,0:T(8,128)(2,1)}, u32[]{:S(2)}) copy-start(bf16[64,48,128]{2,1,0:T(8,128)(2,1)} %get-tuple-element.19) | copy-start | bytes 2359300

commit v2 on v1

v2 whole, which is shorter than its diff:
```python
import functools
import math

import jax
import jax.numpy as jnp
from jax import lax
from jax.experimental import pallas as pl
from jax.experimental.pallas import tpu as pltpu
from jax.sharding import Mesh
from jax.sharding import PartitionSpec as P

BF = jnp.bfloat16
F32 = jnp.float32
HD = 64
HEADS = 16
ROWS = 80
OWN = 1280
LONG = 960
REST = OWN - LONG
SENT = OWN + 16
STEP = 240
WIDE = 1408
SCALE = 1.0 / math.sqrt(HD)
LOG2_SCALE = SCALE * math.log2(math.e)
NEG = -1e30
BLK = ("y", "zl", "c")
VMEM_LIMIT = 24 << 20


def dot_nt(a, b):
    return lax.dot_general(a, b, (((1,), (1,)), ((), ())), preferred_element_type=F32)


def dot_nn(a, b):
    return lax.dot_general(a, b, (((1,), (0,)), ((), ())), preferred_element_type=F32)


def lane_of(x):
    return lax.broadcasted_iota(jnp.int32, x.shape, x.ndim - 1)


def row_of(x):
    return lax.broadcasted_iota(jnp.int32, x.shape, 0)


def swap_halves(x):
    return pltpu.roll(x, HD, 1)


def shape(*dims, dtype=BF):
    return jax.ShapeDtypeStruct(dims, dtype)


def call(kernel, name, outs, args, smem_in=0, smem_out=0, scratch=(), flops=1 << 20):
    vm = pl.BlockSpec(memory_space=pltpu.VMEM)
    sm = pl.BlockSpec(memory_space=pltpu.SMEM)
    return pl.pallas_call(
        kernel,
        out_shape=outs,
        in_specs=[sm] * smem_in + [vm] * (len(args) - smem_in),
        out_specs=[sm] * smem_out + [vm] * (len(outs) - smem_out),
        scratch_shapes=list(scratch),
        compiler_params=pltpu.CompilerParams(vmem_limit_bytes=VMEM_LIMIT),
        cost_estimate=pl.CostEstimate(flops=flops, bytes_accessed=1 << 20, transcendentals=0),
        name=name,
    )(*args)


def pack_kernel(q_ref, k_ref, v_ref, g_ref, doc_ref, out_ref):
    for pair in range(HEADS // 2):
        cols = slice(pair * 128, pair * 128 + 128)
        for a_ref, b_ref, at in ((q_ref, g_ref, 0), (k_ref, v_ref, ROWS)):
            a = a_ref[:, cols].astype(F32)
            b = b_ref[:, cols].astype(F32)
            low = lane_of(a) < HD
            out_ref[2 * pair, at : at + ROWS, :] = jnp.where(low, a, swap_halves(b)).astype(BF)
            out_ref[2 * pair + 1, at : at + ROWS, :] = jnp.where(low, swap_halves(a), b).astype(BF)
    group = lax.axis_index("zh") * 4 + lax.axis_index("x")
    docs = jnp.broadcast_to(doc_ref[...].astype(F32), (16, 640))
    docs = pltpu.roll(docs, lax.rem(640 - group * ROWS, 640), 1)[:, 0:128].astype(BF)
    for h in range(HEADS):
        out_ref[h, 2 * ROWS : 2 * ROWS + 16, :] = docs


def swap_edges(ref, off):
    first = ref[0:16, :]
    last = ref[LONG : LONG + 16, :]
    early = row_of(first) < off
    ref[0:16, :] = jnp.where(early, last, first)
    ref[LONG : LONG + 16, :] = jnp.where(early, first, last)


def columns_of(doc_row):
    return jnp.broadcast_to(doc_row, (128, doc_row.shape[1])).T


def order_kernel(in_ref, at_ref, qg_ref, kv_ref, doc_ref):
    doc_at = slice(2 * ROWS, 2 * ROWS + 16)
    long_doc = in_ref[8, doc_at, :].astype(F32)[0:1, 0:1]
    before = jnp.zeros((1, 128), F32)
    for b in range(16):
        row = in_ref[b, doc_at, :].astype(F32)[0:1, :]
        before += jnp.where((row < long_doc) & (lane_of(row) < ROWS), 1.0, 0.0)
        doc_ref[OWN * 2 + b * ROWS : OWN * 2 + (b + 1) * ROWS, :] = columns_of(row)[0:ROWS, :]
    start = jnp.sum(before).astype(jnp.int32)
    off = lax.rem(start, 16)
    at_ref[0] = start - off
    at_ref[1] = off
    first = lax.div(start, 16)

    def move(i, _):
        at = lax.rem(first + i, OWN // 16)
        chunk = lax.div(at, ROWS // 16)
        part = lax.rem(at, ROWS // 16) * 16
        rows = pl.ds(pl.multiple_of(i * 16, 16), 16)
        qg_ref[rows, :] = in_ref[chunk, pl.ds(pl.multiple_of(part, 16), 16), :]
        kv_ref[rows, :] = in_ref[chunk, pl.ds(pl.multiple_of(ROWS + part, 16), 16), :]
        doc_ref[rows, :] = doc_ref[pl.ds(pl.multiple_of(OWN * 2 + at * 16, 16), 16), :]
        return 0

    lax.fori_loop(0, OWN // 16, move, 0, unroll=8)
    for ref in (qg_ref, kv_ref, doc_ref):
        swap_edges(ref, off)
    docs = doc_ref[LONG : LONG + 384, :].T
    lines = [docs[0:1, n * 128 : n * 128 + 128] for n in range(3)]
    block = jnp.concatenate(lines + [jnp.zeros((13, 128), F32)], axis=0).astype(BF)
    qg_ref[OWN:SENT, :] = block
    kv_ref[OWN:SENT, :] = block


def doc_row_of(ref):
    lines = ref[OWN:SENT, :].astype(F32)
    return jnp.concatenate([lines[n : n + 1, :] for n in range(3)], axis=1)


def same_doc(doc_cols, doc_row):
    wide = jnp.concatenate([doc_cols] * 3, axis=1)
    return (wide == doc_row)[0:REST, 0:REST]


def halves(x):
    zero = jnp.zeros_like(x)
    low = lane_of(x) < HD
    return jnp.where(low, x, zero), jnp.where(low, zero, x)


def totals_tile(kv_refs, vet_ref, col_ref, qg_ref, block, stat_ref, stat_row):
    doc_row = doc_row_of(qg_ref.at[block])
    for q_at, q_width in ((0, LONG), (LONG, REST)):
        rest = q_at == LONG
        qg = qg_ref[block, q_at : q_at + q_width, :]
        q0, _ = halves(qg)
        starts = [(h, at) for h in range(2) for at in (range(LONG, OWN, REST) if rest else range(0, LONG, STEP))]
        scores, tops, outs = {}, [], []

        def finish(key):
            half, at = key
            s = scores.pop(key)
            mask = None
            if rest:
                mask = same_doc(col_ref[half], doc_row)
                s = jnp.where(mask, s, NEG)
            top = jnp.max(s, axis=0, keepdims=True) * LOG2_SCALE
            p = jnp.exp2(s * LOG2_SCALE - top)
            if rest:
                p = jnp.where(mask, p, 0.0)
            lane = half * WIDE + lane_at(at)
            outs.append(dot_nn(vet_ref[:, lane : lane + s.shape[0]], p.astype(BF)))
            tops.append(top)

        for n, (half, at) in enumerate(starts):
            width = REST if rest else STEP
            scores[half, at] = dot_nt(kv_refs[half][at : at + width, :], q0)
            if n:
                finish(starts[n - 1])
        finish(starts[-1])
        top = functools.reduce(jnp.maximum, tops)
        out = sum(o * jnp.exp2(t - top) for o, t in zip(outs, tops))
        total = out[0:1, :]
        grad_t = qg.astype(F32).T
        dot = jnp.sum(out[HD:, :] * grad_t[HD:, :], axis=0, keepdims=True)
        if rest:
            empty = total <= 0.0
            total = jnp.where(empty, 1.0, total)
            top = jnp.where(empty, NEG, top)
        lanes = slice(lane_at(q_at), lane_at(q_at) + q_width)
        stat_ref[stat_row, 0:1, lanes] = top + jnp.log2(total)
        stat_ref[stat_row, 1:2, lanes] = dot / total


def lane_at(row):
    return row // STEP * 256


def values_of(kvt_ref, vet_ref):
    kvt = kvt_ref[...]
    vet_ref[...] = jnp.where(row_of(kvt) < HD, jnp.ones_like(kvt), kvt)


def near_kernel(kv_ref, kv_far_ref, qg0, qg1, qg3, stat_ref, kvt_ref, vet_ref, col_ref, qg_ref):
    for half, ref in enumerate((kv_ref, kv_far_ref)):
        for at in (0, STEP, 2 * STEP, 3 * STEP, LONG):
            width = REST if at == LONG else STEP
            lanes = slice(half * WIDE + lane_at(at), half * WIDE + lane_at(at) + width)
            kvt_ref[:, lanes] = ref[at : at + width, :].astype(F32).T.astype(BF)
        col_ref[half] = columns_of(doc_row_of(ref))
    values_of(kvt_ref, vet_ref)
    for n, ref in enumerate((qg0, qg1, qg3)):
        qg_ref[n] = ref[...]

    def block(n, _):
        totals_tile((kv_ref, kv_far_ref), vet_ref, col_ref, qg_ref, n, stat_ref, n)
        return 0

    lax.fori_loop(0, 3, block, 0)


def far_kernel(kv_ref, kv_far_ref, kvt_ref, qg2, near_ref, stat_ref, vet_ref, col_ref, qg_ref, last_ref):
    for half, ref in enumerate((kv_ref, kv_far_ref)):
        col_ref[half] = columns_of(doc_row_of(ref))
    values_of(kvt_ref, vet_ref)
    qg_ref[0] = qg2[...]
    totals_tile((kv_ref, kv_far_ref), vet_ref, col_ref, qg_ref, 0, last_ref, 0)
    stat_ref[0:2, :] = near_ref[0]
    stat_ref[2:4, :] = near_ref[1]
    stat_ref[4:6, :] = last_ref[0]
    stat_ref[6:8, :] = near_ref[2]


def combined(stat_refs, block):
    lses = [ref[2 * ((block - k) % 4) : 2 * ((block - k) % 4) + 1, :] for k, ref in enumerate(stat_refs)]
    dots = [ref[2 * ((block - k) % 4) + 1 : 2 * ((block - k) % 4) + 2, :] for k, ref in enumerate(stat_refs)]
    top = functools.reduce(jnp.maximum, lses)
    shares = [jnp.exp2(one - top) for one in lses]
    whole = sum(shares)
    return top + jnp.log2(whole), sum(w * d for w, d in zip(shares, dots)) / whole


def pair_grads(block, half, qg_ref, kv_ref, kvt_ref, row_ref, col_ref, dq_ref, dkv_ref):
    doc_row = doc_row_of(qg_ref.at[block])
    doc_col = col_ref[half]
    for q_at, q_width in ((0, LONG), (LONG, REST)):
        rest = q_at == LONG
        q0, g0 = halves(qg_ref[block, q_at : q_at + q_width, :])
        lanes = slice(lane_at(q_at), lane_at(q_at) + q_width)
        lse, dot = row_ref[block, 0:1, lanes], row_ref[block, 1:2, lanes]
        acc = None
        for at in range(LONG, OWN, REST) if rest else range(0, LONG, STEP):
            width = REST if rest else STEP
            kv = kv_ref[half, at : at + width, :]
            p = jnp.exp2(dot_nt(kv, q0) * LOG2_SCALE - lse)
            if rest:
                p = jnp.where(same_doc(doc_col, doc_row), p, 0.0)
            ds = (p * (dot_nt(kv, g0) - dot)).astype(BF)
            dkv_ref[half, at : at + width, :] += dot_nn(p.astype(BF), g0) + dot_nn(ds, q0)
            part = dot_nn(kvt_ref[half, 0:HD, lane_at(at) : lane_at(at) + width], ds)
            acc = part if acc is None else acc + part
        acc = acc * SCALE
        dq_ref[block, q_at : q_at + q_width, :] += jnp.concatenate([acc, acc], axis=0).T


def first_grads_kernel(
    kv0, kv1, kvt_in, qg0, qg1, qg2, qg3, st0, st1, st2, st3,
    dq1_out, dq2_out, dq3_out, dkv_far_out, dq_own_out, dkv_own_out,
    qg_ref, kv_ref, kvt_ref, row_ref, col_ref, dq_ref, dkv_ref,
):
    for n, ref in enumerate((qg0, qg1, qg2, qg3)):
        qg_ref[n] = ref[...]
        row_ref[n, 0:1, :], row_ref[n, 1:2, :] = combined((st0, st1, st2, st3), n)
    for n, ref in enumerate((kv0, kv1)):
        kv_ref[n] = ref[...]
        kvt_ref[n] = kvt_in[0:HD, n * WIDE : (n + 1) * WIDE]
        col_ref[n] = columns_of(doc_row_of(ref))
    dq_ref[...] = jnp.zeros_like(dq_ref)
    dkv_ref[...] = jnp.zeros_like(dkv_ref)

    def pair(n, _):
        far = (n < 4).astype(jnp.int32)
        block = jnp.where(n < 4, n, n - 3)
        pair_grads(block, far, qg_ref, kv_ref, kvt_ref, row_ref, col_ref, dq_ref, dkv_ref)
        return 0

    lax.fori_loop(0, 7, pair, 0)
    low = lax.broadcasted_iota(jnp.int32, (OWN // 2, 128), 1) < HD
    for n, out in ((1, dq1_out), (2, dq2_out), (3, dq3_out)):
        out[...] = jnp.where(low, dq_ref[n, 0 : OWN // 2, :], dq_ref[n, OWN // 2 : OWN, :]).astype(BF)
    dkv_far_out[...] = dkv_ref[1].astype(BF)
    dq_own_out[0] = dq_ref[0]
    dkv_own_out[0] = dkv_ref[0]


def last_grads_kernel(
    kv0, kvt_in, qg0, st0, st1, st2, st3, dq_in, dkv_in, dq_out, dkv_out, qg_ref, kv_ref, kvt_ref, row_ref, col_ref
):
    qg_ref[0] = qg0[...]
    row_ref[0, 0:1, :], row_ref[0, 1:2, :] = combined((st0, st1, st2, st3), 0)
    kv_ref[0] = kv0[...]
    kvt_ref[0] = kvt_in[0:HD, 0:WIDE]
    col_ref[0] = columns_of(doc_row_of(kv0))
    dq_out[...] = dq_in[...]
    dkv_out[...] = dkv_in[...]
    pair_grads(0, 0, qg_ref, kv_ref, kvt_ref, row_ref, col_ref, dq_out, dkv_out)


def merge_kernel(at_ref, own_dq, dq1, dq2, dq3, own_dkv, far_dkv, out_ref, dq_ref, dkv_ref):
    half = OWN // 2
    far = dq1[...].astype(F32) + dq2[...].astype(F32) + dq3[...].astype(F32)
    turned = swap_halves(far)
    low = lane_of(far) < HD
    dq_ref[0:half, :] = own_dq[0, 0:half, :] + jnp.where(low, far, turned)
    dq_ref[half:OWN, :] = own_dq[0, half:OWN, :] + jnp.where(low, turned, far)
    dkv = own_dkv[0] + far_dkv[...].astype(F32)
    dkv_ref[...] = jnp.where(lane_of(dkv) < HD, dkv * SCALE, dkv)
    off = at_ref[1]
    swap_edges(dq_ref, off)
    swap_edges(dkv_ref, off)
    base = at_ref[0]

    def chunk(c, _):
        def sixteen(ref, n):
            spot = lax.rem(c * ROWS + 16 * n + OWN - base, OWN)
            return ref[pl.ds(pl.multiple_of(spot, 16), 16), :]

        for n in range(5):
            out_ref[c, 16 * n : 16 * n + 16, :] = sixteen(dkv_ref, n).astype(BF)
        groups = [sixteen(dq_ref, n) for n in range(5)]
        low = lane_of(groups[0]) < HD
        out_ref[c, 80:96, :] = jnp.where(low, groups[0], groups[1]).astype(BF)
        out_ref[c, 96:112, :] = jnp.where(low, groups[2], groups[3]).astype(BF)
        out_ref[c, 112:128, :] = groups[4].astype(BF)
        return 0

    lax.fori_loop(0, 16, chunk, 0)


def join_kernel(in_ref, q_out, k_out, v_out):
    for pair in range(HEADS // 2):
        cols = slice(pair * 128, pair * 128 + 128)
        a, b = in_ref[2 * pair].astype(F32), in_ref[2 * pair + 1].astype(F32)
        a_swap, b_swap = swap_halves(a), swap_halves(b)
        low = lane_of(a) < HD
        even, odd = jnp.where(low, a, b_swap).astype(BF), jnp.where(low, a_swap, b).astype(BF)
        k_out[:, cols] = even[0:ROWS]
        v_out[:, cols] = odd[0:ROWS]
        for n in range(5):
            part = slice(ROWS + 16 * (n // 2), ROWS + 16 * (n // 2) + 16)
            q_out[16 * n : 16 * n + 16, cols] = (odd if n % 2 else even)[part]


def shifted(array, by):
    return lax.ppermute(array, "x", [(i, (i + by) % 4) for i in range(4)])


def crossed(array):
    return lax.ppermute(array, "zh", [(0, 1), (1, 0)])


def body(queries, keys, values, out_grad, doc_ids):
    packed = call(
        pack_kernel,
        "pack",
        [shape(16, 176, 128)],
        [queries, keys, values, out_grad, doc_ids.reshape(1, 640)],
    )[0]
    packed = lax.all_to_all(packed, BLK, 0, 0, tiled=True)
    at, qg, kv = call(
        order_kernel,
        "order",
        [shape(2, dtype=jnp.int32), shape(SENT, 128), shape(SENT, 128)],
        [packed],
        smem_out=1,
        scratch=[pltpu.VMEM((3 * OWN, 128), F32)],
    )
    kv_far = crossed(kv)
    qgs = [qg, shifted(qg, 1), shifted(qg, 2), shifted(qg, 3)]

    vet = pltpu.VMEM((128, 2 * WIDE), BF)
    col = pltpu.VMEM((2, 384, 128), F32)
    near, kvt = call(
        near_kernel,
        "totals_near",
        [shape(3, 2, WIDE, dtype=F32), shape(128, 2 * WIDE)],
        [kv, kv_far, qgs[0], qgs[1], qgs[3]],
        scratch=[vet, col, pltpu.VMEM((3, SENT, 128), BF)],
        flops=7_500_000_000,
    )
    stats = call(
        far_kernel,
        "totals_far",
        [shape(8, WIDE, dtype=F32)],
        [kv, kv_far, kvt, qgs[2], near],
        scratch=[vet, col, pltpu.VMEM((1, SENT, 128), BF), pltpu.VMEM((1, 2, WIDE), F32)],
        flops=2_500_000_000,
    )[0]
    stats = [stats] + [shifted(stats, k) for k in (1, 2, 3)]

    dq1, dq2, dq3, dkv_far, dq_own, dkv_own = call(
        first_grads_kernel,
        "grads_far",
        [shape(OWN // 2, 128)] * 3
        + [shape(OWN, 128), shape(1, OWN, 128, dtype=F32), shape(1, OWN, 128, dtype=F32)],
        [kv, kv_far, kvt, *qgs, *stats],
        scratch=[
            pltpu.VMEM((4, SENT, 128), BF),
            pltpu.VMEM((2, SENT, 128), BF),
            pltpu.VMEM((2, HD, WIDE), BF),
            pltpu.VMEM((4, 2, WIDE), F32),
            col,
            pltpu.VMEM((4, OWN, 128), F32),
            pltpu.VMEM((2, OWN, 128), F32),
        ],
        flops=20_000_000_000,
    )
    dqs = [shifted(dq, -n) for n, dq in ((1, dq1), (2, dq2), (3, dq3))]
    dkv_far = crossed(dkv_far)
    dq_own, dkv_own = call(
        last_grads_kernel,
        "grads_own",
        [shape(1, OWN, 128, dtype=F32), shape(1, OWN, 128, dtype=F32)],
        [kv, kvt, qg, *stats, dq_own, dkv_own],
        scratch=[
            pltpu.VMEM((1, SENT, 128), BF),
            pltpu.VMEM((1, SENT, 128), BF),
            pltpu.VMEM((1, HD, WIDE), BF),
            pltpu.VMEM((1, 2, WIDE), F32),
            pltpu.VMEM((1, 384, 128), F32),
        ],
        flops=3_000_000_000,
    )
    merged = call(
        merge_kernel,
        "merge",
        [shape(16, 128, 128)],
        [at, dq_own, *dqs, dkv_own, dkv_far],
        smem_in=1,
        scratch=[pltpu.VMEM((OWN, 128), F32), pltpu.VMEM((OWN, 128), F32)],
    )[0]
    merged = lax.all_to_all(merged, BLK, 0, 0, tiled=True)
    return tuple(call(join_kernel, "join", [shape(ROWS, HEADS * HD)] * 3, [merged]))


def solution(mesh):
    fine = Mesh(mesh.devices.reshape(4, 2, 2, 2, 4), BLK + ("zh", "x"))
    rows = P(BLK + ("zh", "x"), None)
    return jax.shard_map(
        body,
        mesh=fine,
        in_specs=(rows, rows, rows, rows, P(BLK)),
        out_specs=(rows, rows, rows),
        check_vma=False,
    )
```

time: 167 us -> 118 us (0.71)
  blocking collectives: 84.9 us -> 32 us
  waiting for transfers between devices: 4.32 us -> 24.4 us
  Pallas kernels: 49.4 us -> 42.3 us
  other arithmetic: 5.62 us -> 0 us
  between operations: 5.91 us -> 0.69 us
  local copies, waits for them, and re-layouts: 2.66 us -> 4.35 us
    all_to_all x3 -> x2, blocking collectives: 60.8 us -> 32 us  [the longest x1 18.5 us: body(): packed = lax.all_to_all(packed, BLK, 0, 0, tiled=True)]
    all_gather x1 -> x0, blocking collectives: 24.1 us -> none  [body(): all_docs = lax.all_gather(doc_ids, BLK, axis=0, tiled=True)]
    ppermute x3 -> x11, waiting for transfers between devices: 4.32 us -> 24.4 us  [the longest x9 21.4 us: shifted(): return lax.ppermute(array, 'x', [(i, (i + by) % 4) for i in range(4)])]
    pallas_call x4 -> x8, Pallas kernels: 49.4 us -> 42.3 us  [call(): pl.pallas_call(kernel, out_shape=outs, in_specs=[sm] * smem_in + [vm] * (...]
    ppermute x3 -> x11, starting transfers between devices: 7.72 us -> 14.2 us  [the longest x9 10.1 us: shifted(): return lax.ppermute(array, 'x', [(i, (i + by) % 4) for i in range(4)])]
    all_to_all x1 -> x0, starting transfers between devices: 5.67 us -> none  [body(): qg = lax.all_to_all(qg, BLK + ('x',), 0, 0, tiled=True).reshape(NQ, 128)]
    unnamed x15 -> x8, local copies, waits for them, and re-layouts: 1.7 us -> 3.66 us
  transfers between devices with their start and end apart: 4 -> 11, of which waited for: 3 -> 9; matrix products, arithmetic and copies ran while one was open for 3% -> 0% of each run, Pallas kernels for 0% -> 11%
where the time goes in v2:
time: 118 us
  Pallas kernels  42.3 us (36%)
  blocking collectives  32 us (27%)
  waiting for transfers between devices  24.4 us (21%)
  starting transfers between devices  14.2 us (12%)
  local copies, waits for them, and re-layouts  4.35 us (4%)
    pallas_call x8, Pallas kernels, call(): pl.pallas_call(kernel, out_shape=outs, in_specs=[sm] * smem_in + [vm] * (...  42.3 us
    ppermute x9, waiting for transfers between devices, shifted(): return lax.ppermute(array, 'x', [(i, (i + by) % 4) for i in range(4)])  21.4 us
    all_to_all x1, blocking collectives, body(): packed = lax.all_to_all(packed, BLK, 0, 0, tiled=True)  18.5 us
    all_to_all x1, blocking collectives, body(): merged = lax.all_to_all(merged, BLK, 0, 0, tiled=True)  13.5 us
    ppermute x9, starting transfers between devices, shifted(): return lax.ppermute(array, 'x', [(i, (i + by) % 4) for i in range(4)])  10.1 us
    ppermute x2, starting transfers between devices, crossed(): return lax.ppermute(array, 'zh', [(0, 1), (1, 0)])  4.11 us
    unnamed x8, local copies, waits for them, and re-layouts  3.66 us
    ppermute x2, waiting for transfers between devices, crossed(): return lax.ppermute(array, 'zh', [(0, 1), (1, 0)])  3.03 us
  transfers between devices with their start and end apart: 11, of which 9 were waited for; matrix products, arithmetic and copies ran while one was open for 0% of the time, Pallas kernels for 11%

profile of v2, /device:TPU:0, one launch (start us, length us, event | category | flops | bytes accessed | tf_op | source)
XLA Modules:
  0.0 117.9 jit_solution(1759974544238078011)
XLA Ops:
  0.6 0.7 reshape.9.doc_ref
  1.3 0.0 copy-start
  1.3 0.9 copy-done
  2.2 0.0 copy-start.1
  2.2 0.9 copy-done.1
  3.2 0.0 copy-start.2
  3.2 0.9 copy-done.2
  4.1 0.0 copy-start.3
  4.1 0.9 copy-done.3
  5.0 0.3 pack.1
  5.3 18.5 %all_to_all.10.in_ref = bf16[16,176,128]{2,1,0:T(8,128)(2,1)S(1)} all-to-all(bf16[16,176,128]{2,1,0:T(8,128)(2,1)S(1)} %pack.1), channel_id=1, replica_groups=mesh['y'=4,'zl'=2,'c'=2,'zh'=2,'x'=4] {'y','zl','c'}, dimensions={0} | all-to-all | bytes 1441792 | tf_op jit(solution)/shard_map/all_to_all | solution.py:365
  23.8 1.9 %order.1 = (s32[2]{0:T(128)S(1)}, bf16[1296,128]{1,0:T(8,128)(2,1)S(1)}, bf16[1296,128]{1,0:T(8,128)(2,1)S(1)}) custom-call(bf16[16,176,128]{2,1,0:T(8,128)(2,1)S(1)} %all_to_all.10.in_ref), custom_call_target="tpu_custom_call" | custom-call | flops 1048576 | bytes 1048576 | tf_op jit(solution)/shard_map/order/pallas_call | solution.py:57
  25.7 3.7 %collective-permute-start = (bf16[1296,128]{1,0:T(8,128)(2,1)S(1)}, bf16[1296,128]{1,0:T(8,128)(2,1)S(1)}, u32[]{:S(2)}, u32[]{:S(2)}) collective-permute-start(bf16[1296,128]{1,0:T(8,128)(2,1)S(1)} %get-tuple-element.17.kv_ref.kv0), channel_id=1, source_target_pairs={{0,4},{4,0},{1,5},{5,1},{2,6},{6,2},{3,7},{7,3},{8,12},{12,8},{9,1... | collective-permute-start | bytes 995336 | tf_op jit(solution)/shard_map/ppermute | solution.py:355
  29.4 2.8 %collective-permute-start.2 = (bf16[1296,128]{1,0:T(8,128)(2,1)S(1)}, bf16[1296,128]{1,0:T(8,128)(2,1)S(1)}, u32[]{:S(2)}, u32[]{:S(2)}) collective-permute-start(bf16[1296,128]{1,0:T(8,128)(2,1)S(1)} %get-tuple-element.18.qg0), channel_id=1, source_target_pairs={{0,3},{1,0},{2,1},{3,2},{4,7},{5,4},{6,5},{7,6},{8,11},{9,8},{10,9... | collective-permute-start | bytes 995336 | tf_op jit(solution)/shard_map/ppermute | solution.py:351
  32.2 0.0 collective-permute-start.1
  32.2 2.3 %collective-permute-start.3 = (bf16[1296,128]{1,0:T(8,128)(2,1)S(1)}, bf16[1296,128]{1,0:T(8,128)(2,1)S(1)}, u32[]{:S(2)}, u32[]{:S(2)}) collective-permute-start(bf16[1296,128]{1,0:T(8,128)(2,1)S(1)} %get-tuple-element.18.qg0), channel_id=1, source_target_pairs={{0,2},{1,3},{2,0},{3,1},{4,6},{5,7},{6,4},{7,5},{8,10},{9,11},{10,... | collective-permute-start | bytes 995336 | tf_op jit(solution)/shard_map/ppermute | solution.py:351
  34.5 3.0 %collective-permute-done.kv_far_ref.kv1 = bf16[1296,128]{1,0:T(8,128)(2,1)S(1)} collective-permute-done((bf16[1296,128]{1,0:T(8,128)(2,1)S(1)}, bf16[1296,128]{1,0:T(8,128)(2,1)S(1)}, u32[]{:S(2)}, u32[]{:S(2)}) %collective-permute-start) | collective-permute-done | bytes 331808 | tf_op jit(solution)/shard_map/ppermute | solution.py:355
  37.5 8.9 %collective-permute-done.2.qg3 = bf16[1296,128]{1,0:T(8,128)(2,1)S(1)} collective-permute-done((bf16[1296,128]{1,0:T(8,128)(2,1)S(1)}, bf16[1296,128]{1,0:T(8,128)(2,1)S(1)}, u32[]{:S(2)}, u32[]{:S(2)}) %collective-permute-start.2) | collective-permute-done | bytes 331808 | tf_op jit(solution)/shard_map/ppermute | solution.py:351
  46.4 3.4 %collective-permute-done.1.qg1 = bf16[1296,128]{1,0:T(8,128)(2,1)S(1)} collective-permute-done((bf16[1296,128]{1,0:T(8,128)(2,1)S(1)}, bf16[1296,128]{1,0:T(8,128)(2,1)S(1)}, u32[]{:S(2)}, u32[]{:S(2)}) %collective-permute-start.1) | collective-permute-done | bytes 331808 | tf_op jit(solution)/shard_map/ppermute | solution.py:351
  49.7 9.3 %totals_near.1 = (f32[3,2,1408]{2,1,0:T(2,128)S(1)}, bf16[128,2816]{1,0:T(8,128)(2,1)S(1)}) custom-call(bf16[1296,128]{1,0:T(8,128)(2,1)S(1)} %get-tuple-element.17.kv_ref.kv0, bf16[1296,128]{1,0:T(8,128)(2,1)S(1)} %collective-permute-done.kv_far_ref.kv1, bf16[1296,128]{1,0:T(8,128)(2,1)S(1)} %get-tuple-element.18.qg0, ...), custom_call_target="tpu_custom_call" | custom-call | flops 7500000256 | bytes 1048576 | tf_op jit(solution)/shard_map/totals_near/pallas_call | solution.py:57
  59.0 0.0 collective-permute-done.3.qg2
  59.0 3.0 %totals_far.1.st0 = f32[8,1408]{1,0:T(8,128)S(1)} custom-call(bf16[1296,128]{1,0:T(8,128)(2,1)S(1)} %get-tuple-element.17.kv_ref.kv0, bf16[1296,128]{1,0:T(8,128)(2,1)S(1)} %collective-permute-done.kv_far_ref.kv1, bf16[128,2816]{1,0:T(8,128)(2,1)S(1)} %get-tuple-element.19.kvt_ref.kvt_in, bf16[1296,128]{1,0:T(8,128)(2,1)S(1)} %collective-permute-done.3.qg2, ...), custom_call_target="tpu_custom_call" | custom-call | flops 2500000000 | bytes 1048576 | tf_op jit(solution)/shard_map/totals_far/pallas_call | solution.py:57
  62.0 0.4 collective-permute-start.6
  62.4 0.0 collective-permute-start.5
  62.4 1.7 %collective-permute-start.4 = (f32[8,1408]{1,0:T(8,128)S(1)}, f32[8,1408]{1,0:T(8,128)S(1)}, u32[]{:S(2)}, u32[]{:S(2)}) collective-permute-start(f32[8,1408]{1,0:T(8,128)S(1)} %totals_far.1.st0), channel_id=1, source_target_pairs={{0,1},{1,2},{2,3},{3,0},{4,5},{5,6},{6,7},{7,4},{8,9},{9,10},{10,1... | collective-permute-start | bytes 135176 | tf_op jit(solution)/shard_map/ppermute | solution.py:351
  64.1 2.0 %collective-permute-done.6.st3 = f32[8,1408]{1,0:T(8,128)S(1)} collective-permute-done((f32[8,1408]{1,0:T(8,128)S(1)}, f32[8,1408]{1,0:T(8,128)S(1)}, u32[]{:S(2)}, u32[]{:S(2)}) %collective-permute-start.6) | collective-permute-done | bytes 45088 | tf_op jit(solution)/shard_map/ppermute | solution.py:351
  66.1 1.8 %collective-permute-done.5.st2 = f32[8,1408]{1,0:T(8,128)S(1)} collective-permute-done((f32[8,1408]{1,0:T(8,128)S(1)}, f32[8,1408]{1,0:T(8,128)S(1)}, u32[]{:S(2)}, u32[]{:S(2)}) %collective-permute-start.5) | collective-permute-done | bytes 45088 | tf_op jit(solution)/shard_map/ppermute | solution.py:351
  67.9 0.9 collective-permute-done.4.st1
  68.8 22.4 %grads_far.1 = (bf16[640,128]{1,0:T(8,128)(2,1)S(1)}, bf16[640,128]{1,0:T(8,128)(2,1)S(1)}, bf16[640,128]{1,0:T(8,128)(2,1)S(1)}, bf16[1280,128]{1,0:T(8,128)(2,...) custom-call(bf16[1296,128]{1,0:T(8,128)(2,1)S(1)} %get-tuple-element.17.kv_ref.kv0, ...), custom_call_target="tpu_custom_call" | custom-call | flops 20000000000 | bytes 1048576 | tf_op jit(solution)/shard_map/grads_far/pallas_call | solution.py:57
  91.2 0.4 collective-permute-start.10
  91.7 2.0 %collective-permute-start.7 = (bf16[640,128]{1,0:T(8,128)(2,1)S(1)}, bf16[640,128]{1,0:T(8,128)(2,1)S(1)}, u32[]{:S(2)}, u32[]{:S(2)}) collective-permute-start(bf16[640,128]{1,0:T(8,128)(2,1)S(1)} %get-tuple-element.24), channel_id=1, source_target_pairs={{0,3},{1,0},{2,1},{3,2},{4,7},{5,4},{6,5},{7,6},{8,11},{9,8},{10,9... | collective-permute-start | bytes 491528 | tf_op jit(solution)/shard_map/ppermute | solution.py:351
  93.7 0.9 collective-permute-start.8
  94.6 0.0 collective-permute-start.9
  94.6 3.2 %grads_own.1 = (f32[1,1280,128]{2,1,0:T(8,128)S(1)}, f32[1,1280,128]{2,1,0:T(8,128)S(1)}) custom-call(bf16[1296,128]{1,0:T(8,128)(2,1)S(1)} %get-tuple-element.17.kv_ref.kv0, bf16[128,2816]{1,0:T(8,128)(2,1)S(1)} %get-tuple-element.19.kvt_ref.kvt_in, bf16[1296,128]{1,0:T(8,128)(2,1)S(1)} %get-tuple-element.18.qg0, f32[8,1408]{1,0:T(8,128)S(1)} %totals_far.1.st0, ...), custom_call_target="tpu_custom_call" | custom-call | flops 3000000000 | bytes 1048576 | tf_op jit(solution)/shard_map/grads_own/pallas_call | solution.py:57
  97.8 0.5 collective-permute-done.7.dq1
  98.3 2.3 %collective-permute-done.8.dq2 = bf16[640,128]{1,0:T(8,128)(2,1)S(1)} collective-permute-done((bf16[640,128]{1,0:T(8,128)(2,1)S(1)}, bf16[640,128]{1,0:T(8,128)(2,1)S(1)}, u32[]{:S(2)}, u32[]{:S(2)}) %collective-permute-start.8) | collective-permute-done | bytes 163872 | tf_op jit(solution)/shard_map/ppermute | solution.py:351
  100.6 1.7 %collective-permute-done.9.dq3 = bf16[640,128]{1,0:T(8,128)(2,1)S(1)} collective-permute-done((bf16[640,128]{1,0:T(8,128)(2,1)S(1)}, bf16[640,128]{1,0:T(8,128)(2,1)S(1)}, u32[]{:S(2)}, u32[]{:S(2)}) %collective-permute-start.9) | collective-permute-done | bytes 163872 | tf_op jit(solution)/shard_map/ppermute | solution.py:351
  102.2 0.0 collective-permute-done.10.far_dkv
  102.3 1.1 merge.1
  103.4 13.5 %all_to_all.11.in_ref = bf16[16,128,128]{2,1,0:T(8,128)(2,1)S(1)} all-to-all(bf16[16,128,128]{2,1,0:T(8,128)(2,1)S(1)} %merge.1), channel_id=1, replica_groups=mesh['y'=4,'zl'=2,'c'=2,'zh'=2,'x'=4] {'y','zl','c'}, dimensions={0} | all-to-all | bytes 1048576 | tf_op jit(solution)/shard_map/all_to_all | solution.py:438
  116.9 1.0 join.1
Async XLA Ops:
  1.3 0.9 copy-start
  2.2 0.9 copy-start.1
  3.2 0.9 copy-start.2
  4.1 0.9 copy-start.3
  25.7 11.7 %collective-permute-start = (bf16[1296,128]{1,0:T(8,128)(2,1)S(1)}, bf16[1296,128]{1,0:T(8,128)(2,1)S(1)}, u32[]{:S(2)}, u32[]{:S(2)}) collective-permute-start(bf16[1296,128]{1,0:T(8,128)(2,1)S(1)} %get-tuple-element.17.kv_ref.kv0), channel_id=1, source_target_pairs={{0,4},{4,0},{1,5},{5,1},{2,6},{6,2},{3,7},{7,3},{8,12},{12,8},{9,1... | collective-permute-start | bytes 995336 | tf_op jit(solution)/shard_map/ppermute | solution.py:355
  29.4 17.0 %collective-permute-start.2 = (bf16[1296,128]{1,0:T(8,128)(2,1)S(1)}, bf16[1296,128]{1,0:T(8,128)(2,1)S(1)}, u32[]{:S(2)}, u32[]{:S(2)}) collective-permute-start(bf16[1296,128]{1,0:T(8,128)(2,1)S(1)} %get-tuple-element.18.qg0), channel_id=1, source_target_pairs={{0,3},{1,0},{2,1},{3,2},{4,7},{5,4},{6,5},{7,6},{8,11},{9,8},{10,9... | collective-permute-start | bytes 995336 | tf_op jit(solution)/shard_map/ppermute | solution.py:351
  32.2 17.6 %collective-permute-start.1 = (bf16[1296,128]{1,0:T(8,128)(2,1)S(1)}, bf16[1296,128]{1,0:T(8,128)(2,1)S(1)}, u32[]{:S(2)}, u32[]{:S(2)}) collective-permute-start(bf16[1296,128]{1,0:T(8,128)(2,1)S(1)} %get-tuple-element.18.qg0), channel_id=1, source_target_pairs={{0,1},{1,2},{2,3},{3,0},{4,5},{5,6},{6,7},{7,4},{8,9},{9,10},{10,1... | collective-permute-start | bytes 995336 | tf_op jit(solution)/shard_map/ppermute | solution.py:351
  32.2 26.8 %collective-permute-start.3 = (bf16[1296,128]{1,0:T(8,128)(2,1)S(1)}, bf16[1296,128]{1,0:T(8,128)(2,1)S(1)}, u32[]{:S(2)}, u32[]{:S(2)}) collective-permute-start(bf16[1296,128]{1,0:T(8,128)(2,1)S(1)} %get-tuple-element.18.qg0), channel_id=1, source_target_pairs={{0,2},{1,3},{2,0},{3,1},{4,6},{5,7},{6,4},{7,5},{8,10},{9,11},{10,... | collective-permute-start | bytes 995336 | tf_op jit(solution)/shard_map/ppermute | solution.py:351
  62.0 4.1 %collective-permute-start.6 = (f32[8,1408]{1,0:T(8,128)S(1)}, f32[8,1408]{1,0:T(8,128)S(1)}, u32[]{:S(2)}, u32[]{:S(2)}) collective-permute-start(f32[8,1408]{1,0:T(8,128)S(1)} %totals_far.1.st0), channel_id=1, source_target_pairs={{0,3},{1,0},{2,1},{3,2},{4,7},{5,4},{6,5},{7,6},{8,11},{9,8},{10,9... | collective-permute-start | bytes 135176 | tf_op jit(solution)/shard_map/ppermute | solution.py:351
  62.4 5.6 %collective-permute-start.5 = (f32[8,1408]{1,0:T(8,128)S(1)}, f32[8,1408]{1,0:T(8,128)S(1)}, u32[]{:S(2)}, u32[]{:S(2)}) collective-permute-start(f32[8,1408]{1,0:T(8,128)S(1)} %totals_far.1.st0), channel_id=1, source_target_pairs={{0,2},{1,3},{2,0},{3,1},{4,6},{5,7},{6,4},{7,5},{8,10},{9,11},{10,... | collective-permute-start | bytes 135176 | tf_op jit(solution)/shard_map/ppermute | solution.py:351
  62.4 6.4 %collective-permute-start.4 = (f32[8,1408]{1,0:T(8,128)S(1)}, f32[8,1408]{1,0:T(8,128)S(1)}, u32[]{:S(2)}, u32[]{:S(2)}) collective-permute-start(f32[8,1408]{1,0:T(8,128)S(1)} %totals_far.1.st0), channel_id=1, source_target_pairs={{0,1},{1,2},{2,3},{3,0},{4,5},{5,6},{6,7},{7,4},{8,9},{9,10},{10,1... | collective-permute-start | bytes 135176 | tf_op jit(solution)/shard_map/ppermute | solution.py:351
  91.2 11.0 %collective-permute-start.10 = (bf16[1280,128]{1,0:T(8,128)(2,1)S(1)}, bf16[1280,128]{1,0:T(8,128)(2,1)S(1)}, u32[]{:S(2)}, u32[]{:S(2)}) collective-permute-start(bf16[1280,128]{1,0:T(8,128)(2,1)S(1)} %get-tuple-element.28), channel_id=1, source_target_pairs={{0,4},{4,0},{1,5},{5,1},{2,6},{6,2},{3,7},{7,3},{8,12},{12,8},{9,1... | collective-permute-start | bytes 983048 | tf_op jit(solution)/shard_map/ppermute | solution.py:355
  91.7 6.6 %collective-permute-start.7 = (bf16[640,128]{1,0:T(8,128)(2,1)S(1)}, bf16[640,128]{1,0:T(8,128)(2,1)S(1)}, u32[]{:S(2)}, u32[]{:S(2)}) collective-permute-start(bf16[640,128]{1,0:T(8,128)(2,1)S(1)} %get-tuple-element.24), channel_id=1, source_target_pairs={{0,3},{1,0},{2,1},{3,2},{4,7},{5,4},{6,5},{7,6},{8,11},{9,8},{10,9... | collective-permute-start | bytes 491528 | tf_op jit(solution)/shard_map/ppermute | solution.py:351
  93.7 6.9 %collective-permute-start.8 = (bf16[640,128]{1,0:T(8,128)(2,1)S(1)}, bf16[640,128]{1,0:T(8,128)(2,1)S(1)}, u32[]{:S(2)}, u32[]{:S(2)}) collective-permute-start(bf16[640,128]{1,0:T(8,128)(2,1)S(1)} %get-tuple-element.25), channel_id=1, source_target_pairs={{0,2},{1,3},{2,0},{3,1},{4,6},{5,7},{6,4},{7,5},{8,10},{9,11},{10,... | collective-permute-start | bytes 491528 | tf_op jit(solution)/shard_map/ppermute | solution.py:351
  94.6 7.7 %collective-permute-start.9 = (bf16[640,128]{1,0:T(8,128)(2,1)S(1)}, bf16[640,128]{1,0:T(8,128)(2,1)S(1)}, u32[]{:S(2)}, u32[]{:S(2)}) collective-permute-start(bf16[640,128]{1,0:T(8,128)(2,1)S(1)} %get-tuple-element.26), channel_id=1, source_target_pairs={{0,1},{1,2},{2,3},{3,0},{4,5},{5,6},{6,7},{7,4},{8,9},{9,10},{10,1... | collective-permute-start | bytes 491528 | tf_op jit(solution)/shard_map/ppermute | solution.py:351

commit v3 on v2

--- a/solution.py
+++ b/solution.py
@@ -18,6 +18,7 @@
 LONG = 960
 REST = OWN - LONG
 SENT = OWN + 16
+CUT = 656
 STEP = 240
 WIDE = 1408
 SCALE = 1.0 / math.sqrt(HD)
@@ -51,7 +52,7 @@
     return jax.ShapeDtypeStruct(dims, dtype)
 
 
-def call(kernel, name, outs, args, smem_in=0, smem_out=0, scratch=(), flops=1 << 20):
+def call(kernel, name, outs, args, smem_in=0, smem_out=0, scratch=(), flops=1 << 20, vmem=VMEM_LIMIT):
     vm = pl.BlockSpec(memory_space=pltpu.VMEM)
     sm = pl.BlockSpec(memory_space=pltpu.SMEM)
     return pl.pallas_call(
@@ -60,7 +61,7 @@
         in_specs=[sm] * smem_in + [vm] * (len(args) - smem_in),
         out_specs=[sm] * smem_out + [vm] * (len(outs) - smem_out),
         scratch_shapes=list(scratch),
-        compiler_params=pltpu.CompilerParams(vmem_limit_bytes=VMEM_LIMIT),
+        compiler_params=pltpu.CompilerParams(vmem_limit_bytes=vmem),
         cost_estimate=pl.CostEstimate(flops=flops, bytes_accessed=1 << 20, transcendentals=0),
         name=name,
     )(*args)
@@ -144,13 +145,14 @@
     return jnp.where(low, x, zero), jnp.where(low, zero, x)
 
 
-def totals_tile(kv_refs, vet_ref, col_ref, qg_ref, block, stat_ref, stat_row):
+def totals_tile(kv_refs, vet_ref, col_ref, qg_ref, block, stat_ref):
     doc_row = doc_row_of(qg_ref.at[block])
     for q_at, q_width in ((0, LONG), (LONG, REST)):
         rest = q_at == LONG
         qg = qg_ref[block, q_at : q_at + q_width, :]
         q0, _ = halves(qg)
-        starts = [(h, at) for h in range(2) for at in (range(LONG, OWN, REST) if rest else range(0, LONG, STEP))]
+        steps = range(LONG, OWN, REST) if rest else range(0, LONG, STEP)
+        starts = [(half, at) for half in range(len(kv_refs)) for at in steps]
         scores, tops, outs = {}, [], []
 
         def finish(key):
@@ -184,56 +186,77 @@
             total = jnp.where(empty, 1.0, total)
             top = jnp.where(empty, NEG, top)
         lanes = slice(lane_at(q_at), lane_at(q_at) + q_width)
-        stat_ref[stat_row, 0:1, lanes] = top + jnp.log2(total)
-        stat_ref[stat_row, 1:2, lanes] = dot / total
+        stat_ref[block, 0:1, lanes] = top + jnp.log2(total)
+        stat_ref[block, 1:2, lanes] = dot / total
 
 
 def lane_at(row):
     return row // STEP * 256
 
 
-def values_of(kvt_ref, vet_ref):
-    kvt = kvt_ref[...]
-    vet_ref[...] = jnp.where(row_of(kvt) < HD, jnp.ones_like(kvt), kvt)
-
-
-def near_kernel(kv_ref, kv_far_ref, qg0, qg1, qg3, stat_ref, kvt_ref, vet_ref, col_ref, qg_ref):
-    for half, ref in enumerate((kv_ref, kv_far_ref)):
-        for at in (0, STEP, 2 * STEP, 3 * STEP, LONG):
-            width = REST if at == LONG else STEP
-            lanes = slice(half * WIDE + lane_at(at), half * WIDE + lane_at(at) + width)
-            kvt_ref[:, lanes] = ref[at : at + width, :].astype(F32).T.astype(BF)
-        col_ref[half] = columns_of(doc_row_of(ref))
-    values_of(kvt_ref, vet_ref)
-    for n, ref in enumerate((qg0, qg1, qg3)):
-        qg_ref[n] = ref[...]
+def prepare_keys(kv_refs, kvt_refs, vet_ref, col_ref, fresh):
+    for half, (kv_ref, kvt_ref) in enumerate(zip(kv_refs, kvt_refs)):
+        if fresh:
+            for at in (0, STEP, 2 * STEP, 3 * STEP, LONG):
+                width = REST if at == LONG else STEP
+                kvt_ref[:, lane_at(at) : lane_at(at) + width] = (
+                    kv_ref[at : at + width, :].astype(F32).T.astype(BF)
+                )
+        kvt = kvt_ref[...]
+        vet_ref[:, half * WIDE : (half + 1) * WIDE] = jnp.where(
+            row_of(kvt) < HD, jnp.ones_like(kvt), kvt
+        )
+        col_ref[half] = columns_of(doc_row_of(kv_ref))
+
+
+def own_totals_kernel(kv_ref, qg_in, stat_ref, kvt_ref, vet_ref, col_ref, qg_ref):
+    prepare_keys([kv_ref], [kvt_ref], vet_ref, col_ref, True)
+    qg_ref[0] = qg_in[...]
+    totals_tile([kv_ref], vet_ref, col_ref, qg_ref, 0, stat_ref)
+
+
+def near_totals_kernel(kv0, kv1, kvt0, kvt1, qg1, qg3, stat_ref, vet_ref, col_ref, qg_ref):
+    prepare_keys([kv0, kv1], [kvt0, kvt1], vet_ref, col_ref, False)
+    qg_ref[0] = qg1[...]
+    qg_ref[1] = qg3[...]
 
     def block(n, _):
-        totals_tile((kv_ref, kv_far_ref), vet_ref, col_ref, qg_ref, n, stat_ref, n)
+        totals_tile([kv0, kv1], vet_ref, col_ref, qg_ref, n, stat_ref)
         return 0
 
-    lax.fori_loop(0, 3, block, 0)
-
-
-def far_kernel(kv_ref, kv_far_ref, kvt_ref, qg2, near_ref, stat_ref, vet_ref, col_ref, qg_ref, last_ref):
-    for half, ref in enumerate((kv_ref, kv_far_ref)):
-        col_ref[half] = columns_of(doc_row_of(ref))
-    values_of(kvt_ref, vet_ref)
-    qg_ref[0] = qg2[...]
-    totals_tile((kv_ref, kv_far_ref), vet_ref, col_ref, qg_ref, 0, last_ref, 0)
-    stat_ref[0:2, :] = near_ref[0]
-    stat_ref[2:4, :] = near_ref[1]
+    lax.fori_loop(0, 2, block, 0)
+
+
+def added(pairs):
+    top = functools.reduce(jnp.maximum, [lse for lse, _ in pairs])
+    shares = [jnp.exp2(lse - top) for lse, _ in pairs]
+    whole = sum(shares)
+    return top + jnp.log2(whole), sum(w * dot for w, (_, dot) in zip(shares, pairs)) / whole
+
+
+def far_totals_kernel(
+    kv0, kv1, kvt0, kvt1, qg2a, qg2b, own_ref, own_far_ref, near_ref, stat_ref, qg_out,
+    vet_ref, col_ref, qg_ref, last_ref,
+):
+    prepare_keys([kv0, kv1], [kvt0, kvt1], vet_ref, col_ref, False)
+    qg_ref[0, 0:CUT, :] = qg2a[...]
+    qg_ref[0, CUT:SENT, :] = qg2b[...]
+    qg_out[...] = qg_ref[0]
+    totals_tile([kv0, kv1], vet_ref, col_ref, qg_ref, 0, last_ref)
+    lse, dot = added([(ref[0, 0:1, :], ref[0, 1:2, :]) for ref in (own_ref, own_far_ref)])
+    stat_ref[0:1, :] = lse
+    stat_ref[1:2, :] = dot
+    stat_ref[2:4, :] = near_ref[0]
     stat_ref[4:6, :] = last_ref[0]
-    stat_ref[6:8, :] = near_ref[2]
+    stat_ref[6:8, :] = near_ref[1]
 
 
 def combined(stat_refs, block):
-    lses = [ref[2 * ((block - k) % 4) : 2 * ((block - k) % 4) + 1, :] for k, ref in enumerate(stat_refs)]
-    dots = [ref[2 * ((block - k) % 4) + 1 : 2 * ((block - k) % 4) + 2, :] for k, ref in enumerate(stat_refs)]
-    top = functools.reduce(jnp.maximum, lses)
-    shares = [jnp.exp2(one - top) for one in lses]
-    whole = sum(shares)
-    return top + jnp.log2(whole), sum(w * d for w, d in zip(shares, dots)) / whole
+    pairs = []
+    for k, ref in enumerate(stat_refs):
+        at = 2 * ((block - k) % 4)
+        pairs.append((ref[at : at + 1, :], ref[at + 1 : at + 2, :]))
+    return added(pairs)
 
 
 def pair_grads(block, half, qg_ref, kv_ref, kvt_ref, row_ref, col_ref, dq_ref, dkv_ref):
@@ -259,57 +282,109 @@
         dq_ref[block, q_at : q_at + q_width, :] += jnp.concatenate([acc, acc], axis=0).T
 
 
-def first_grads_kernel(
-    kv0, kv1, kvt_in, qg0, qg1, qg2, qg3, st0, st1, st2, st3,
-    dq1_out, dq2_out, dq3_out, dkv_far_out, dq_own_out, dkv_own_out,
-    qg_ref, kv_ref, kvt_ref, row_ref, col_ref, dq_ref, dkv_ref,
-):
-    for n, ref in enumerate((qg0, qg1, qg2, qg3)):
-        qg_ref[n] = ref[...]
+def packed_dq(dq):
+    low = lax.broadcasted_iota(jnp.int32, (OWN // 2, 128), 1) < HD
+    return jnp.where(low, dq[0 : OWN // 2, :], dq[OWN // 2 : OWN, :])
+
+
+def grads_kernel(plan, names, *refs):
+    ref = dict(zip(names, refs))
+    blocks, own_keys = plan["blocks"], plan["halves"]
+    for n, block in enumerate(blocks):
+        ref["qg_all"][n] = ref["qg", block][...]
+        ref["row_all"][n] = ref["rows"][block]
+        if ("dq_in", block) in ref:
+            ref["dq_all"][n] = ref["dq_in", block][...]
+        else:
+            ref["dq_all"][n] = jnp.zeros((OWN, 128), F32)
+    for n, half in enumerate(own_keys):
+        ref["kv_all"][n] = ref["kv", half][...]
+        ref["kvt_all"][n] = ref["kvt", half][0:HD, :]
+        ref["col_all"][n] = columns_of(doc_row_of(ref["kv", half]))
+        if ("dkv_in", half) in ref:
+            ref["dkv_all"][n] = ref["dkv_in", half][...]
+        else:
+            ref["dkv_all"][n] = jnp.zeros((OWN, 128), F32)
+
+    def pair(n, _):
+        pair_grads(
+            lax.div(n, len(own_keys)),
+            lax.rem(n, len(own_keys)),
+            *(ref[name] for name in ("qg_all", "kv_all", "kvt_all", "row_all", "col_all", "dq_all", "dkv_all")),
+        )
+        return 0
+
+    lax.fori_loop(0, len(blocks) * len(own_keys), pair, 0)
+    for n, block in enumerate(blocks):
+        if ("dq_out", block) in ref:
+            ref["dq_out", block][...] = ref["dq_all"][n]
+    for n, half in enumerate(own_keys):
+        if ("dkv_out", half) in ref:
+            ref["dkv_out", half][...] = ref["dkv_all"][n]
+        if ("dkv_send", half) in ref:
+            ref["dkv_send", half][...] = ref["dkv_all"][n].astype(BF)
+    if "dq_a" in ref:
+        packed = packed_dq(ref["dq_all"][0]).astype(BF)
+        ref["dq_a"][...] = packed[0 : OWN // 4, :]
+        ref["dq_b"][...] = packed[OWN // 4 : OWN // 2, :]
+    if "dq_send" in ref:
+        packed = packed_dq(ref["dq_all"][0])
+        relay = ref["relay"][...].astype(F32)
+        first, second = packed[0 : OWN // 4, :], packed[OWN // 4 : OWN // 2, :]
+        if blocks[0] == 3:
+            first = first + relay
+        else:
+            second = second + relay
+        ref["dq_send"][0 : OWN // 4, :] = first.astype(BF)
+        ref["dq_send"][OWN // 4 : OWN // 2, :] = second.astype(BF)
+
+
+def rows_kernel(st0, st1, st2, st3, row_ref):
+    for n in range(4):
         row_ref[n, 0:1, :], row_ref[n, 1:2, :] = combined((st0, st1, st2, st3), n)
-    for n, ref in enumerate((kv0, kv1)):
-        kv_ref[n] = ref[...]
-        kvt_ref[n] = kvt_in[0:HD, n * WIDE : (n + 1) * WIDE]
-        col_ref[n] = columns_of(doc_row_of(ref))
-    dq_ref[...] = jnp.zeros_like(dq_ref)
-    dkv_ref[...] = jnp.zeros_like(dkv_ref)
-
-    def pair(n, _):
-        far = (n < 4).astype(jnp.int32)
-        block = jnp.where(n < 4, n, n - 3)
-        pair_grads(block, far, qg_ref, kv_ref, kvt_ref, row_ref, col_ref, dq_ref, dkv_ref)
-        return 0
-
-    lax.fori_loop(0, 7, pair, 0)
-    low = lax.broadcasted_iota(jnp.int32, (OWN // 2, 128), 1) < HD
-    for n, out in ((1, dq1_out), (2, dq2_out), (3, dq3_out)):
-        out[...] = jnp.where(low, dq_ref[n, 0 : OWN // 2, :], dq_ref[n, OWN // 2 : OWN, :]).astype(BF)
-    dkv_far_out[...] = dkv_ref[1].astype(BF)
-    dq_own_out[0] = dq_ref[0]
-    dkv_own_out[0] = dkv_ref[0]
-
-
-def last_grads_kernel(
-    kv0, kvt_in, qg0, st0, st1, st2, st3, dq_in, dkv_in, dq_out, dkv_out, qg_ref, kv_ref, kvt_ref, row_ref, col_ref
-):
-    qg_ref[0] = qg0[...]
-    row_ref[0, 0:1, :], row_ref[0, 1:2, :] = combined((st0, st1, st2, st3), 0)
-    kv_ref[0] = kv0[...]
-    kvt_ref[0] = kvt_in[0:HD, 0:WIDE]
-    col_ref[0] = columns_of(doc_row_of(kv0))
-    dq_out[...] = dq_in[...]
-    dkv_out[...] = dkv_in[...]
-    pair_grads(0, 0, qg_ref, kv_ref, kvt_ref, row_ref, col_ref, dq_out, dkv_out)
-
-
-def merge_kernel(at_ref, own_dq, dq1, dq2, dq3, own_dkv, far_dkv, out_ref, dq_ref, dkv_ref):
+
+
+def grads(name, blocks, halves_, arrays, takes=(), gives=()):
+    ins = [("kv", h) for h in halves_] + [("kvt", h) for h in halves_] + ["rows"]
+    ins += [("qg", b) for b in blocks] + list(takes)
+    shapes = {"dq_a": shape(OWN // 4, 128), "dq_b": shape(OWN // 4, 128), "dq_send": shape(OWN // 2, 128)}
+    outs = [
+        shapes[g] if g in shapes else shape(OWN, 128, dtype=BF if g[0] == "dkv_send" else F32)
+        for g in gives
+    ]
+    nb, nh = len(blocks), len(halves_)
+    scratch = dict(
+        qg_all=pltpu.VMEM((nb, SENT, 128), BF),
+        row_all=pltpu.VMEM((nb, 2, WIDE), F32),
+        dq_all=pltpu.VMEM((nb, OWN, 128), F32),
+        kv_all=pltpu.VMEM((nh, SENT, 128), BF),
+        kvt_all=pltpu.VMEM((nh, HD, WIDE), BF),
+        col_all=pltpu.VMEM((nh, 384, 128), F32),
+        dkv_all=pltpu.VMEM((nh, OWN, 128), F32),
+    )
+    results = call(
+        functools.partial(
+            grads_kernel,
+            dict(blocks=blocks, halves=halves_),
+            ins + list(gives) + list(scratch),
+        ),
+        name,
+        outs,
+        [arrays[n] for n in ins],
+        scratch=scratch.values(),
+        flops=nb * nh * 3_000_000_000,
+    )
+    arrays.update(zip(gives, results))
+
+
+def merge_kernel(at_ref, own_dq, dq1, dq3, own_dkv, far_dkv, out_ref, dq_ref, dkv_ref):
     half = OWN // 2
-    far = dq1[...].astype(F32) + dq2[...].astype(F32) + dq3[...].astype(F32)
+    far = dq1[...].astype(F32) + dq3[...].astype(F32)
     turned = swap_halves(far)
     low = lane_of(far) < HD
-    dq_ref[0:half, :] = own_dq[0, 0:half, :] + jnp.where(low, far, turned)
-    dq_ref[half:OWN, :] = own_dq[0, half:OWN, :] + jnp.where(low, turned, far)
-    dkv = own_dkv[0] + far_dkv[...].astype(F32)
+    dq_ref[0:half, :] = own_dq[0:half, :] + jnp.where(low, far, turned)
+    dq_ref[half:OWN, :] = own_dq[half:OWN, :] + jnp.where(low, turned, far)
+    dkv = own_dkv[...] + far_dkv[...].astype(F32)
     dkv_ref[...] = jnp.where(lane_of(dkv) < HD, dkv * SCALE, dkv)
     off = at_ref[1]
     swap_edges(dq_ref, off)
@@ -361,6 +436,7 @@
         "pack",
         [shape(16, 176, 128)],
         [queries, keys, values, out_grad, doc_ids.reshape(1, 640)],
+        vmem=56 << 20,
     )[0]
     packed = lax.all_to_all(packed, BLK, 0, 0, tiled=True)
     at, qg, kv = call(
@@ -372,66 +448,79 @@
         scratch=[pltpu.VMEM((3 * OWN, 128), F32)],
     )
     kv_far = crossed(kv)
-    qgs = [qg, shifted(qg, 1), shifted(qg, 2), shifted(qg, 3)]
-
-    vet = pltpu.VMEM((128, 2 * WIDE), BF)
-    col = pltpu.VMEM((2, 384, 128), F32)
-    near, kvt = call(
-        near_kernel,
+    qg1, qg3 = shifted(qg, 1), shifted(qg, -1)
+    qg2 = shifted(qg1[:CUT], 1), shifted(qg3[CUT:], -1)
+
+    def side(sets, blocks):
+        return [
+            pltpu.VMEM((128, sets * WIDE), BF),
+            pltpu.VMEM((sets, 384, 128), F32),
+            pltpu.VMEM((blocks, SENT, 128), BF),
+        ]
+
+    own, kvt = call(
+        own_totals_kernel,
+        "totals_own",
+        [shape(1, 2, WIDE, dtype=F32), shape(128, WIDE)],
+        [kv, qg],
+        scratch=side(1, 1),
+        flops=1_250_000_000,
+    )
+    own_far, kvt_far = call(
+        own_totals_kernel,
+        "totals_own_far",
+        [shape(1, 2, WIDE, dtype=F32), shape(128, WIDE)],
+        [kv_far, qg],
+        scratch=side(1, 1),
+        flops=1_250_000_000,
+    )
+    near = call(
+        near_totals_kernel,
         "totals_near",
-        [shape(3, 2, WIDE, dtype=F32), shape(128, 2 * WIDE)],
-        [kv, kv_far, qgs[0], qgs[1], qgs[3]],
-        scratch=[vet, col, pltpu.VMEM((3, SENT, 128), BF)],
-        flops=7_500_000_000,
-    )
-    stats = call(
-        far_kernel,
+        [shape(2, 2, WIDE, dtype=F32)],
+        [kv, kv_far, kvt, kvt_far, qg1, qg3],
+        scratch=side(2, 2),
+        flops=5_000_000_000,
+    )[0]
+    stats, qg2 = call(
+        far_totals_kernel,
         "totals_far",
-        [shape(8, WIDE, dtype=F32)],
-        [kv, kv_far, kvt, qgs[2], near],
-        scratch=[vet, col, pltpu.VMEM((1, SENT, 128), BF), pltpu.VMEM((1, 2, WIDE), F32)],
+        [shape(8, WIDE, dtype=F32), shape(SENT, 128)],
+        [kv, kv_far, kvt, kvt_far, *qg2, own, own_far, near],
+        scratch=side(2, 1) + [pltpu.VMEM((1, 2, WIDE), F32)],
         flops=2_500_000_000,
+    )
+    rows = call(
+        rows_kernel,
+        "rows",
+        [shape(4, 2, WIDE, dtype=F32)],
+        [stats] + [shifted(stats, k) for k in (1, 2, 3)],
     )[0]
-    stats = [stats] + [shifted(stats, k) for k in (1, 2, 3)]
-
-    dq1, dq2, dq3, dkv_far, dq_own, dkv_own = call(
-        first_grads_kernel,
-        "grads_far",
-        [shape(OWN // 2, 128)] * 3
-        + [shape(OWN, 128), shape(1, OWN, 128, dtype=F32), shape(1, OWN, 128, dtype=F32)],
-        [kv, kv_far, kvt, *qgs, *stats],
-        scratch=[
-            pltpu.VMEM((4, SENT, 128), BF),
-            pltpu.VMEM((2, SENT, 128), BF),
-            pltpu.VMEM((2, HD, WIDE), BF),
-            pltpu.VMEM((4, 2, WIDE), F32),
-            col,
-            pltpu.VMEM((4, OWN, 128), F32),
-            pltpu.VMEM((2, OWN, 128), F32),
-        ],
-        flops=20_000_000_000,
-    )
-    dqs = [shifted(dq, -n) for n, dq in ((1, dq1), (2, dq2), (3, dq3))]
-    dkv_far = crossed(dkv_far)
-    dq_own, dkv_own = call(
-        last_grads_kernel,
-        "grads_own",
-        [shape(1, OWN, 128, dtype=F32), shape(1, OWN, 128, dtype=F32)],
-        [kv, kvt, qg, *stats, dq_own, dkv_own],
-        scratch=[
-            pltpu.VMEM((1, SENT, 128), BF),
-            pltpu.VMEM((1, SENT, 128), BF),
-            pltpu.VMEM((1, HD, WIDE), BF),
-            pltpu.VMEM((1, 2, WIDE), F32),
-            pltpu.VMEM((1, 384, 128), F32),
-        ],
-        flops=3_000_000_000,
-    )
+
+    arrays = {("qg", n): one for n, one in enumerate((qg, qg1, qg2, qg3))}
+    arrays.update({("kv", 0): kv, ("kv", 1): kv_far, ("kvt", 0): kvt, ("kvt", 1): kvt_far, "rows": rows})
+    grads("grads_far", (2,), (0, 1), arrays, (), ("dq_a", "dq_b", ("dkv_out", 0), ("dkv_out", 1)))
+    arrays["dkv_in", 0], arrays["dkv_in", 1] = arrays["dkv_out", 0], arrays["dkv_out", 1]
+    to_three, to_one = shifted(arrays["dq_a"], 1), shifted(arrays["dq_b"], -1)
+    three = ("dq_out", 1), ("dq_out", 3), ("dq_out", 0)
+    grads("grads_partner", (1, 3, 0), (1,), arrays, [("dkv_in", 1)], [*three, ("dkv_send", 1)])
+    for n in (0, 1, 3):
+        arrays["dq_in", n] = arrays["dq_out", n]
+    dkv_far = crossed(arrays["dkv_send", 1])
+    sent = {}
+    for n, relay, by in ((1, to_one, -1), (3, to_three, 1)):
+        arrays["relay"] = relay
+        takes = [("dkv_in", 0), ("dq_in", n), "relay"]
+        grads(f"grads_near_{n}", (n,), (0,), arrays, takes, ["dq_send", ("dkv_out", 0)])
+        arrays["dkv_in", 0] = arrays["dkv_out", 0]
+        sent[n] = shifted(arrays["dq_send"], by)
+    takes = [("dkv_in", 0), ("dq_in", 0)]
+    grads("grads_own", (0,), (0,), arrays, takes, [("dq_out", 0), ("dkv_out", 0)])
     merged = call(
         merge_kernel,
         "merge",
         [shape(16, 128, 128)],
-        [at, dq_own, *dqs, dkv_own, dkv_far],
+        [at, arrays["dq_out", 0], sent[1], sent[3], arrays["dkv_out", 0], dkv_far],
         smem_in=1,
         scratch=[pltpu.VMEM((OWN, 128), F32), pltpu.VMEM((OWN, 128), F32)],
     )[0]

time: 118 us -> 111 us (0.941)
  waiting for transfers between devices: 24.4 us -> 6.72 us
  starting transfers between devices: 14.2 us -> 23.9 us
  Pallas kernels: 42.3 us -> 45.4 us
  local copies, waits for them, and re-layouts: 4.35 us -> 1.29 us
    ppermute x9 -> x11, waiting for transfers between devices: 21.4 us -> 6.72 us  [shifted(): return lax.ppermute(array, 'x', [(i, (i + by) % 4) for i in range(4)])]
    ppermute x9 -> x11, starting transfers between devices: 10.1 us -> 16.7 us  [shifted(): return lax.ppermute(array, 'x', [(i, (i + by) % 4) for i in range(4)])]
    unnamed x8 -> x0, local copies, waits for them, and re-layouts: 3.66 us -> none
    ppermute x2, starting transfers between devices: 4.11 us -> 7.25 us  [crossed(): return lax.ppermute(array, 'zh', [(0, 1), (1, 0)])]
    pallas_call x8 -> x14, Pallas kernels: 42.3 us -> 45.4 us  [call(): pl.pallas_call(kernel, out_shape=outs, in_specs=[sm] * smem_in + [vm] * (...]
    ppermute x2, waiting for transfers between devices: 3.03 us -> 0.01 us  [crossed(): return lax.ppermute(array, 'zh', [(0, 1), (1, 0)])]
  transfers between devices with their start and end apart: 11 -> 13, of which waited for: 9 -> 5; matrix products, arithmetic and copies ran while one was open for 0% -> 0% of each run, Pallas kernels for 11% -> 27%
where the time goes in v3:
time: 111 us; the launch traced here: 110 us
  Pallas kernels  45.4 us (41%)
  blocking collectives  32.2 us (29%)
  starting transfers between devices  23.9 us (22%)
  waiting for transfers between devices  6.72 us (6%)
  local copies, waits for them, and re-layouts  1.29 us (1%)
    pallas_call x14, Pallas kernels, call(): pl.pallas_call(kernel, out_shape=outs, in_specs=[sm] * smem_in + [vm] * (...  45.4 us
    all_to_all x1, blocking collectives, body(): packed = lax.all_to_all(packed, BLK, 0, 0, tiled=True)  18.7 us
    ppermute x11, starting transfers between devices, shifted(): return lax.ppermute(array, 'x', [(i, (i + by) % 4) for i in range(4)])  16.7 us
    all_to_all x1, blocking collectives, body(): merged = lax.all_to_all(merged, BLK, 0, 0, tiled=True)  13.5 us
    ppermute x2, starting transfers between devices, crossed(): return lax.ppermute(array, 'zh', [(0, 1), (1, 0)])  7.25 us
    ppermute x11, waiting for transfers between devices, shifted(): return lax.ppermute(array, 'x', [(i, (i + by) % 4) for i in range(4)])  6.72 us
  transfers between devices with their start and end apart: 13, of which 5 were waited for; matrix products, arithmetic and copies ran while one was open for 0% of the time, Pallas kernels for 27%

profile of v3, /device:TPU:0, one launch (start us, length us, event | category | flops | bytes accessed | tf_op | source)
XLA Modules:
  0.0 110.3 jit_solution(14069767681591050453)
XLA Ops:
  0.6 1.3 %reshape.9.doc_ref = s32[1,640]{1,0:T(1,128)} reshape(s32[640]{0:T(1024)} %param.9) | data formatting | bytes 5120 | tf_op jit(solution)/shard_map/reshape | solution.py:438
  1.9 2.3 %pack.1 = bf16[16,176,128]{2,1,0:T(8,128)(2,1)} custom-call(bf16[80,1024]{1,0:T(8,128)(2,1)} %q_ref.1, bf16[80,1024]{1,0:T(8,128)(2,1)} %k_ref.1, bf16[80,1024]{1,0:T(8,128)(2,1)} %v_ref.1, bf16[80,1024]{1,0:T(8,128)(2,1)} %g_ref.1, s32[1,640]{1,0:T(1,128)} %reshape.9.doc_ref), custom_call_target="tpu_custom_call" | custom-call | flops 1048576 | bytes 1048576 | tf_op jit(solution)/shard_map/pack/pallas_call | solution.py:58
  4.2 18.7 %all_to_all.10.in_ref = bf16[16,176,128]{2,1,0:T(8,128)(2,1)S(1)} all-to-all(bf16[16,176,128]{2,1,0:T(8,128)(2,1)} %pack.1), channel_id=1, replica_groups=mesh['y'=4,'zl'=2,'c'=2,'zh'=2,'x'=4] {'y','zl','c'}, dimensions={0} | all-to-all | bytes 1441792 | tf_op jit(solution)/shard_map/all_to_all | solution.py:441
  22.9 1.9 %order.1 = (s32[2]{0:T(128)S(1)}, bf16[1296,128]{1,0:T(8,128)(2,1)S(1)}, bf16[1296,128]{1,0:T(8,128)(2,1)S(1)}) custom-call(bf16[16,176,128]{2,1,0:T(8,128)(2,1)S(1)} %all_to_all.10.in_ref), custom_call_target="tpu_custom_call" | custom-call | flops 1048576 | bytes 1048576 | tf_op jit(solution)/shard_map/order/pallas_call | solution.py:58
  24.9 2.8 %collective-permute-start.3 = (bf16[1296,128]{1,0:T(8,128)(2,1)S(1)}, bf16[1296,128]{1,0:T(8,128)(2,1)S(1)}, u32[]{:S(2)}, u32[]{:S(2)}) collective-permute-start(bf16[1296,128]{1,0:T(8,128)(2,1)S(1)} %get-tuple-element.28.qg_in.refs_5_.refs_3_), channel_id=1, source_target_pairs={{0,3},{1,0},{2,1},{3,2},{4,7},{5,4},{6,5},{7,6},{8,11},{9,8},{10,9... | collective-permute-start | bytes 995336 | tf_op jit(solution)/shard_map/ppermute | solution.py:426
  27.7 0.0 collective-permute-start.1
  27.7 3.6 %collective-permute-start = (bf16[1296,128]{1,0:T(8,128)(2,1)S(1)}, bf16[1296,128]{1,0:T(8,128)(2,1)S(1)}, u32[]{:S(2)}, u32[]{:S(2)}) collective-permute-start(bf16[1296,128]{1,0:T(8,128)(2,1)S(1)} %get-tuple-element.27.kv_ref.kv0.refs_0_), channel_id=1, source_target_pairs={{0,4},{4,0},{1,5},{5,1},{2,6},{6,2},{3,7},{7,3},{8,12},{12,8},{9,1... | collective-permute-start | bytes 995336 | tf_op jit(solution)/shard_map/ppermute | solution.py:430
  31.3 1.9 %totals_own.1 = (f32[1,2,1408]{2,1,0:T(2,128)S(1)}, bf16[128,1408]{1,0:T(8,128)(2,1)S(1)}) custom-call(bf16[1296,128]{1,0:T(8,128)(2,1)S(1)} %get-tuple-element.27.kv_ref.kv0.refs_0_, bf16[1296,128]{1,0:T(8,128)(2,1)S(1)} %get-tuple-element.28.qg_in.refs_5_.refs_3_), custom_call_target="tpu_custom_call" | custom-call | flops 1250000000 | bytes 1048576 | tf_op jit(solution)/shard_map/totals_own/pallas_call | solution.py:58
  33.2 1.8 %collective-permute-done.3.qg3.refs_4_.refs_3_ = bf16[1296,128]{1,0:T(8,128)(2,1)S(1)} collective-permute-done((bf16[1296,128]{1,0:T(8,128)(2,1)S(1)}, bf16[1296,128]{1,0:T(8,128)(2,1)S(1)}, u32[]{:S(2)}, u32[]{:S(2)}) %collective-permute-start.3) | collective-permute-done | bytes 331808 | tf_op jit(solution)/shard_map/ppermute | solution.py:426
  35.1 3.8 %collective-permute-start.4 = (bf16[640,128]{1,0:T(8,128)(2,1)S(1)}, bf16[640,128]{1,0:T(8,128)(2,1)S(1)}, u32[]{:S(2)}, u32[]{:S(2)}) collective-permute-start(bf16[640,128]{1,0:T(8,128)(2,1)S(1)} %slice.9), channel_id=1, source_target_pairs={{0,3},{1,0},{2,1},{3,2},{4,7},{5,4},{6,5},{7,6},{8,11},{9,8},{10,9... | collective-permute-start | bytes 491528 | tf_op jit(solution)/shard_map/ppermute | solution.py:426
  38.8 0.0 collective-permute-done.1.qg1.refs_3_
  38.8 0.3 collective-permute-start.2
  39.1 0.0 collective-permute-done.kv_ref.kv1.refs_1_.refs_0_
  39.1 1.9 %totals_own_far.1 = (f32[1,2,1408]{2,1,0:T(2,128)S(1)}, bf16[128,1408]{1,0:T(8,128)(2,1)S(1)}) custom-call(bf16[1296,128]{1,0:T(8,128)(2,1)S(1)} %collective-permute-done.kv_ref.kv1.refs_1_.refs_0_, bf16[1296,128]{1,0:T(8,128)(2,1)S(1)} %get-tuple-element.28.qg_in.refs_5_.refs_3_), custom_call_target="tpu_custom_call" | custom-call | flops 1250000000 | bytes 1048576 | tf_op jit(solution)/shard_map/totals_own_far/pallas_call | solution.py:58
  41.0 6.2 %totals_near.1.near_ref = f32[2,2,1408]{2,1,0:T(2,128)S(1)} custom-call(bf16[1296,128]{1,0:T(8,128)(2,1)S(1)} %get-tuple-element.27.kv_ref.kv0.refs_0_, bf16[1296,128]{1,0:T(8,128)(2,1)S(1)} %collective-permute-done.kv_ref.kv1.refs_1_.refs_0_, bf16[128,1408]{1,0:T(8,128)(2,1)S(1)} %get-tuple-element.29.kvt0.refs_2_.refs_1_, ...), custom_call_target="tpu_custom_call" | custom-call | flops 5000000000 | bytes 1048576 | tf_op jit(solution)/shard_map/totals_near/pallas_call | solution.py:58
  47.2 0.0 collective-permute-done.4.qg2b
  47.2 0.0 collective-permute-done.2.qg2a
  47.2 3.1 %totals_far.1 = (f32[8,1408]{1,0:T(8,128)S(1)}, bf16[1296,128]{1,0:T(8,128)(2,1)S(1)}) custom-call(bf16[1296,128]{1,0:T(8,128)(2,1)S(1)} %get-tuple-element.27.kv_ref.kv0.refs_0_, bf16[1296,128]{1,0:T(8,128)(2,1)S(1)} %collective-permute-done.kv_ref.kv1.refs_1_.refs_0_, bf16[128,1408]{1,0:T(8,128)(2,1)S(1)} %get-tuple-element.29.kvt0.refs_2_.refs_1_, ...), custom_call_target="tpu_custom_call" | custom-call | flops 2500000000 | bytes 1048576 | tf_op jit(solution)/shard_map/totals_far/pallas_call | solution.py:58
  50.3 3.3 %collective-permute-start.7 = (f32[8,1408]{1,0:T(8,128)S(1)}, f32[8,1408]{1,0:T(8,128)S(1)}, u32[]{:S(2)}, u32[]{:S(2)}) collective-permute-start(f32[8,1408]{1,0:T(8,128)S(1)} %get-tuple-element.33.st0), channel_id=1, source_target_pairs={{0,3},{1,0},{2,1},{3,2},{4,7},{5,4},{6,5},{7,6},{8,11},{9,8},{10,9... | collective-permute-start | bytes 135176 | tf_op jit(solution)/shard_map/ppermute | solution.py:426
  53.6 0.0 collective-permute-start.6
  53.6 0.9 collective-permute-start.5
  54.6 0.8 collective-permute-done.7.st3
  55.3 3.9 %collective-permute-done.6.st2 = f32[8,1408]{1,0:T(8,128)S(1)} collective-permute-done((f32[8,1408]{1,0:T(8,128)S(1)}, f32[8,1408]{1,0:T(8,128)S(1)}, u32[]{:S(2)}, u32[]{:S(2)}) %collective-permute-start.6) | collective-permute-done | bytes 45088 | tf_op jit(solution)/shard_map/ppermute | solution.py:426
  59.3 0.1 collective-permute-done.5.st1
  59.4 6.5 %grads_far.1 = (bf16[320,128]{1,0:T(8,128)(2,1)S(1)}, bf16[320,128]{1,0:T(8,128)(2,1)S(1)}, f32[1280,128]{1,0:T(8,128)S(1)}, f32[1280,128]{1,0:T(8,128)S(1)}) custom-call(bf16[1296,128]{1,0:T(8,128)(2,1)S(1)} %get-tuple-element.27.kv_ref.kv0.refs_0_, bf16[1296,128]{1,0:T(8,128)(2,1)S(1)} %collective-permute-done.kv_ref.kv1.refs_1_.refs_0_, ...), custom_call_target="tpu_custom_call" | custom-call | flops 6000000000 | bytes 1048576 | tf_op jit(solution)/shard_map/grads_far/pallas_call | solution.py:58
  65.9 1.1 %collective-permute-start.8 = (bf16[320,128]{1,0:T(8,128)(2,1)S(1)}, bf16[320,128]{1,0:T(8,128)(2,1)S(1)}, u32[]{:S(2)}, u32[]{:S(2)}) collective-permute-start(bf16[320,128]{1,0:T(8,128)(2,1)S(1)} %get-tuple-element.38), channel_id=1, source_target_pairs={{0,3},{1,0},{2,1},{3,2},{4,7},{5,4},{6,5},{7,6},{8,11},{9,8},{10,9... | collective-permute-start | bytes 245768 | tf_op jit(solution)/shard_map/ppermute | solution.py:426
  67.0 1.2 %collective-permute-start.9 = (bf16[320,128]{1,0:T(8,128)(2,1)S(1)}, bf16[320,128]{1,0:T(8,128)(2,1)S(1)}, u32[]{:S(2)}, u32[]{:S(2)}) collective-permute-start(bf16[320,128]{1,0:T(8,128)(2,1)S(1)} %get-tuple-element.41), channel_id=1, source_target_pairs={{0,1},{1,2},{2,3},{3,0},{4,5},{5,6},{6,7},{7,4},{8,9},{9,10},{10,1... | collective-permute-start | bytes 245768 | tf_op jit(solution)/shard_map/ppermute | solution.py:426
  68.2 9.7 %grads_partner.1 = (f32[1280,128]{1,0:T(8,128)S(1)}, f32[1280,128]{1,0:T(8,128)S(1)}, f32[1280,128]{1,0:T(8,128)S(1)}, bf16[1280,128]{1,0:T(8,128)(2,1)S(1)}) custom-call(bf16[1296,128]{1,0:T(8,128)(2,1)S(1)} %collective-permute-done.kv_ref.kv1.refs_1_.refs_0_, bf16[128,1408]{1,0:T(8,128)(2,1)S(1)} %get-tuple-element.30.kvt1.refs_3_.refs_1_, ...), custom_call_target="tpu_custom_call" | custom-call | flops 8999999488 | bytes 1048576 | tf_op jit(solution)/shard_map/grads_partner/pallas_call | solution.py:58
  77.9 3.7 %collective-permute-start.12 = (bf16[1280,128]{1,0:T(8,128)(2,1)S(1)}, bf16[1280,128]{1,0:T(8,128)(2,1)S(1)}, u32[]{:S(2)}, u32[]{:S(2)}) collective-permute-start(bf16[1280,128]{1,0:T(8,128)(2,1)S(1)} %get-tuple-element.48), channel_id=1, source_target_pairs={{0,4},{4,0},{1,5},{5,1},{2,6},{6,2},{3,7},{7,3},{8,12},{12,8},{9,1... | collective-permute-start | bytes 983048 | tf_op jit(solution)/shard_map/ppermute | solution.py:430
  81.6 0.0 collective-permute-done.8.refs_6_
  81.6 3.2 %grads_near_1.1 = (bf16[640,128]{1,0:T(8,128)(2,1)S(1)}, f32[1280,128]{1,0:T(8,128)S(1)}) custom-call(bf16[1296,128]{1,0:T(8,128)(2,1)S(1)} %get-tuple-element.27.kv_ref.kv0.refs_0_, bf16[128,1408]{1,0:T(8,128)(2,1)S(1)} %get-tuple-element.29.kvt0.refs_2_.refs_1_, f32[4,2,1408]{2,1,0:T(2,128)S(1)} %rows.1.refs_4_.refs_2_, ...), custom_call_target="tpu_custom_call" | custom-call | flops 3000000000 | bytes 1048576 | tf_op jit(solution)/shard_map/grads_near_1/pallas_call | solution.py:58
  84.8 0.0 collective-permute-done.9.refs_6_
  84.8 3.2 %grads_near_3.1 = (bf16[640,128]{1,0:T(8,128)(2,1)S(1)}, f32[1280,128]{1,0:T(8,128)S(1)}) custom-call(bf16[1296,128]{1,0:T(8,128)(2,1)S(1)} %get-tuple-element.27.kv_ref.kv0.refs_0_, bf16[128,1408]{1,0:T(8,128)(2,1)S(1)} %get-tuple-element.29.kvt0.refs_2_.refs_1_, f32[4,2,1408]{2,1,0:T(2,128)S(1)} %rows.1.refs_4_.refs_2_, ...), custom_call_target="tpu_custom_call" | custom-call | flops 3000000000 | bytes 1048576 | tf_op jit(solution)/shard_map/grads_near_3/pallas_call | solution.py:58
  88.1 0.1 collective-permute-start.11
  88.1 3.2 %collective-permute-start.10 = (bf16[640,128]{1,0:T(8,128)(2,1)S(1)}, bf16[640,128]{1,0:T(8,128)(2,1)S(1)}, u32[]{:S(2)}, u32[]{:S(2)}) collective-permute-start(bf16[640,128]{1,0:T(8,128)(2,1)S(1)} %get-tuple-element.45), channel_id=1, source_target_pairs={{0,3},{1,0},{2,1},{3,2},{4,7},{5,4},{6,5},{7,6},{8,11},{9,8},{10,9... | collective-permute-start | bytes 491528 | tf_op jit(solution)/shard_map/ppermute | solution.py:426
  91.4 3.2 %grads_own.1 = (f32[1280,128]{1,0:T(8,128)S(1)}, f32[1280,128]{1,0:T(8,128)S(1)}) custom-call(bf16[1296,128]{1,0:T(8,128)(2,1)S(1)} %get-tuple-element.27.kv_ref.kv0.refs_0_, bf16[128,1408]{1,0:T(8,128)(2,1)S(1)} %get-tuple-element.29.kvt0.refs_2_.refs_1_, f32[4,2,1408]{2,1,0:T(2,128)S(1)} %rows.1.refs_4_.refs_2_, ...), custom_call_target="tpu_custom_call" | custom-call | flops 3000000000 | bytes 1048576 | tf_op jit(solution)/shard_map/grads_own/pallas_call | solution.py:58
  94.6 0.1 collective-permute-done.11.dq3
  94.7 0.0 collective-permute-done.10.dq1
  94.7 0.0 collective-permute-done.12.far_dkv
  94.7 1.1 %merge.1 = bf16[16,128,128]{2,1,0:T(8,128)(2,1)S(1)} custom-call(s32[2]{0:T(128)S(1)} %get-tuple-element.26.at_ref, f32[1280,128]{1,0:T(8,128)S(1)} %get-tuple-element.44.own_dq, bf16[640,128]{1,0:T(8,128)(2,1)S(1)} %collective-permute-done.10.dq1, bf16[640,128]{1,0:T(8,128)(2,1)S(1)} %collective-permute-done.11.dq3, ...), custom_call_target="tpu_custom_call" | custom-call | flops 1048576 | bytes 1048576 | tf_op jit(solution)/shard_map/merge/pallas_call | solution.py:58
  95.8 13.5 %all_to_all.11.in_ref = bf16[16,128,128]{2,1,0:T(8,128)(2,1)S(1)} all-to-all(bf16[16,128,128]{2,1,0:T(8,128)(2,1)S(1)} %merge.1), channel_id=1, replica_groups=mesh['y'=4,'zl'=2,'c'=2,'zh'=2,'x'=4] {'y','zl','c'}, dimensions={0} | all-to-all | bytes 1048576 | tf_op jit(solution)/shard_map/all_to_all | solution.py:527
  109.3 1.0 join.1
  (3 shorter events, 0.1 us)
Async XLA Ops:
  24.9 10.2 %collective-permute-start.3 = (bf16[1296,128]{1,0:T(8,128)(2,1)S(1)}, bf16[1296,128]{1,0:T(8,128)(2,1)S(1)}, u32[]{:S(2)}, u32[]{:S(2)}) collective-permute-start(bf16[1296,128]{1,0:T(8,128)(2,1)S(1)} %get-tuple-element.28.qg_in.refs_5_.refs_3_), channel_id=1, source_target_pairs={{0,3},{1,0},{2,1},{3,2},{4,7},{5,4},{6,5},{7,6},{8,11},{9,8},{10,9... | collective-permute-start | bytes 995336 | tf_op jit(solution)/shard_map/ppermute | solution.py:426
  27.7 11.1 %collective-permute-start.1 = (bf16[1296,128]{1,0:T(8,128)(2,1)S(1)}, bf16[1296,128]{1,0:T(8,128)(2,1)S(1)}, u32[]{:S(2)}, u32[]{:S(2)}) collective-permute-start(bf16[1296,128]{1,0:T(8,128)(2,1)S(1)} %get-tuple-element.28.qg_in.refs_5_.refs_3_), channel_id=1, source_target_pairs={{0,1},{1,2},{2,3},{3,0},{4,5},{5,6},{6,7},{7,4},{8,9},{9,10},{10,1... | collective-permute-start | bytes 995336 | tf_op jit(solution)/shard_map/ppermute | solution.py:426
  27.7 11.4 %collective-permute-start = (bf16[1296,128]{1,0:T(8,128)(2,1)S(1)}, bf16[1296,128]{1,0:T(8,128)(2,1)S(1)}, u32[]{:S(2)}, u32[]{:S(2)}) collective-permute-start(bf16[1296,128]{1,0:T(8,128)(2,1)S(1)} %get-tuple-element.27.kv_ref.kv0.refs_0_), channel_id=1, source_target_pairs={{0,4},{4,0},{1,5},{5,1},{2,6},{6,2},{3,7},{7,3},{8,12},{12,8},{9,1... | collective-permute-start | bytes 995336 | tf_op jit(solution)/shard_map/ppermute | solution.py:430
  35.1 12.1 %collective-permute-start.4 = (bf16[640,128]{1,0:T(8,128)(2,1)S(1)}, bf16[640,128]{1,0:T(8,128)(2,1)S(1)}, u32[]{:S(2)}, u32[]{:S(2)}) collective-permute-start(bf16[640,128]{1,0:T(8,128)(2,1)S(1)} %slice.9), channel_id=1, source_target_pairs={{0,3},{1,0},{2,1},{3,2},{4,7},{5,4},{6,5},{7,6},{8,11},{9,8},{10,9... | collective-permute-start | bytes 491528 | tf_op jit(solution)/shard_map/ppermute | solution.py:426
  38.8 8.4 %collective-permute-start.2 = (bf16[656,128]{1,0:T(8,128)(2,1)S(1)}, bf16[656,128]{1,0:T(8,128)(2,1)S(1)}, u32[]{:S(2)}, u32[]{:S(2)}) collective-permute-start(bf16[656,128]{1,0:T(8,128)(2,1)S(1)} %slice.8), channel_id=1, source_target_pairs={{0,1},{1,2},{2,3},{3,0},{4,5},{5,6},{6,7},{7,4},{8,9},{9,10},{10,1... | collective-permute-start | bytes 503816 | tf_op jit(solution)/shard_map/ppermute | solution.py:426
  50.3 5.0 %collective-permute-start.7 = (f32[8,1408]{1,0:T(8,128)S(1)}, f32[8,1408]{1,0:T(8,128)S(1)}, u32[]{:S(2)}, u32[]{:S(2)}) collective-permute-start(f32[8,1408]{1,0:T(8,128)S(1)} %get-tuple-element.33.st0), channel_id=1, source_target_pairs={{0,3},{1,0},{2,1},{3,2},{4,7},{5,4},{6,5},{7,6},{8,11},{9,8},{10,9... | collective-permute-start | bytes 135176 | tf_op jit(solution)/shard_map/ppermute | solution.py:426
  53.6 5.7 %collective-permute-start.6 = (f32[8,1408]{1,0:T(8,128)S(1)}, f32[8,1408]{1,0:T(8,128)S(1)}, u32[]{:S(2)}, u32[]{:S(2)}) collective-permute-start(f32[8,1408]{1,0:T(8,128)S(1)} %get-tuple-element.33.st0), channel_id=1, source_target_pairs={{0,2},{1,3},{2,0},{3,1},{4,6},{5,7},{6,4},{7,5},{8,10},{9,11},{10,... | collective-permute-start | bytes 135176 | tf_op jit(solution)/shard_map/ppermute | solution.py:426
  53.6 5.7 %collective-permute-start.5 = (f32[8,1408]{1,0:T(8,128)S(1)}, f32[8,1408]{1,0:T(8,128)S(1)}, u32[]{:S(2)}, u32[]{:S(2)}) collective-permute-start(f32[8,1408]{1,0:T(8,128)S(1)} %get-tuple-element.33.st0), channel_id=1, source_target_pairs={{0,1},{1,2},{2,3},{3,0},{4,5},{5,6},{6,7},{7,4},{8,9},{9,10},{10,1... | collective-permute-start | bytes 135176 | tf_op jit(solution)/shard_map/ppermute | solution.py:426
  65.9 15.7 %collective-permute-start.8 = (bf16[320,128]{1,0:T(8,128)(2,1)S(1)}, bf16[320,128]{1,0:T(8,128)(2,1)S(1)}, u32[]{:S(2)}, u32[]{:S(2)}) collective-permute-start(bf16[320,128]{1,0:T(8,128)(2,1)S(1)} %get-tuple-element.38), channel_id=1, source_target_pairs={{0,3},{1,0},{2,1},{3,2},{4,7},{5,4},{6,5},{7,6},{8,11},{9,8},{10,9... | collective-permute-start | bytes 245768 | tf_op jit(solution)/shard_map/ppermute | solution.py:426
  67.0 17.8 %collective-permute-start.9 = (bf16[320,128]{1,0:T(8,128)(2,1)S(1)}, bf16[320,128]{1,0:T(8,128)(2,1)S(1)}, u32[]{:S(2)}, u32[]{:S(2)}) collective-permute-start(bf16[320,128]{1,0:T(8,128)(2,1)S(1)} %get-tuple-element.41), channel_id=1, source_target_pairs={{0,1},{1,2},{2,3},{3,0},{4,5},{5,6},{6,7},{7,4},{8,9},{9,10},{10,1... | collective-permute-start | bytes 245768 | tf_op jit(solution)/shard_map/ppermute | solution.py:426
  77.9 16.7 %collective-permute-start.12 = (bf16[1280,128]{1,0:T(8,128)(2,1)S(1)}, bf16[1280,128]{1,0:T(8,128)(2,1)S(1)}, u32[]{:S(2)}, u32[]{:S(2)}) collective-permute-start(bf16[1280,128]{1,0:T(8,128)(2,1)S(1)} %get-tuple-element.48), channel_id=1, source_target_pairs={{0,4},{4,0},{1,5},{5,1},{2,6},{6,2},{3,7},{7,3},{8,12},{12,8},{9,1... | collective-permute-start | bytes 983048 | tf_op jit(solution)/shard_map/ppermute | solution.py:430
  88.1 6.6 %collective-permute-start.11 = (bf16[640,128]{1,0:T(8,128)(2,1)S(1)}, bf16[640,128]{1,0:T(8,128)(2,1)S(1)}, u32[]{:S(2)}, u32[]{:S(2)}) collective-permute-start(bf16[640,128]{1,0:T(8,128)(2,1)S(1)} %get-tuple-element.46), channel_id=1, source_target_pairs={{0,1},{1,2},{2,3},{3,0},{4,5},{5,6},{6,7},{7,4},{8,9},{9,10},{10,1... | collective-permute-start | bytes 491528 | tf_op jit(solution)/shard_map/ppermute | solution.py:426
  88.1 6.5 %collective-permute-start.10 = (bf16[640,128]{1,0:T(8,128)(2,1)S(1)}, bf16[640,128]{1,0:T(8,128)(2,1)S(1)}, u32[]{:S(2)}, u32[]{:S(2)}) collective-permute-start(bf16[640,128]{1,0:T(8,128)(2,1)S(1)} %get-tuple-element.45), channel_id=1, source_target_pairs={{0,3},{1,0},{2,1},{3,2},{4,7},{5,4},{6,5},{7,6},{8,11},{9,8},{10,9... | collective-permute-start | bytes 491528 | tf_op jit(solution)/shard_map/ppermute | solution.py:426

commit v4 on v3

--- a/solution.py
+++ b/solution.py
@@ -25,6 +25,7 @@
 LOG2_SCALE = SCALE * math.log2(math.e)
 NEG = -1e30
 BLK = ("y", "zl", "c")
+BY_HEAD = ("y", "zl", "zh")
 VMEM_LIMIT = 24 << 20
 
 
@@ -77,7 +78,7 @@
             out_ref[2 * pair, at : at + ROWS, :] = jnp.where(low, a, swap_halves(b)).astype(BF)
             out_ref[2 * pair + 1, at : at + ROWS, :] = jnp.where(low, swap_halves(a), b).astype(BF)
     group = lax.axis_index("zh") * 4 + lax.axis_index("x")
-    docs = jnp.broadcast_to(doc_ref[...].astype(F32), (16, 640))
+    docs = jnp.broadcast_to(doc_ref[...].astype(F32).reshape(1, 640), (16, 640))
     docs = pltpu.roll(docs, lax.rem(640 - group * ROWS, 640), 1)[:, 0:128].astype(BF)
     for h in range(HEADS):
         out_ref[h, 2 * ROWS : 2 * ROWS + 16, :] = docs
@@ -145,7 +146,7 @@
     return jnp.where(low, x, zero), jnp.where(low, zero, x)
 
 
-def totals_tile(kv_refs, vet_ref, col_ref, qg_ref, block, stat_ref):
+def totals_tile(kv_refs, vet_ref, col_ref, qg_ref, block, stat_ref, p_refs, top_refs):
     doc_row = doc_row_of(qg_ref.at[block])
     for q_at, q_width in ((0, LONG), (LONG, REST)):
         rest = q_at == LONG
@@ -167,8 +168,12 @@
             if rest:
                 p = jnp.where(mask, p, 0.0)
             lane = half * WIDE + lane_at(at)
-            outs.append(dot_nn(vet_ref[:, lane : lane + s.shape[0]], p.astype(BF)))
+            p = p.astype(BF)
+            outs.append(dot_nn(vet_ref[:, lane : lane + s.shape[0]], p))
             tops.append(top)
+            if not rest:
+                p_refs[half][block, at : at + STEP, :] = p
+                top_refs[half][block, at // STEP, :, 0:LONG] = top
 
         for n, (half, at) in enumerate(starts):
             width = REST if rest else STEP
@@ -194,14 +199,13 @@
     return row // STEP * 256
 
 
-def prepare_keys(kv_refs, kvt_refs, vet_ref, col_ref, fresh):
+def prepare_keys(kv_refs, kvt_refs, vet_ref, col_ref):
     for half, (kv_ref, kvt_ref) in enumerate(zip(kv_refs, kvt_refs)):
-        if fresh:
-            for at in (0, STEP, 2 * STEP, 3 * STEP, LONG):
-                width = REST if at == LONG else STEP
-                kvt_ref[:, lane_at(at) : lane_at(at) + width] = (
-                    kv_ref[at : at + width, :].astype(F32).T.astype(BF)
-                )
+        for at in (0, STEP, 2 * STEP, 3 * STEP, LONG):
+            width = REST if at == LONG else STEP
+            kvt_ref[:, lane_at(at) : lane_at(at) + width] = (
+                kv_ref[at : at + width, :].astype(F32).T.astype(BF)
+            )
         kvt = kvt_ref[...]
         vet_ref[:, half * WIDE : (half + 1) * WIDE] = jnp.where(
             row_of(kvt) < HD, jnp.ones_like(kvt), kvt
@@ -209,19 +213,17 @@
         col_ref[half] = columns_of(doc_row_of(kv_ref))
 
 
-def own_totals_kernel(kv_ref, qg_in, stat_ref, kvt_ref, vet_ref, col_ref, qg_ref):
-    prepare_keys([kv_ref], [kvt_ref], vet_ref, col_ref, True)
-    qg_ref[0] = qg_in[...]
-    totals_tile([kv_ref], vet_ref, col_ref, qg_ref, 0, stat_ref)
-
-
-def near_totals_kernel(kv0, kv1, kvt0, kvt1, qg1, qg3, stat_ref, vet_ref, col_ref, qg_ref):
-    prepare_keys([kv0, kv1], [kvt0, kvt1], vet_ref, col_ref, False)
-    qg_ref[0] = qg1[...]
-    qg_ref[1] = qg3[...]
+def totals_kernel(sets, *refs):
+    kv_refs, refs = refs[:sets], refs[sets:]
+    qg0, qg1, stat_ref = refs[:3]
+    kvt_refs, p_refs, top_refs = (refs[3 + n * sets : 3 + (n + 1) * sets] for n in range(3))
+    vet_ref, col_ref, qg_ref = refs[3 + 3 * sets :]
+    prepare_keys(kv_refs, kvt_refs, vet_ref, col_ref)
+    qg_ref[0] = qg0[...]
+    qg_ref[1] = qg1[...]
 
     def block(n, _):
-        totals_tile([kv0, kv1], vet_ref, col_ref, qg_ref, n, stat_ref)
+        totals_tile(kv_refs, vet_ref, col_ref, qg_ref, n, stat_ref, p_refs, top_refs)
         return 0
 
     lax.fori_loop(0, 2, block, 0)
@@ -234,32 +236,19 @@
     return top + jnp.log2(whole), sum(w * dot for w, (_, dot) in zip(shares, pairs)) / whole
 
 
-def far_totals_kernel(
-    kv0, kv1, kvt0, kvt1, qg2a, qg2b, own_ref, own_far_ref, near_ref, stat_ref, qg_out,
+def last_totals_kernel(
+    kv2a, kv2b, qg0, qg1, first_ref, near_ref, stat_ref, kv_ref, kvt_ref, p_ref, top_ref,
     vet_ref, col_ref, qg_ref, last_ref,
 ):
-    prepare_keys([kv0, kv1], [kvt0, kvt1], vet_ref, col_ref, False)
-    qg_ref[0, 0:CUT, :] = qg2a[...]
-    qg_ref[0, CUT:SENT, :] = qg2b[...]
-    qg_out[...] = qg_ref[0]
-    totals_tile([kv0, kv1], vet_ref, col_ref, qg_ref, 0, last_ref)
-    lse, dot = added([(ref[0, 0:1, :], ref[0, 1:2, :]) for ref in (own_ref, own_far_ref)])
-    stat_ref[0:1, :] = lse
-    stat_ref[1:2, :] = dot
-    stat_ref[2:4, :] = near_ref[0]
-    stat_ref[4:6, :] = last_ref[0]
-    stat_ref[6:8, :] = near_ref[1]
-
-
-def combined(stat_refs, block):
-    pairs = []
-    for k, ref in enumerate(stat_refs):
-        at = 2 * ((block - k) % 4)
-        pairs.append((ref[at : at + 1, :], ref[at + 1 : at + 2, :]))
-    return added(pairs)
-
-
-def pair_grads(block, half, qg_ref, kv_ref, kvt_ref, row_ref, col_ref, dq_ref, dkv_ref):
+    kv_ref[0:CUT, :] = kv2a[...]
+    kv_ref[CUT:SENT, :] = kv2b[...]
+    totals_kernel(1, kv_ref, qg0, qg1, last_ref, kvt_ref, p_ref, top_ref, vet_ref, col_ref, qg_ref)
+    for n in range(2):
+        parts = [(ref[n, 0:1, :], ref[n, 1:2, :]) for ref in (first_ref, near_ref, last_ref)]
+        stat_ref[n, 0:1, :], stat_ref[n, 1:2, :] = added(parts)
+
+
+def pair_grads(block, half, p_ref, top_ref, qg_ref, kv_ref, kvt_ref, row_ref, col_ref, dq_ref, dkv_ref):
     doc_row = doc_row_of(qg_ref.at[block])
     doc_col = col_ref[half]
     for q_at, q_width in ((0, LONG), (LONG, REST)):
@@ -271,9 +260,12 @@
         for at in range(LONG, OWN, REST) if rest else range(0, LONG, STEP):
             width = REST if rest else STEP
             kv = kv_ref[half, at : at + width, :]
-            p = jnp.exp2(dot_nt(kv, q0) * LOG2_SCALE - lse)
             if rest:
+                p = jnp.exp2(dot_nt(kv, q0) * LOG2_SCALE - lse)
                 p = jnp.where(same_doc(doc_col, doc_row), p, 0.0)
+            else:
+                top = top_ref[block, at // STEP, :, 0:LONG]
+                p = p_ref[block, at : at + STEP, :].astype(F32) * jnp.exp2(top - lse)
             ds = (p * (dot_nt(kv, g0) - dot)).astype(BF)
             dkv_ref[half, at : at + width, :] += dot_nn(p.astype(BF), g0) + dot_nn(ds, q0)
             part = dot_nn(kvt_ref[half, 0:HD, lane_at(at) : lane_at(at) + width], ds)
@@ -292,7 +284,14 @@
     blocks, own_keys = plan["blocks"], plan["halves"]
     for n, block in enumerate(blocks):
         ref["qg_all"][n] = ref["qg", block][...]
-        ref["row_all"][n] = ref["rows"][block]
+        if "rows" in ref:
+            ref["row_all"][n] = ref["rows"][block]
+        else:
+            near, far = ref["stats"], ref["stats_far"]
+            lse, dot = added([(r[k, 0:1, :], r[k, 1:2, :]) for r, k in ((near, n), (far, 1 - n))])
+            ref["row_all"][n, 0:1, :] = lse
+            ref["row_all"][n, 1:2, :] = dot
+            ref["rows_out"][n] = ref["row_all"][n]
         if ("dq_in", block) in ref:
             ref["dq_all"][n] = ref["dq_in", block][...]
         else:
@@ -310,6 +309,8 @@
         pair_grads(
             lax.div(n, len(own_keys)),
             lax.rem(n, len(own_keys)),
+            ref["p", own_keys[0]],
+            ref["top", own_keys[0]],
             *(ref[name] for name in ("qg_all", "kv_all", "kvt_all", "row_all", "col_all", "dq_all", "dkv_all")),
         )
         return 0
@@ -321,37 +322,21 @@
     for n, half in enumerate(own_keys):
         if ("dkv_out", half) in ref:
             ref["dkv_out", half][...] = ref["dkv_all"][n]
-        if ("dkv_send", half) in ref:
-            ref["dkv_send", half][...] = ref["dkv_all"][n].astype(BF)
-    if "dq_a" in ref:
-        packed = packed_dq(ref["dq_all"][0]).astype(BF)
-        ref["dq_a"][...] = packed[0 : OWN // 4, :]
-        ref["dq_b"][...] = packed[OWN // 4 : OWN // 2, :]
+    if "dkv_send" in ref:
+        ref["dkv_send"][...] = ref["dkv_all"][0].astype(BF)
     if "dq_send" in ref:
-        packed = packed_dq(ref["dq_all"][0])
-        relay = ref["relay"][...].astype(F32)
-        first, second = packed[0 : OWN // 4, :], packed[OWN // 4 : OWN // 2, :]
-        if blocks[0] == 3:
-            first = first + relay
-        else:
-            second = second + relay
-        ref["dq_send"][0 : OWN // 4, :] = first.astype(BF)
-        ref["dq_send"][OWN // 4 : OWN // 2, :] = second.astype(BF)
-
-
-def rows_kernel(st0, st1, st2, st3, row_ref):
-    for n in range(4):
-        row_ref[n, 0:1, :], row_ref[n, 1:2, :] = combined((st0, st1, st2, st3), n)
+        ref["dq_send"][...] = packed_dq(ref["dq_all"][1]).astype(BF)
 
 
 def grads(name, blocks, halves_, arrays, takes=(), gives=()):
-    ins = [("kv", h) for h in halves_] + [("kvt", h) for h in halves_] + ["rows"]
+    ins = [(kind, h) for kind in ("kv", "kvt", "p", "top") for h in halves_]
     ins += [("qg", b) for b in blocks] + list(takes)
-    shapes = {"dq_a": shape(OWN // 4, 128), "dq_b": shape(OWN // 4, 128), "dq_send": shape(OWN // 2, 128)}
-    outs = [
-        shapes[g] if g in shapes else shape(OWN, 128, dtype=BF if g[0] == "dkv_send" else F32)
-        for g in gives
-    ]
+    shapes = {
+        "dkv_send": shape(OWN, 128),
+        "dq_send": shape(OWN // 2, 128),
+        "rows_out": shape(2, 2, WIDE, dtype=F32),
+    }
+    outs = [shapes[g] if g in shapes else shape(OWN, 128, dtype=F32) for g in gives]
     nb, nh = len(blocks), len(halves_)
     scratch = dict(
         qg_all=pltpu.VMEM((nb, SENT, 128), BF),
@@ -377,14 +362,14 @@
     arrays.update(zip(gives, results))
 
 
-def merge_kernel(at_ref, own_dq, dq1, dq3, own_dkv, far_dkv, out_ref, dq_ref, dkv_ref):
+def merge_kernel(at_ref, own_dq, far_dq, own_dkv, dkv2, dkv1, dkv3, out_ref, dq_ref, dkv_ref):
     half = OWN // 2
-    far = dq1[...].astype(F32) + dq3[...].astype(F32)
+    far = far_dq[...].astype(F32)
     turned = swap_halves(far)
     low = lane_of(far) < HD
     dq_ref[0:half, :] = own_dq[0:half, :] + jnp.where(low, far, turned)
     dq_ref[half:OWN, :] = own_dq[half:OWN, :] + jnp.where(low, turned, far)
-    dkv = own_dkv[...] + far_dkv[...].astype(F32)
+    dkv = own_dkv[...] + sum(ref[...].astype(F32) for ref in (dkv2, dkv1, dkv3))
     dkv_ref[...] = jnp.where(lane_of(dkv) < HD, dkv * SCALE, dkv)
     off = at_ref[1]
     swap_edges(dq_ref, off)
@@ -427,7 +412,7 @@
 
 
 def crossed(array):
-    return lax.ppermute(array, "zh", [(0, 1), (1, 0)])
+    return lax.ppermute(array, "c", [(0, 1), (1, 0)])
 
 
 def body(queries, keys, values, out_grad, doc_ids):
@@ -435,10 +420,10 @@
         pack_kernel,
         "pack",
         [shape(16, 176, 128)],
-        [queries, keys, values, out_grad, doc_ids.reshape(1, 640)],
+        [queries, keys, values, out_grad, doc_ids],
         vmem=56 << 20,
     )[0]
-    packed = lax.all_to_all(packed, BLK, 0, 0, tiled=True)
+    packed = lax.all_to_all(packed, BY_HEAD, 0, 0, tiled=True)
     at, qg, kv = call(
         order_kernel,
         "order",
@@ -447,84 +432,75 @@
         smem_out=1,
         scratch=[pltpu.VMEM((3 * OWN, 128), F32)],
     )
-    kv_far = crossed(kv)
-    qg1, qg3 = shifted(qg, 1), shifted(qg, -1)
-    qg2 = shifted(qg1[:CUT], 1), shifted(qg3[CUT:], -1)
-
-    def side(sets, blocks):
+    qg_far = crossed(qg)
+    kv1, kv3 = shifted(kv, 1), shifted(kv, -1)
+
+    def side(sets):
         return [
             pltpu.VMEM((128, sets * WIDE), BF),
             pltpu.VMEM((sets, 384, 128), F32),
-            pltpu.VMEM((blocks, SENT, 128), BF),
+            pltpu.VMEM((2, SENT, 128), BF),
         ]
 
-    own, kvt = call(
-        own_totals_kernel,
+    stat, turned = shape(2, 2, WIDE, dtype=F32), shape(128, WIDE)
+    kept, kept_top = shape(2, LONG, LONG), shape(2, LONG // STEP, 1, 1024, dtype=F32)
+    first, kvt0, p0, top0 = call(
+        functools.partial(totals_kernel, 1),
         "totals_own",
-        [shape(1, 2, WIDE, dtype=F32), shape(128, WIDE)],
-        [kv, qg],
-        scratch=side(1, 1),
-        flops=1_250_000_000,
-    )
-    own_far, kvt_far = call(
-        own_totals_kernel,
-        "totals_own_far",
-        [shape(1, 2, WIDE, dtype=F32), shape(128, WIDE)],
-        [kv_far, qg],
-        scratch=side(1, 1),
-        flops=1_250_000_000,
-    )
-    near = call(
-        near_totals_kernel,
+        [stat, turned, kept, kept_top],
+        [kv, qg, qg_far],
+        scratch=side(1),
+        flops=2_500_000_000,
+    )
+    kv1, kv3, first = lax.optimization_barrier((kv1, kv3, first))
+    kv2 = shifted(kv1[:CUT], 1), shifted(kv3[CUT:], -1)
+    near, kvt1, kvt3, p1, p3, top1, top3 = call(
+        functools.partial(totals_kernel, 2),
         "totals_near",
-        [shape(2, 2, WIDE, dtype=F32)],
-        [kv, kv_far, kvt, kvt_far, qg1, qg3],
-        scratch=side(2, 2),
+        [stat, turned, turned, kept, kept, kept_top, kept_top],
+        [kv1, kv3, qg, qg_far],
+        scratch=side(2),
         flops=5_000_000_000,
-    )[0]
-    stats, qg2 = call(
-        far_totals_kernel,
+    )
+    stats, kv2, kvt2, p2, top2 = call(
+        last_totals_kernel,
         "totals_far",
-        [shape(8, WIDE, dtype=F32), shape(SENT, 128)],
-        [kv, kv_far, kvt, kvt_far, *qg2, own, own_far, near],
-        scratch=side(2, 1) + [pltpu.VMEM((1, 2, WIDE), F32)],
+        [stat, shape(SENT, 128), turned, kept, kept_top],
+        [*kv2, qg, qg_far, first, near],
+        scratch=side(1) + [pltpu.VMEM((2, 2, WIDE), F32)],
         flops=2_500_000_000,
     )
-    rows = call(
-        rows_kernel,
-        "rows",
-        [shape(4, 2, WIDE, dtype=F32)],
-        [stats] + [shifted(stats, k) for k in (1, 2, 3)],
-    )[0]
-
-    arrays = {("qg", n): one for n, one in enumerate((qg, qg1, qg2, qg3))}
-    arrays.update({("kv", 0): kv, ("kv", 1): kv_far, ("kvt", 0): kvt, ("kvt", 1): kvt_far, "rows": rows})
-    grads("grads_far", (2,), (0, 1), arrays, (), ("dq_a", "dq_b", ("dkv_out", 0), ("dkv_out", 1)))
-    arrays["dkv_in", 0], arrays["dkv_in", 1] = arrays["dkv_out", 0], arrays["dkv_out", 1]
-    to_three, to_one = shifted(arrays["dq_a"], 1), shifted(arrays["dq_b"], -1)
-    three = ("dq_out", 1), ("dq_out", 3), ("dq_out", 0)
-    grads("grads_partner", (1, 3, 0), (1,), arrays, [("dkv_in", 1)], [*three, ("dkv_send", 1)])
-    for n in (0, 1, 3):
-        arrays["dq_in", n] = arrays["dq_out", n]
-    dkv_far = crossed(arrays["dkv_send", 1])
-    sent = {}
-    for n, relay, by in ((1, to_one, -1), (3, to_three, 1)):
-        arrays["relay"] = relay
-        takes = [("dkv_in", 0), ("dq_in", n), "relay"]
-        grads(f"grads_near_{n}", (n,), (0,), arrays, takes, ["dq_send", ("dkv_out", 0)])
-        arrays["dkv_in", 0] = arrays["dkv_out", 0]
-        sent[n] = shifted(arrays["dq_send"], by)
-    takes = [("dkv_in", 0), ("dq_in", 0)]
-    grads("grads_own", (0,), (0,), arrays, takes, [("dq_out", 0), ("dkv_out", 0)])
+
+    arrays = {("qg", 0): qg, ("qg", 1): qg_far, "stats": stats, "stats_far": crossed(stats)}
+    arrays.update({("kv", n): one for n, one in enumerate((kv, kv1, kv2, kv3))})
+    arrays.update({("kvt", n): one for n, one in enumerate((kvt0, kvt1, kvt2, kvt3))})
+    arrays.update({("p", n): one for n, one in enumerate((p0, p1, p2, p3))})
+    arrays.update({("top", n): one for n, one in enumerate((top0, top1, top2, top3))})
+    both = (0, 1)
+    dq_in, dq_out = [("dq_in", 0), ("dq_in", 1)], [("dq_out", 0), ("dq_out", 1)]
+
+    def hand_on():
+        for n in both:
+            arrays["dq_in", n] = arrays["dq_out", n]
+
+    takes, gives, sent = ["stats", "stats_far"], ["rows_out", *dq_out, "dkv_send"], []
+    for name, n in (("grads_far", 2), ("grads_one", 1), ("grads_three", 3)):
+        grads(name, both, (n,), arrays, takes, gives)
+        hand_on()
+        arrays["rows"] = arrays["rows_out"]
+        takes, gives = ["rows", *dq_in], [*dq_out, "dkv_send"]
+        sent.append(shifted(arrays["dkv_send"], -n))
+    sent[0], arrays["dq_in", 0] = lax.optimization_barrier((sent[0], arrays["dq_in", 0]))
+    grads("grads_own", both, (0,), arrays, ["rows", *dq_in], [("dq_out", 0), "dq_send", ("dkv_out", 0)])
     merged = call(
         merge_kernel,
         "merge",
         [shape(16, 128, 128)],
-        [at, arrays["dq_out", 0], sent[1], sent[3], arrays["dkv_out", 0], dkv_far],
+        [at, arrays["dq_out", 0], crossed(arrays["dq_send"]), arrays["dkv_out", 0], *sent],
         smem_in=1,
         scratch=[pltpu.VMEM((OWN, 128), F32), pltpu.VMEM((OWN, 128), F32)],
     )[0]
-    merged = lax.all_to_all(merged, BLK, 0, 0, tiled=True)
+    merged = lax.all_to_all(merged, BY_HEAD, 0, 0, tiled=True)
     return tuple(call(join_kernel, "join", [shape(ROWS, HEADS * HD)] * 3, [merged]))
 
 

time: 111 us -> 99.6 us (0.90)
  starting transfers between devices: 23.9 us -> 8.75 us
  waiting for transfers between devices: 6.72 us -> 10.9 us
  blocking collectives: 32.2 us -> 35.4 us
  Pallas kernels: 45.4 us -> 43.5 us
  local copies, waits for them, and re-layouts: 1.29 us -> 0.02 us
    ppermute x11 -> x7, starting transfers between devices: 16.7 us -> 8.32 us  [shifted(): return lax.ppermute(array, 'x', [(i, (i + by) % 4) for i in range(4)])]
    ppermute x2 -> x3, starting transfers between devices: 7.25 us -> 0.44 us  [crossed(): return lax.ppermute(array, 'c', [(0, 1), (1, 0)])]
    all_to_all x2, blocking collectives: 32.2 us -> 35.4 us  [the longest x1 21.9 us: body(): packed = lax.all_to_all(packed, BY_HEAD, 0, 0, tiled=True)]
    ppermute x11 -> x7, waiting for transfers between devices: 6.72 us -> 9.7 us  [shifted(): return lax.ppermute(array, 'x', [(i, (i + by) % 4) for i in range(4)])]
    pallas_call x14 -> x11, Pallas kernels: 45.4 us -> 43.5 us  [call(): pl.pallas_call(kernel, out_shape=outs, in_specs=[sm] * smem_in + [vm] * (...]
    reshape x1 -> x0, local copies, waits for them, and re-layouts: 1.27 us -> none  [body(): doc_ids.reshape(1, 640)]
    ppermute x2 -> x3, waiting for transfers between devices: 0.01 us -> 1.18 us  [crossed(): return lax.ppermute(array, 'c', [(0, 1), (1, 0)])]
  transfers between devices with their start and end apart: 13 -> 10, of which waited for: 5 -> 5; matrix products, arithmetic and copies ran while one was open for 0% -> 0% of each run, Pallas kernels for 27% -> 28%
where the time goes in v4:
time: 99.6 us; the launch traced here: 99.4 us
  Pallas kernels  43.5 us (44%)
  blocking collectives  35.4 us (36%)
  waiting for transfers between devices  10.9 us (11%)
  starting transfers between devices  8.75 us (9%)
    pallas_call x11, Pallas kernels, call(): pl.pallas_call(kernel, out_shape=outs, in_specs=[sm] * smem_in + [vm] * (...  43.5 us
    all_to_all x1, blocking collectives, body(): packed = lax.all_to_all(packed, BY_HEAD, 0, 0, tiled=True)  21.9 us
    all_to_all x1, blocking collectives, body(): merged = lax.all_to_all(merged, BY_HEAD, 0, 0, tiled=True)  13.5 us
    ppermute x7, waiting for transfers between devices, shifted(): return lax.ppermute(array, 'x', [(i, (i + by) % 4) for i in range(4)])  9.7 us
    ppermute x7, starting transfers between devices, shifted(): return lax.ppermute(array, 'x', [(i, (i + by) % 4) for i in range(4)])  8.32 us
  transfers between devices with their start and end apart: 10, of which 5 were waited for; matrix products, arithmetic and copies ran while one was open for 0% of the time, Pallas kernels for 28%

profile of v4, /device:TPU:0, one launch (start us, length us, event | category | flops | bytes accessed | tf_op | source)
XLA Modules:
  0.0 99.4 jit_solution(6893998156213348768)
XLA Ops:
  0.6 2.3 %pack.1 = bf16[16,176,128]{2,1,0:T(8,128)(2,1)} custom-call(bf16[80,1024]{1,0:T(8,128)(2,1)} %q_ref.1, bf16[80,1024]{1,0:T(8,128)(2,1)} %k_ref.1, bf16[80,1024]{1,0:T(8,128)(2,1)} %v_ref.1, bf16[80,1024]{1,0:T(8,128)(2,1)} %g_ref.1, s32[640]{0:T(1024)} %doc_ref.1), custom_call_target="tpu_custom_call" | custom-call | flops 1048576 | bytes 1048576 | tf_op jit(solution)/shard_map/pack/pallas_call | solution.py:59
  2.9 21.9 %all_to_all.10.in_ref = bf16[16,176,128]{2,1,0:T(8,128)(2,1)S(1)} all-to-all(bf16[16,176,128]{2,1,0:T(8,128)(2,1)} %pack.1), channel_id=1, replica_groups=mesh['y'=4,'zl'=2,'c'=2,'zh'=2,'x'=4] {'y','zl','zh'}, dimensions={0} | all-to-all | bytes 1441792 | tf_op jit(solution)/shard_map/all_to_all | solution.py:426
  24.9 1.9 %order.1 = (s32[2]{0:T(128)S(1)}, bf16[1296,128]{1,0:T(8,128)(2,1)S(1)}, bf16[1296,128]{1,0:T(8,128)(2,1)S(1)}) custom-call(bf16[16,176,128]{2,1,0:T(8,128)(2,1)S(1)} %all_to_all.10.in_ref), custom_call_target="tpu_custom_call" | custom-call | flops 1048576 | bytes 1048576 | tf_op jit(solution)/shard_map/order/pallas_call | solution.py:59
  26.8 0.1 collective-permute-start
  26.9 2.8 %collective-permute-start.2 = (bf16[1296,128]{1,0:T(8,128)(2,1)S(1)}, bf16[1296,128]{1,0:T(8,128)(2,1)S(1)}, u32[]{:S(2)}, u32[]{:S(2)}) collective-permute-start(bf16[1296,128]{1,0:T(8,128)(2,1)S(1)} %get-tuple-element.41.refs_0_), channel_id=1, source_target_pairs={{0,3},{1,0},{2,1},{3,2},{4,7},{5,4},{6,5},{7,6},{8,11},{9,8},{10,9... | collective-permute-start | bytes 995336 | tf_op jit(solution)/shard_map/ppermute | solution.py:411
  29.8 0.0 collective-permute-start.1
  29.8 0.0 collective-permute-done.refs_2_.refs_3_.qg1.refs_5_
  29.8 4.1 %totals_own.1 = (f32[2,2,1408]{2,1,0:T(2,128)S(1)}, bf16[128,1408]{1,0:T(8,128)(2,1)S(1)}, bf16[2,960,960]{2,1,0:T(8,128)(2,1)S(1)}, f32[2,4,1,1024]{3,2,1,0:T(1,128)S(1)}) custom-call(bf16[1296,128]{1,0:T(8,128)(2,1)S(1)} %get-tuple-element.41.refs_0_, bf16[1296,128]{1,0:T(8,128)(2,1)S(1)} %get-tuple-element.42.refs_1_.refs_2_.qg0.refs_4_, ...), custom_call_target="tpu_custom_call" | custom-call | flops 2500000000 | bytes 1048576 | tf_op jit(solution)/shard_map/totals_own/pallas_call | solution.py:59
  33.8 3.6 %collective-permute-done.2.refs_1_.refs_0_ = bf16[1296,128]{1,0:T(8,128)(2,1)S(1)} collective-permute-done((bf16[1296,128]{1,0:T(8,128)(2,1)S(1)}, bf16[1296,128]{1,0:T(8,128)(2,1)S(1)}, u32[]{:S(2)}, u32[]{:S(2)}) %collective-permute-start.2) | collective-permute-done | bytes 331808 | tf_op jit(solution)/shard_map/ppermute | solution.py:411
  37.4 3.4 %collective-permute-done.1.refs_0_ = bf16[1296,128]{1,0:T(8,128)(2,1)S(1)} collective-permute-done((bf16[1296,128]{1,0:T(8,128)(2,1)S(1)}, bf16[1296,128]{1,0:T(8,128)(2,1)S(1)}, u32[]{:S(2)}, u32[]{:S(2)}) %collective-permute-start.1) | collective-permute-done | bytes 331808 | tf_op jit(solution)/shard_map/ppermute | solution.py:411
  40.9 0.4 collective-permute-start.4
  41.2 1.7 %collective-permute-start.3 = (bf16[656,128]{1,0:T(8,128)(2,1)S(1)}, bf16[656,128]{1,0:T(8,128)(2,1)S(1)}, u32[]{:S(2)}, u32[]{:S(2)}) collective-permute-start(bf16[656,128]{1,0:T(8,128)(2,1)S(1)} %slice.6), channel_id=1, source_target_pairs={{0,1},{1,2},{2,3},{3,0},{4,5},{5,6},{6,7},{7,4},{8,9},{9,10},{10,1... | collective-permute-start | bytes 503816 | tf_op jit(solution)/shard_map/ppermute | solution.py:411
  43.0 6.7 %totals_near.1 = (f32[2,2,1408]{2,1,0:T(2,128)S(1)}, bf16[128,1408]{1,0:T(8,128)(2,1)S(1)}, bf16[128,1408]{1,0:T(8,128)(2,1)S(1)}, bf16[2,960,960]{2,1,0:T(8,128...) custom-call(bf16[1296,128]{1,0:T(8,128)(2,1)S(1)} %collective-permute-don, ...), custom_call_target="tpu_custom_call" | custom-call | flops 5000000000 | bytes 1048576 | tf_op jit(solution)/shard_map/totals_near/pallas_call | solution.py:59
  49.6 0.0 collective-permute-done.4.kv2b
  49.6 0.0 collective-permute-done.3.kv2a
  49.6 4.1 %totals_far.1 = (f32[2,2,1408]{2,1,0:T(2,128)S(1)}, bf16[1296,128]{1,0:T(8,128)(2,1)S(1)}, bf16[128,1408]{1,0:T(8,128)(2,1)S(1)}, bf16[2,960,960]{2,1,0:T(8,128)(2,1)S(1)}, f32[2,4,1,1024]{3,2,1,0:T(1,128)S(1)}) custom-call(bf16[656,128]{1,0:T(8,128)(2,1)S(1)} %collective-permute-done.3.kv2a, bf16[640,128]{1,0:T(8,128)(2,1)S(1)} %collective-permute-done.4.kv2b, ...), custom_call_target="tpu_custom_call" | custom-call | flops 2500000000 | bytes 1048576 | tf_op jit(solution)/shard_map/totals_far/pallas_call | solution.py:59
  53.8 0.3 collective-permute-start.5
  54.1 1.2 %collective-permute-done.5.refs_7_ = f32[2,2,1408]{2,1,0:T(2,128)S(1)} collective-permute-done((f32[2,2,1408]{2,1,0:T(2,128)S(1)}, f32[2,2,1408]{2,1,0:T(2,128)S(1)}, u32[]{:S(2)}, u32[]{:S(2)}) %collective-permute-start.5) | collective-permute-done | bytes 22560 | tf_op jit(solution)/shard_map/ppermute | solution.py:415
  55.2 5.5 %grads_far.1 = (f32[2,2,1408]{2,1,0:T(2,128)S(1)}, f32[1280,128]{1,0:T(8,128)S(1)}, f32[1280,128]{1,0:T(8,128)S(1)}, bf16[1280,128]{1,0:T(8,128)(2,1)S(1)}) custom-call(bf16[1296,128]{1,0:T(8,128)(2,1)S(1)} %get-tuple-element.51.refs_0_, bf16[128,1408]{1,0:T(8,128)(2,1)S(1)} %get-tuple-element.52.refs_1_, ...), custom_call_target="tpu_custom_call" | custom-call | flops 6000000000 | bytes 1048576 | tf_op jit(solution)/shard_map/grads_far/pallas_call | solution.py:59
  60.7 0.1 collective-permute-start.6
  60.8 5.5 %grads_one.1 = (f32[1280,128]{1,0:T(8,128)S(1)}, f32[1280,128]{1,0:T(8,128)S(1)}, bf16[1280,128]{1,0:T(8,128)(2,1)S(1)}) custom-call(bf16[1296,128]{1,0:T(8,128)(2,1)S(1)} %collective-permute-done.1.refs_0_, bf16[128,1408]{1,0:T(8,128)(2,1)S(1)} %get-tuple-element.61.refs_1_, bf16[2,960,960]{2,1,0:T(8,128)(2,1)S(1)} %get-tuple-element.62.refs_2_, ...), custom_call_target="tpu_custom_call" | custom-call | flops 6000000000 | bytes 1048576 | tf_op jit(solution)/shard_map/grads_one/pallas_call | solution.py:59
  66.3 5.6 %grads_three.1 = (f32[1280,128]{1,0:T(8,128)S(1)}, f32[1280,128]{1,0:T(8,128)S(1)}, bf16[1280,128]{1,0:T(8,128)(2,1)S(1)}) custom-call(bf16[1296,128]{1,0:T(8,128)(2,1)S(1)} %collective-permute-done.2.refs_1_.refs_0_, bf16[128,1408]{1,0:T(8,128)(2,1)S(1)} %get-tuple-element.58.refs_1_, bf16[2,960,960]{2,1,0:T(8,128)(2,1)S(1)} %get-tuple-element.59.refs_2_, ...), custom_call_target="tpu_custom_call" | custom-call | flops 6000000000 | bytes 1048576 | tf_op jit(solution)/shard_map/grads_three/pallas_call | solution.py:59
  72.0 2.4 %collective-permute-start.9 = (bf16[1280,128]{1,0:T(8,128)(2,1)S(1)}, bf16[1280,128]{1,0:T(8,128)(2,1)S(1)}, u32[]{:S(2)}, u32[]{:S(2)}) collective-permute-start(bf16[1280,128]{1,0:T(8,128)(2,1)S(1)} %get-tuple-element.76), channel_id=1, source_target_pairs={{0,1},{1,2},{2,3},{3,0},{4,5},{5,6},{6,7},{7,4},{8,9},{9,10},{10,1... | collective-permute-start | bytes 983048 | tf_op jit(solution)/shard_map/ppermute | solution.py:411
  74.3 0.9 collective-permute-start.8
  75.3 0.0 collective-permute-done.6.dkv2
  75.3 5.5 %grads_own.1 = (f32[1280,128]{1,0:T(8,128)S(1)}, bf16[640,128]{1,0:T(8,128)(2,1)S(1)}, f32[1280,128]{1,0:T(8,128)S(1)}) custom-call(bf16[1296,128]{1,0:T(8,128)(2,1)S(1)} %get-tuple-element.41.refs_0_, bf16[128,1408]{1,0:T(8,128)(2,1)S(1)} %get-tuple-element.43.refs_1_, bf16[2,960,960]{2,1,0:T(8,128)(2,1)S(1)} %get-tuple-element.44.refs_2_, ...), custom_call_target="tpu_custom_call" | custom-call | flops 6000000000 | bytes 1048576 | tf_op jit(solution)/shard_map/grads_own/pallas_call | solution.py:59
  80.8 0.1 collective-permute-start.7
  80.9 2.2 %collective-permute-done.9.dkv3 = bf16[1280,128]{1,0:T(8,128)(2,1)S(1)} collective-permute-done((bf16[1280,128]{1,0:T(8,128)(2,1)S(1)}, bf16[1280,128]{1,0:T(8,128)(2,1)S(1)}, u32[]{:S(2)}, u32[]{:S(2)}) %collective-permute-start.9) | collective-permute-done | bytes 327712 | tf_op jit(solution)/shard_map/ppermute | solution.py:411
  83.1 0.5 collective-permute-done.8.dkv1
  83.6 0.0 collective-permute-done.7.far_dq
  83.6 1.3 %merge.1 = bf16[16,128,128]{2,1,0:T(8,128)(2,1)S(1)} custom-call(s32[2]{0:T(128)S(1)} %get-tuple-element.40.at_ref, f32[1280,128]{1,0:T(8,128)S(1)} %get-tuple-element.71.own_dq, bf16[640,128]{1,0:T(8,128)(2,1)S(1)} %collective-permute-done.7.far_dq, f32[1280,128]{1,0:T(8,128)S(1)} %get-tuple-element.73.own_dkv, ...), custom_call_target="tpu_custom_call" | custom-call | flops 1048576 | bytes 1048576 | tf_op jit(solution)/shard_map/merge/pallas_call | solution.py:59
  84.9 13.5 %all_to_all.11.in_ref = bf16[16,128,128]{2,1,0:T(8,128)(2,1)S(1)} all-to-all(bf16[16,128,128]{2,1,0:T(8,128)(2,1)S(1)} %merge.1), channel_id=1, replica_groups=mesh['y'=4,'zl'=2,'c'=2,'zh'=2,'x'=4] {'y','zl','zh'}, dimensions={0} | all-to-all | bytes 1048576 | tf_op jit(solution)/shard_map/all_to_all | solution.py:503
  98.4 1.0 %join.1 = (bf16[80,1024]{1,0:T(8,128)(2,1)}, bf16[80,1024]{1,0:T(8,128)(2,1)}, bf16[80,1024]{1,0:T(8,128)(2,1)}) custom-call(bf16[16,128,128]{2,1,0:T(8,128)(2,1)S(1)} %all_to_all.11.in_ref), custom_call_target="tpu_custom_call" | custom-call | flops 1048576 | bytes 1048576 | tf_op jit(solution)/shard_map/join/pallas_call | solution.py:59
  (2 shorter events, 0.0 us)
Async XLA Ops:
  26.8 2.9 %collective-permute-start = (bf16[1296,128]{1,0:T(8,128)(2,1)S(1)}, bf16[1296,128]{1,0:T(8,128)(2,1)S(1)}, u32[]{:S(2)}, u32[]{:S(2)}) collective-permute-start(bf16[1296,128]{1,0:T(8,128)(2,1)S(1)} %get-tuple-element.42.refs_1_.refs_2_.qg0.refs_4_), channel_id=1, source_target_pairs={{0,8},{8,0},{1,9},{9,1},{2,10},{10,2},{3,11},{11,3},{4,12},{12,4},... | collective-permute-start | bytes 995336 | tf_op jit(solution)/shard_map/ppermute | solution.py:415
  26.9 10.5 %collective-permute-start.2 = (bf16[1296,128]{1,0:T(8,128)(2,1)S(1)}, bf16[1296,128]{1,0:T(8,128)(2,1)S(1)}, u32[]{:S(2)}, u32[]{:S(2)}) collective-permute-start(bf16[1296,128]{1,0:T(8,128)(2,1)S(1)} %get-tuple-element.41.refs_0_), channel_id=1, source_target_pairs={{0,3},{1,0},{2,1},{3,2},{4,7},{5,4},{6,5},{7,6},{8,11},{9,8},{10,9... | collective-permute-start | bytes 995336 | tf_op jit(solution)/shard_map/ppermute | solution.py:411
  29.8 11.1 %collective-permute-start.1 = (bf16[1296,128]{1,0:T(8,128)(2,1)S(1)}, bf16[1296,128]{1,0:T(8,128)(2,1)S(1)}, u32[]{:S(2)}, u32[]{:S(2)}) collective-permute-start(bf16[1296,128]{1,0:T(8,128)(2,1)S(1)} %get-tuple-element.41.refs_0_), channel_id=1, source_target_pairs={{0,1},{1,2},{2,3},{3,0},{4,5},{5,6},{6,7},{7,4},{8,9},{9,10},{10,1... | collective-permute-start | bytes 995336 | tf_op jit(solution)/shard_map/ppermute | solution.py:411
  40.9 8.8 %collective-permute-start.4 = (bf16[640,128]{1,0:T(8,128)(2,1)S(1)}, bf16[640,128]{1,0:T(8,128)(2,1)S(1)}, u32[]{:S(2)}, u32[]{:S(2)}) collective-permute-start(bf16[640,128]{1,0:T(8,128)(2,1)S(1)} %slice.7), channel_id=1, source_target_pairs={{0,3},{1,0},{2,1},{3,2},{4,7},{5,4},{6,5},{7,6},{8,11},{9,8},{10,9... | collective-permute-start | bytes 491528 | tf_op jit(solution)/shard_map/ppermute | solution.py:411
  41.2 8.4 %collective-permute-start.3 = (bf16[656,128]{1,0:T(8,128)(2,1)S(1)}, bf16[656,128]{1,0:T(8,128)(2,1)S(1)}, u32[]{:S(2)}, u32[]{:S(2)}) collective-permute-start(bf16[656,128]{1,0:T(8,128)(2,1)S(1)} %slice.6), channel_id=1, source_target_pairs={{0,1},{1,2},{2,3},{3,0},{4,5},{5,6},{6,7},{7,4},{8,9},{9,10},{10,1... | collective-permute-start | bytes 503816 | tf_op jit(solution)/shard_map/ppermute | solution.py:411
  53.8 1.5 %collective-permute-start.5 = (f32[2,2,1408]{2,1,0:T(2,128)S(1)}, f32[2,2,1408]{2,1,0:T(2,128)S(1)}, u32[]{:S(2)}, u32[]{:S(2)}) collective-permute-start(f32[2,2,1408]{2,1,0:T(2,128)S(1)} %get-tuple-element.55.refs_6_), channel_id=1, source_target_pairs={{0,8},{8,0},{1,9},{9,1},{2,10},{10,2},{3,11},{11,3},{4,12},{12,4},... | collective-permute-start | bytes 67592 | tf_op jit(solution)/shard_map/ppermute | solution.py:415
  60.7 14.5 %collective-permute-start.6 = (bf16[1280,128]{1,0:T(8,128)(2,1)S(1)}, bf16[1280,128]{1,0:T(8,128)(2,1)S(1)}, u32[]{:S(2)}, u32[]{:S(2)}) collective-permute-start(bf16[1280,128]{1,0:T(8,128)(2,1)S(1)} %get-tuple-element.57), channel_id=1, source_target_pairs={{0,2},{1,3},{2,0},{3,1},{4,6},{5,7},{6,4},{7,5},{8,10},{9,11},{10,... | collective-permute-start | bytes 983048 | tf_op jit(solution)/shard_map/ppermute | solution.py:411
  72.0 11.1 %collective-permute-start.9 = (bf16[1280,128]{1,0:T(8,128)(2,1)S(1)}, bf16[1280,128]{1,0:T(8,128)(2,1)S(1)}, u32[]{:S(2)}, u32[]{:S(2)}) collective-permute-start(bf16[1280,128]{1,0:T(8,128)(2,1)S(1)} %get-tuple-element.76), channel_id=1, source_target_pairs={{0,1},{1,2},{2,3},{3,0},{4,5},{5,6},{6,7},{7,4},{8,9},{9,10},{10,1... | collective-permute-start | bytes 983048 | tf_op jit(solution)/shard_map/ppermute | solution.py:411
  74.3 9.3 %collective-permute-start.8 = (bf16[1280,128]{1,0:T(8,128)(2,1)S(1)}, bf16[1280,128]{1,0:T(8,128)(2,1)S(1)}, u32[]{:S(2)}, u32[]{:S(2)}) collective-permute-start(bf16[1280,128]{1,0:T(8,128)(2,1)S(1)} %get-tuple-element.75), channel_id=1, source_target_pairs={{0,3},{1,0},{2,1},{3,2},{4,7},{5,4},{6,5},{7,6},{8,11},{9,8},{10,9... | collective-permute-start | bytes 983048 | tf_op jit(solution)/shard_map/ppermute | solution.py:411
  80.8 2.8 %collective-permute-start.7 = (bf16[640,128]{1,0:T(8,128)(2,1)S(1)}, bf16[640,128]{1,0:T(8,128)(2,1)S(1)}, u32[]{:S(2)}, u32[]{:S(2)}) collective-permute-start(bf16[640,128]{1,0:T(8,128)(2,1)S(1)} %get-tuple-element.72), channel_id=1, source_target_pairs={{0,8},{8,0},{1,9},{9,1},{2,10},{10,2},{3,11},{11,3},{4,12},{12,4},... | collective-permute-start | bytes 491528 | tf_op jit(solution)/shard_map/ppermute | solution.py:415

commit v5 on v4

v5 whole, which is shorter than its diff:
```python
import functools
import math

import jax
import jax.numpy as jnp
from jax import lax
from jax.experimental import pallas as pl
from jax.experimental.pallas import tpu as pltpu
from jax.sharding import Mesh
from jax.sharding import PartitionSpec as P

BF = jnp.bfloat16
F32 = jnp.float32
HD = 64
HEADS = 16
ROWS = 80
OWN = 1280
LONG = 960
REST = OWN - LONG
SENT = OWN + 16
STEP = 240
WIDE = 1408
SCALE = 1.0 / math.sqrt(HD)
LOG2_SCALE = SCALE * math.log2(math.e)
NEG = -1e30
BLK = ("y", "zl", "c")
BY_HEAD = ("y", "zl", "zh")
VMEM_LIMIT = 24 << 20


def dot_nt(a, b):
    return lax.dot_general(a, b, (((1,), (1,)), ((), ())), preferred_element_type=F32)


def dot_nn(a, b):
    return lax.dot_general(a, b, (((1,), (0,)), ((), ())), preferred_element_type=F32)


def lane_of(x):
    return lax.broadcasted_iota(jnp.int32, x.shape, x.ndim - 1)


def row_of(x):
    return lax.broadcasted_iota(jnp.int32, x.shape, 0)


def swap_halves(x):
    return pltpu.roll(x, HD, 1)


def shape(*dims, dtype=BF):
    return jax.ShapeDtypeStruct(dims, dtype)


def call(kernel, name, outs, args, smem_in=0, smem_out=0, scratch=(), flops=1 << 20, vmem=VMEM_LIMIT):
    vm = pl.BlockSpec(memory_space=pltpu.VMEM)
    sm = pl.BlockSpec(memory_space=pltpu.SMEM)
    return pl.pallas_call(
        kernel,
        out_shape=outs,
        in_specs=[sm] * smem_in + [vm] * (len(args) - smem_in),
        out_specs=[sm] * smem_out + [vm] * (len(outs) - smem_out),
        scratch_shapes=list(scratch),
        compiler_params=pltpu.CompilerParams(vmem_limit_bytes=vmem),
        cost_estimate=pl.CostEstimate(flops=flops, bytes_accessed=1 << 20, transcendentals=0),
        name=name,
    )(*args)


def pack_kernel(q_ref, k_ref, v_ref, g_ref, doc_ref, out_ref):
    for pair in range(HEADS // 2):
        cols = slice(pair * 128, pair * 128 + 128)
        for a_ref, b_ref, at in ((q_ref, g_ref, 0), (k_ref, v_ref, ROWS)):
            a = a_ref[:, cols].astype(F32)
            b = b_ref[:, cols].astype(F32)
            low = lane_of(a) < HD
            out_ref[2 * pair, at : at + ROWS, :] = jnp.where(low, a, swap_halves(b)).astype(BF)
            out_ref[2 * pair + 1, at : at + ROWS, :] = jnp.where(low, swap_halves(a), b).astype(BF)
    group = lax.axis_index("zh") * 4 + lax.axis_index("x")
    docs = jnp.broadcast_to(doc_ref[...].astype(F32).reshape(1, 640), (16, 640))
    docs = pltpu.roll(docs, lax.rem(640 - group * ROWS, 640), 1)[:, 0:128].astype(BF)
    for h in range(HEADS):
        out_ref[h, 2 * ROWS : 2 * ROWS + 16, :] = docs


def swap_edges(ref, off):
    first = ref[0:16, :]
    last = ref[LONG : LONG + 16, :]
    early = row_of(first) < off
    ref[0:16, :] = jnp.where(early, last, first)
    ref[LONG : LONG + 16, :] = jnp.where(early, first, last)


def columns_of(doc_row):
    return jnp.broadcast_to(doc_row, (128, doc_row.shape[1])).T


def order_kernel(in_ref, at_ref, qg_ref, kv_ref, doc_ref):
    doc_at = slice(2 * ROWS, 2 * ROWS + 16)
    docs = jnp.concatenate([in_ref[b, doc_at, :].astype(F32)[0:1, :] for b in range(16)], axis=0)
    before = jnp.where((docs < docs[8:9, 0:1]) & (lane_of(docs) < ROWS), 1.0, 0.0)
    turned = jnp.concatenate([docs, jnp.zeros((112, 128), F32)], axis=0).T
    for b in range(16):
        doc_ref[OWN * 2 + b * ROWS : OWN * 2 + (b + 1) * ROWS, :] = jnp.broadcast_to(
            turned[0:ROWS, b : b + 1], (ROWS, 128)
        )
    start = jnp.sum(before).astype(jnp.int32)
    off = start & 15
    at_ref[0] = start - off
    at_ref[1] = off
    first = lax.shift_right_logical(start, 4)

    def place(i):
        at = first + i
        return at - jnp.where(at >= OWN // 16, OWN // 16, 0)

    def move(i, _):
        at = place(i)
        chunk = lax.shift_right_logical(at * 205, 10)
        part = (at - chunk * 5) * 16
        rows = pl.ds(pl.multiple_of(i * 16, 16), 16)
        qg_ref[rows, :] = in_ref[chunk, pl.ds(pl.multiple_of(part, 16), 16), :]
        kv_ref[rows, :] = in_ref[chunk, pl.ds(pl.multiple_of(ROWS + part, 16), 16), :]
        return 0

    lax.fori_loop(0, OWN // 16, move, 0, unroll=8)

    def move_docs(i, _):
        at = place(i) * 16
        rows = pl.ds(pl.multiple_of(i * 16, 16), 16)
        doc_ref[rows, :] = doc_ref[pl.ds(pl.multiple_of(OWN * 2 + at, 16), 16), :]
        return 0

    move_docs(0, 0)
    lax.fori_loop(LONG // 16, OWN // 16, move_docs, 0, unroll=4)
    for ref in (qg_ref, kv_ref, doc_ref):
        swap_edges(ref, off)
    docs = doc_ref[LONG : LONG + 384, :].T
    lines = [docs[0:1, n * 128 : n * 128 + 128] for n in range(3)]
    block = jnp.concatenate(lines + [jnp.zeros((13, 128), F32)], axis=0).astype(BF)
    qg_ref[OWN:SENT, :] = block
    kv_ref[OWN:SENT, :] = block


def doc_row_of(ref):
    lines = ref[OWN:SENT, :].astype(F32)
    return jnp.concatenate([lines[n : n + 1, :] for n in range(3)], axis=1)


def same_doc(doc_cols, doc_row):
    wide = jnp.concatenate([doc_cols] * (2 * REST // 128), axis=1)
    return (wide == doc_row)[0:REST, :]


def halves(x):
    zero = jnp.zeros_like(x)
    low = lane_of(x) < HD
    return jnp.where(low, x, zero), jnp.where(low, zero, x)


def totals_of(kv_refs, vet_ref, qg, grad_t, starts, mask_of, keep):
    q0, _ = halves(qg)
    scores, tops, outs = {}, [], []

    def finish(half, at, width):
        s = scores.pop((half, at))
        mask = mask_of(half) if mask_of else None
        if mask_of:
            s = jnp.where(mask, s, NEG)
        top = jnp.max(s, axis=0, keepdims=True) * LOG2_SCALE
        p = jnp.exp2(s * LOG2_SCALE - top)
        if mask_of:
            p = jnp.where(mask, p, 0.0)
        p = p.astype(BF)
        keep(half, at, p, top)
        lane = half * WIDE + lane_at(at)
        outs.append(dot_nn(vet_ref[:, lane : lane + width], p))
        tops.append(top)

    for n, (half, at, width) in enumerate(starts):
        scores[half, at] = dot_nt(kv_refs[half][at : at + width, :], q0)
        if n:
            finish(*starts[n - 1])
    finish(*starts[-1])
    top = functools.reduce(jnp.maximum, tops)
    shares = [jnp.exp2(t - top) for t in tops]
    total = sum(o[0:1, :] * w for o, w in zip(outs, shares))
    out = sum(o[HD:, :] * w for o, w in zip(outs, shares))
    dot = jnp.sum(out * grad_t.astype(F32), axis=0, keepdims=True)
    if mask_of:
        empty = total <= 0.0
        total = jnp.where(empty, 1.0, total)
        top = jnp.where(empty, NEG, top)
    return top + jnp.log2(total), dot / total


def lane_at(row):
    return row // STEP * 256


def prepare_keys(kv_refs, kvt_refs, vet_ref, col_ref):
    for half, (kv_ref, kvt_ref) in enumerate(zip(kv_refs, kvt_refs)):
        for at in (0, STEP, 2 * STEP, 3 * STEP, LONG):
            width = REST if at == LONG else STEP
            kvt_ref[:, lane_at(at) : lane_at(at) + width] = (
                kv_ref[at : at + width, :].T
            )
        kvt = kvt_ref[...]
        vet_ref[:, half * WIDE : (half + 1) * WIDE] = jnp.where(
            row_of(kvt) < HD, jnp.ones_like(kvt), kvt
        )
        col_ref[half] = columns_of(doc_row_of(kv_ref))


def rest_rows(first, second):
    return jnp.concatenate([first[LONG:OWN, :], second[LONG:OWN, :]], axis=0)


def totals(
    kv_refs, qg0, qg1, gt_ref, gt_rest_ref, stat_ref, kvt_refs, p_refs, rest_refs, top_refs,
    vet_ref, col_ref, qg_ref,
):
    prepare_keys(kv_refs, kvt_refs, vet_ref, col_ref)
    qg_ref[0] = qg0[0:LONG, :]
    qg_ref[1] = qg1[0:LONG, :]

    def block(n, _):
        def keep(half, at, p, top):
            p_refs[half][n, at : at + STEP, :] = p
            top_refs[half][n, at // STEP, :, 0:LONG] = top

        starts = [(half, at, STEP) for half in range(len(kv_refs)) for at in range(0, LONG, STEP)]
        lse, dot = totals_of(kv_refs, vet_ref, qg_ref[n], gt_ref[n], starts, None, keep)
        stat_ref[n, 0:1, 0:LONG] = lse
        stat_ref[n, 1:2, 0:LONG] = dot
        return 0

    lax.fori_loop(0, 2, block, 0)

    def keep_rest(half, at, p, top):
        rest_refs[half][...] = p
        top_refs[half][2, 0, :, 0 : 2 * REST] = top

    doc_row = jnp.concatenate([doc_row_of(ref)[:, 0:REST] for ref in (qg0, qg1)], axis=1)
    lse, dot = totals_of(
        kv_refs,
        vet_ref,
        rest_rows(qg0, qg1),
        gt_rest_ref[...],
        [(half, LONG, REST) for half in range(len(kv_refs))],
        lambda half: same_doc(col_ref[half], doc_row),
        keep_rest,
    )
    stat_ref[2, 0:1, 0 : 2 * REST] = lse
    stat_ref[2, 1:2, 0 : 2 * REST] = dot


def added(pairs):
    top = functools.reduce(jnp.maximum, [lse for lse, _ in pairs])
    shares = [jnp.exp2(lse - top) for lse, _ in pairs]
    whole = sum(shares)
    return top + jnp.log2(whole), sum(w * dot for w, (_, dot) in zip(shares, pairs)) / whole


def own_totals_kernel(
    kv, qg0, qg1, stat_ref, gt_ref, gt_rest_ref, kvt, p, rest, top, *scratch
):
    for n, ref in enumerate((qg0, qg1)):
        gt_ref[n] = ref[0:LONG, :].T[HD:, :]
    gt_rest_ref[...] = rest_rows(qg0, qg1).T[HD:, :]
    totals([kv], qg0, qg1, gt_ref, gt_rest_ref, stat_ref, [kvt], [p], [rest], [top], *scratch)


def near_totals_kernel(kv1, kv3, qg0, qg1, gt_ref, gt_rest_ref, stat_ref, *refs):
    kvts, ps, rests, tops = (refs[2 * n : 2 * n + 2] for n in range(4))
    totals(
        [kv1, kv3], qg0, qg1, gt_ref, gt_rest_ref, stat_ref, kvts, ps, rests, tops, *refs[8:]
    )


def last_totals_kernel(
    kv, qg0, qg1, gt_ref, gt_rest_ref, first_ref, near_ref,
    stat_ref, kvt, p, rest, top, vet_ref, col_ref, qg_ref, last_ref,
):
    totals(
        [kv], qg0, qg1, gt_ref, gt_rest_ref, last_ref, [kvt], [p], [rest], [top],
        vet_ref, col_ref, qg_ref,
    )
    for n in range(3):
        parts = [(ref[n, 0:1, :], ref[n, 1:2, :]) for ref in (first_ref, near_ref, last_ref)]
        stat_ref[n, 0:1, :], stat_ref[n, 1:2, :] = added(parts)


def tile_grads(qg, starts, weights_of, dot, kv_ref, kvt_ref, dkv_ref):
    q0, g0 = halves(qg)
    acc = None
    for at, width in starts:
        kv = kv_ref[at : at + width, :]
        p = weights_of(at)
        ds = (p * (dot_nt(kv, g0) - dot)).astype(BF)
        dkv_ref[at : at + width, :] += dot_nn(p.astype(BF), g0) + dot_nn(ds, q0)
        part = dot_nn(kvt_ref[0:HD, lane_at(at) : lane_at(at) + width], ds)
        acc = part if acc is None else acc + part
    return acc


def packed_dq(dq):
    low = lax.broadcasted_iota(jnp.int32, (OWN // 2, 128), 1) < HD
    return jnp.where(low, dq[0 : OWN // 2, :], dq[OWN // 2 : OWN, :])


def grads_kernel(names, *refs):
    ref = dict(zip(names, refs))
    dq_ref, dq_rest_ref, dkv_ref, row_ref = ref["dq"], ref["dq_rest"], ref["dkv"], ref["row"]
    kv_ref, kvt_ref, qg_ref = ref["kv"], ref["kvt"], ref["qg"]
    p_ref, rest_ref, top_ref = ref["p"], ref["rest"], ref["top"]
    if "rows" in ref:
        row_ref[...] = ref["rows"][...]
    else:
        for n in range(3):
            mine = [ref["stats"][n, k : k + 1, :] for k in range(2)]
            far = [ref["stats_far"][(1, 0, 2)[n], k : k + 1, :] for k in range(2)]
            if n == 2:
                far = [
                    jnp.concatenate([x[:, REST : 2 * REST], x[:, 0:REST], x[:, 2 * REST :]], axis=1)
                    for x in far
                ]
            row_ref[n, 0:1, :], row_ref[n, 1:2, :] = added([mine, far])
        ref["rows_out"][...] = row_ref[...]
    for n in range(2):
        qg_ref[n] = ref["qg", n][0:LONG, :]
    for out, known in ((dq_ref, "dq_in"), (dq_rest_ref, "dq_rest_in")):
        out[...] = ref[known][...] if known in ref else jnp.zeros_like(out)
    dkv_ref[...] = jnp.zeros_like(dkv_ref)

    def block(n, _):
        lse = row_ref[n, 0:1, 0:LONG]

        def weights_of(at):
            share = jnp.exp2(top_ref[n, at // STEP, :, 0:LONG] - lse)
            return p_ref[n, at : at + STEP, :].astype(F32) * share

        starts = [(at, STEP) for at in range(0, LONG, STEP)]
        dot = row_ref[n, 1:2, 0:LONG]
        dq_ref[n] += tile_grads(qg_ref[n], starts, weights_of, dot, kv_ref, kvt_ref, dkv_ref)
        return 0

    lax.fori_loop(0, 2, block, 0)
    both = slice(0, 2 * REST)
    share = jnp.exp2(top_ref[2, 0, :, both] - row_ref[2, 0:1, both])
    dq_rest_ref[...] += tile_grads(
        rest_rows(ref["qg", 0], ref["qg", 1]),
        [(LONG, REST)],
        lambda at: rest_ref[...].astype(F32) * share,
        row_ref[2, 1:2, both],
        kv_ref,
        kvt_ref,
        dkv_ref,
    )
    if "dkv_out" in ref:
        ref["dkv_out"][...] = dkv_ref[...]
    if "dkv_send" in ref:
        relay = ref["relay"][...].astype(F32) if "relay" in ref else 0.0
        ref["dkv_send"][...] = (dkv_ref[...] + relay).astype(BF)
    if "dq_send" in ref:
        rows_ref = ref["dq_rows"]
        rest = jnp.concatenate([dq_rest_ref[...] * SCALE] * 2, axis=0).T
        for n, out in enumerate((ref["dq_out"], rows_ref)):
            out[0:LONG, :] = jnp.concatenate([dq_ref[n] * SCALE] * 2, axis=0).T
            out[LONG:OWN, :] = rest[n * REST : (n + 1) * REST, :]
        ref["dq_send"][...] = packed_dq(rows_ref[...]).astype(BF)


def grads(name, keys, arrays, takes, gives, flops=6_000_000_000):
    arrays.update(keys)
    ins = [*keys, ("qg", 0), ("qg", 1), *takes]
    shapes = {
        "dq": shape(2, HD, LONG, dtype=F32),
        "dq_rest": shape(HD, 2 * REST, dtype=F32),
        "dkv_send": shape(OWN, 128),
        "dq_send": shape(OWN // 2, 128),
        "rows_out": shape(3, 2, 1024, dtype=F32),
    }
    scratch = dict(
        dkv=pltpu.VMEM((OWN, 128), F32),
        row=pltpu.VMEM((3, 2, 1024), F32),
        qg=pltpu.VMEM((2, LONG, 128), BF),
    )
    if "dq_send" in gives:
        scratch["dq"] = pltpu.VMEM((2, HD, LONG), F32)
        scratch["dq_rest"] = pltpu.VMEM((HD, 2 * REST), F32)
        scratch["dq_rows"] = pltpu.VMEM((OWN, 128), F32)
    results = call(
        functools.partial(grads_kernel, ins + list(gives) + list(scratch)),
        name,
        [shapes[g] if g in shapes else shape(OWN, 128, dtype=F32) for g in gives],
        [arrays[n] for n in ins],
        scratch=scratch.values(),
        flops=flops,
    )
    arrays.update(zip(gives, results))


def merge_kernel(at_ref, own_dq, far_dq, own_dkv, dkv1, dkv3, out_ref, dq_ref, dkv_ref):
    half = OWN // 2
    far = far_dq[...].astype(F32)
    turned = swap_halves(far)
    low = lane_of(far) < HD
    dq_ref[0:half, :] = own_dq[0:half, :] + jnp.where(low, far, turned)
    dq_ref[half:OWN, :] = own_dq[half:OWN, :] + jnp.where(low, turned, far)
    dkv = own_dkv[...] + sum(ref[...].astype(F32) for ref in (dkv1, dkv3))
    dkv_ref[...] = jnp.where(lane_of(dkv) < HD, dkv * SCALE, dkv)
    off = at_ref[1]
    swap_edges(dq_ref, off)
    swap_edges(dkv_ref, off)
    base = at_ref[0]

    def chunk(c, _):
        def sixteen(ref, n):
            spot = c * ROWS + 16 * n - base
            spot = spot + jnp.where(spot < 0, OWN, 0)
            return ref[pl.ds(pl.multiple_of(spot, 16), 16), :]

        for n in range(5):
            out_ref[c, 16 * n : 16 * n + 16, :] = sixteen(dkv_ref, n).astype(BF)
        groups = [sixteen(dq_ref, n) for n in range(5)]
        low = lane_of(groups[0]) < HD
        out_ref[c, 80:96, :] = jnp.where(low, groups[0], groups[1]).astype(BF)
        out_ref[c, 96:112, :] = jnp.where(low, groups[2], groups[3]).astype(BF)
        out_ref[c, 112:128, :] = groups[4].astype(BF)
        return 0

    lax.fori_loop(0, 16, chunk, 0)


def join_kernel(in_ref, q_out, k_out, v_out):
    for pair in range(HEADS // 2):
        cols = slice(pair * 128, pair * 128 + 128)
        a, b = in_ref[2 * pair].astype(F32), in_ref[2 * pair + 1].astype(F32)
        a_swap, b_swap = swap_halves(a), swap_halves(b)
        low = lane_of(a) < HD
        even, odd = jnp.where(low, a, b_swap).astype(BF), jnp.where(low, a_swap, b).astype(BF)
        k_out[:, cols] = even[0:ROWS]
        v_out[:, cols] = odd[0:ROWS]
        for n in range(5):
            part = slice(ROWS + 16 * (n // 2), ROWS + 16 * (n // 2) + 16)
            q_out[16 * n : 16 * n + 16, cols] = (odd if n % 2 else even)[part]


def shifted(array, by):
    pairs = [
        (c * 4 + x, c * 4 + (x + (by if c == 0 else -by)) % 4) for c in range(2) for x in range(4)
    ]
    return lax.ppermute(array, ("c", "x"), pairs)


def crossed(array):
    return lax.ppermute(array, "c", [(0, 1), (1, 0)])


def body(queries, keys, values, out_grad, doc_ids):
    packed = call(
        pack_kernel,
        "pack",
        [shape(16, 176, 128)],
        [queries, keys, values, out_grad, doc_ids],
        vmem=56 << 20,
    )[0]
    packed = lax.all_to_all(packed, BY_HEAD, 0, 0, tiled=True)
    at, qg, kv = call(
        order_kernel,
        "order",
        [shape(2, dtype=jnp.int32), shape(SENT, 128), shape(SENT, 128)],
        [packed],
        smem_out=1,
        scratch=[pltpu.VMEM((3 * OWN, 128), F32)],
    )
    qg_far = crossed(qg)
    kv1, kv3 = shifted(kv, 1), shifted(kv, -1)

    def side(sets):
        return [
            pltpu.VMEM((128, sets * WIDE), BF),
            pltpu.VMEM((sets, 384, 128), F32),
            pltpu.VMEM((2, LONG, 128), BF),
        ]

    stat, turned = shape(3, 2, 1024, dtype=F32), shape(128, WIDE)
    kept, kept_rest = shape(2, LONG, LONG), shape(REST, 2 * REST)
    kept_top = shape(3, LONG // STEP, 1, 1024, dtype=F32)
    grad_t = [shape(2, HD, LONG), shape(HD, 2 * REST)]
    first, *grad_t, kvt0, p0, rest0, top0 = call(
        own_totals_kernel,
        "totals_own",
        [stat, *grad_t, turned, kept, kept_rest, kept_top],
        [kv, qg, qg_far],
        scratch=side(1),
        flops=2_500_000_000,
    )
    kv1, kv3, first = lax.optimization_barrier((kv1, kv3, first))
    kv2 = shifted(kv1, 1)
    near, kvt1, kvt3, p1, p3, rest1, rest3, top1, top3 = call(
        near_totals_kernel,
        "totals_near",
        [stat] + [turned] * 2 + [kept] * 2 + [kept_rest] * 2 + [kept_top] * 2,
        [kv1, kv3, qg, qg_far, *grad_t],
        scratch=side(2),
        flops=5_000_000_000,
    )
    stats, kvt2, p2, rest2, top2 = call(
        last_totals_kernel,
        "totals_far",
        [stat, turned, kept, kept_rest, kept_top],
        [kv2, qg, qg_far, *grad_t, first, near],
        scratch=side(1) + [pltpu.VMEM((3, 2, 1024), F32)],
        flops=2_500_000_000,
    )

    sets = [
        dict(zip(("kv", "kvt", "p", "rest", "top"), one))
        for one in (
            (kv, kvt0, p0, rest0, top0),
            (kv1, kvt1, p1, rest1, top1),
            (kv2, kvt2, p2, rest2, top2),
            (kv3, kvt3, p3, rest3, top3),
        )
    ]
    arrays = {("qg", 0): qg, ("qg", 1): qg_far, "stats": stats, "stats_far": crossed(stats)}
    takes, gives = ["stats", "stats_far"], ["rows_out", "dq", "dq_rest", "dkv_send"]
    sent = {}
    for name, n, by in (("grads_far", 2, 1), ("grads_one", 1, -1), ("grads_three", 3, 1)):
        grads(name, sets[n], arrays, takes, gives)
        arrays["rows"] = arrays["rows_out"]
        arrays["dq_in"], arrays["dq_rest_in"] = arrays["dq"], arrays["dq_rest"]
        takes, gives = ["rows", "dq_in", "dq_rest_in"], ["dq", "dq_rest", "dkv_send"]
        sent[n] = shifted(arrays["dkv_send"], by)
        if n == 1:
            arrays["relay"] = sent[2]
            takes = [*takes, "relay"]
    sent[1], arrays["dq_in"] = lax.optimization_barrier((sent[1], arrays["dq_in"]))
    grads("grads_own", sets[0], arrays, takes, ["dq_out", "dq_send", "dkv_out"])
    merged = call(
        merge_kernel,
        "merge",
        [shape(16, 128, 128)],
        [at, arrays["dq_out"], crossed(arrays["dq_send"]), arrays["dkv_out"], sent[1], sent[3]],
        smem_in=1,
        scratch=[pltpu.VMEM((OWN, 128), F32), pltpu.VMEM((OWN, 128), F32)],
    )[0]
    merged = lax.all_to_all(merged, BY_HEAD, 0, 0, tiled=True)
    return tuple(call(join_kernel, "join", [shape(ROWS, HEADS * HD)] * 3, [merged]))


def solution(mesh):
    fine = Mesh(mesh.devices.reshape(4, 2, 2, 2, 4), BLK + ("zh", "x"))
    rows = P(BLK + ("zh", "x"), None)
    return jax.shard_map(
        body,
        mesh=fine,
        in_specs=(rows, rows, rows, rows, P(BLK)),
        out_specs=(rows, rows, rows),
        check_vma=False,
    )
```

time: 99.6 us -> 95.8 us (0.962)
  Pallas kernels: 43.5 us -> 40.6 us
  waiting for transfers between devices: 10.9 us -> 9 us
    ppermute x7 -> x6, waiting for transfers between devices: 9.7 us -> 6.77 us  [shifted(): return lax.ppermute(array, ('c', 'x'), pairs)]
    pallas_call x11, Pallas kernels: 43.5 us -> 40.6 us  [call(): pl.pallas_call(kernel, out_shape=outs, in_specs=[sm] * smem_in + [vm] * (...]
    ppermute x3, waiting for transfers between devices: 1.18 us -> 2.23 us  [crossed(): return lax.ppermute(array, 'c', [(0, 1), (1, 0)])]
    ppermute x7 -> x6, starting transfers between devices: 8.32 us -> 7.54 us  [shifted(): return lax.ppermute(array, ('c', 'x'), pairs)]
  transfers between devices with their start and end apart: 10 -> 9, of which waited for: 5 -> 7; matrix products, arithmetic and copies ran while one was open for 0% -> 0% of each run, Pallas kernels for 28% -> 27%
where the time goes in v5:
time: 95.8 us; the launch traced here: 95 us
  Pallas kernels  40.6 us (42%)
  blocking collectives  36 us (38%)
  waiting for transfers between devices  9 us (9%)
  starting transfers between devices  8.72 us (9%)
    pallas_call x11, Pallas kernels, call(): pl.pallas_call(kernel, out_shape=outs, in_specs=[sm] * smem_in + [vm] * (...  40.6 us
    all_to_all x1, blocking collectives, body(): packed = lax.all_to_all(packed, BY_HEAD, 0, 0, tiled=True)  21.9 us
    all_to_all x1, blocking collectives, body(): merged = lax.all_to_all(merged, BY_HEAD, 0, 0, tiled=True)  14 us
    ppermute x6, starting transfers between devices, shifted(): return lax.ppermute(array, ('c', 'x'), pairs)  7.54 us
    ppermute x6, waiting for transfers between devices, shifted(): return lax.ppermute(array, ('c', 'x'), pairs)  6.77 us
    ppermute x3, waiting for transfers between devices, crossed(): return lax.ppermute(array, 'c', [(0, 1), (1, 0)])  2.23 us
  transfers between devices with their start and end apart: 9, of which 7 were waited for; matrix products, arithmetic and copies ran while one was open for 0% of the time, Pallas kernels for 27%

profile of v5, /device:TPU:0, one launch (start us, length us, event | category | flops | bytes accessed | tf_op | source)
XLA Modules:
  0.0 95.0 jit_solution(5763128730869977702)
XLA Ops:
  0.6 2.3 %pack.1 = bf16[16,176,128]{2,1,0:T(8,128)(2,1)} custom-call(bf16[80,1024]{1,0:T(8,128)(2,1)} %q_ref.1, bf16[80,1024]{1,0:T(8,128)(2,1)} %k_ref.1, bf16[80,1024]{1,0:T(8,128)(2,1)} %v_ref.1, bf16[80,1024]{1,0:T(8,128)(2,1)} %g_ref.1, s32[640]{0:T(1024)} %doc_ref.1), custom_call_target="tpu_custom_call" | custom-call | flops 1048576 | bytes 1048576 | tf_op jit(solution)/shard_map/pack/pallas_call | solution.py:58
  2.9 21.9 %all_to_all.10.in_ref = bf16[16,176,128]{2,1,0:T(8,128)(2,1)S(1)} all-to-all(bf16[16,176,128]{2,1,0:T(8,128)(2,1)} %pack.1), channel_id=1, replica_groups=mesh['y'=4,'zl'=2,'c'=2,'zh'=2,'x'=4] {'y','zl','zh'}, dimensions={0} | all-to-all | bytes 1441792 | tf_op jit(solution)/shard_map/all_to_all | solution.py:469
  24.9 1.7 %order.1 = (s32[2]{0:T(128)S(1)}, bf16[1296,128]{1,0:T(8,128)(2,1)S(1)}, bf16[1296,128]{1,0:T(8,128)(2,1)S(1)}) custom-call(bf16[16,176,128]{2,1,0:T(8,128)(2,1)S(1)} %all_to_all.10.in_ref), custom_call_target="tpu_custom_call" | custom-call | flops 1048576 | bytes 1048576 | tf_op jit(solution)/shard_map/order/pallas_call | solution.py:58
  26.6 0.1 collective-permute-start
  26.6 2.8 %collective-permute-start.2 = (bf16[1296,128]{1,0:T(8,128)(2,1)S(1)}, bf16[1296,128]{1,0:T(8,128)(2,1)S(1)}, u32[]{:S(2)}, u32[]{:S(2)}) collective-permute-start(bf16[1296,128]{1,0:T(8,128)(2,1)S(1)} %get-tuple-element.46.kv.refs_0_), channel_id=1, source_target_pairs={{0,3},{1,0},{2,1},{3,2},{8,9},{9,10},{10,11},{11,8},{4,7},{5,4},{6... | collective-permute-start | bytes 995336 | tf_op jit(solution)/shard_map/ppermute | solution.py:454
  29.5 0.0 collective-permute-start.1
  29.5 0.0 collective-permute-done.qg1.refs_6_
  29.5 4.1 %totals_own.1 = (f32[3,2,1024]{2,1,0:T(2,128)S(1)}, bf16[2,64,960]{2,1,0:T(8,128)(2,1)S(1)}, bf16[64,640]{1,0:T(8,128)(2,1)S(1)}, bf16[128,1408]{1,0:T(8,128)(2,...) custom-call(bf16[1296,128]{1,0:T(8,128)(2,1)S(1)} %get-tuple-element.46.kv.ref, ...), custom_call_target="tpu_custom_call" | custom-call | flops 2500000000 | bytes 1048576 | tf_op jit(solution)/shard_map/totals_own/pallas_call | solution.py:58
  33.6 3.7 %collective-permute-done.2.kv3.refs_0_ = bf16[1296,128]{1,0:T(8,128)(2,1)S(1)} collective-permute-done((bf16[1296,128]{1,0:T(8,128)(2,1)S(1)}, bf16[1296,128]{1,0:T(8,128)(2,1)S(1)}, u32[]{:S(2)}, u32[]{:S(2)}) %collective-permute-start.2) | collective-permute-done | bytes 331808 | tf_op jit(solution)/shard_map/ppermute | solution.py:454
  37.3 0.7 collective-permute-done.1.kv1.refs_0_
  38.1 0.3 collective-permute-start.3
  38.3 6.6 %totals_near.1 = (f32[3,2,1024]{2,1,0:T(2,128)S(1)}, bf16[128,1408]{1,0:T(8,128)(2,1)S(1)}, bf16[128,1408]{1,0:T(8,128)(2,1)S(1)}, bf16[2,960,960]{2,1,0:T(8,128...) custom-call(bf16[1296,128]{1,0:T(8,128)(2,1)S(1)} %collective-permut, ...), custom_call_target="tpu_custom_call" | custom-call | flops 5000000000 | bytes 1048576 | tf_op jit(solution)/shard_map/totals_near/pallas_call | solution.py:58
  45.0 1.4 %collective-permute-done.3.kv.refs_0_ = bf16[1296,128]{1,0:T(8,128)(2,1)S(1)} collective-permute-done((bf16[1296,128]{1,0:T(8,128)(2,1)S(1)}, bf16[1296,128]{1,0:T(8,128)(2,1)S(1)}, u32[]{:S(2)}, u32[]{:S(2)}) %collective-permute-start.3) | collective-permute-done | bytes 331808 | tf_op jit(solution)/shard_map/ppermute | solution.py:454
  46.4 3.9 %totals_far.1 = (f32[3,2,1024]{2,1,0:T(2,128)S(1)}, bf16[128,1408]{1,0:T(8,128)(2,1)S(1)}, bf16[2,960,960]{2,1,0:T(8,128)(2,1)S(1)}, bf16[320,640]{1,0:T(8,128)(2,1)S(1)}, f32[3,4,1,1024]{3,2,1,0:T(1,128)S(1)}) custom-call(bf16[1296,128]{1,0:T(8,128)(2,1)S(1)} %collective-permute-done.3.kv.refs_0_, bf16[1296,128]{1,0:T(8,128)(2,1)S(1)} %get-tuple-element.47.qg0.refs_5_, ...), custom_call_target="tpu_custom_call" | custom-call | flops 2500000000 | bytes 1048576 | tf_op jit(solution)/shard_map/totals_far/pallas_call | solution.py:58
  50.3 1.0 %collective-permute-start.4 = (f32[3,2,1024]{2,1,0:T(2,128)S(1)}, f32[3,2,1024]{2,1,0:T(2,128)S(1)}, u32[]{:S(2)}, u32[]{:S(2)}) collective-permute-start(f32[3,2,1024]{2,1,0:T(2,128)S(1)} %get-tuple-element.63.refs_7_), channel_id=1, source_target_pairs={{0,8},{8,0},{1,9},{9,1},{2,10},{10,2},{3,11},{11,3},{4,12},{12,4},... | collective-permute-start | bytes 73736 | tf_op jit(solution)/shard_map/ppermute | solution.py:458
  51.3 0.8 collective-permute-done.4.refs_8_
  52.2 5.0 %grads_far.1 = (f32[3,2,1024]{2,1,0:T(2,128)S(1)}, f32[2,64,960]{2,1,0:T(8,128)S(1)}, f32[64,640]{1,0:T(8,128)S(1)}, bf16[1280,128]{1,0:T(8,128)(2,1)S(1)}) custom-call(bf16[1296,128]{1,0:T(8,128)(2,1)S(1)} %collective-permute-done.3.kv.refs_0_, bf16[128,1408]{1,0:T(8,128)(2,1)S(1)} %get-tuple-element.59.refs_1_, ...), custom_call_target="tpu_custom_call" | custom-call | flops 6000000000 | bytes 1048576 | tf_op jit(solution)/shard_map/grads_far/pallas_call | solution.py:58
  57.2 0.1 collective-permute-start.6
  57.2 4.9 %grads_one.1 = (f32[2,64,960]{2,1,0:T(8,128)S(1)}, f32[64,640]{1,0:T(8,128)S(1)}, bf16[1280,128]{1,0:T(8,128)(2,1)S(1)}) custom-call(bf16[1296,128]{1,0:T(8,128)(2,1)S(1)} %collective-permute-done.1.kv1.refs_0_, bf16[128,1408]{1,0:T(8,128)(2,1)S(1)} %get-tuple-element.65.refs_1_, bf16[2,960,960]{2,1,0:T(8,128)(2,1)S(1)} %get-tuple-element.66.refs_2_, ...), custom_call_target="tpu_custom_call" | custom-call | flops 6000000000 | bytes 1048576 | tf_op jit(solution)/shard_map/grads_one/pallas_call | solution.py:58
  62.1 3.3 %collective-permute-start.5 = (bf16[1280,128]{1,0:T(8,128)(2,1)S(1)}, bf16[1280,128]{1,0:T(8,128)(2,1)S(1)}, u32[]{:S(2)}, u32[]{:S(2)}) collective-permute-start(bf16[1280,128]{1,0:T(8,128)(2,1)S(1)} %get-tuple-element.71), channel_id=1, source_target_pairs={{0,3},{1,0},{2,1},{3,2},{8,9},{9,10},{10,11},{11,8},{4,7},{5,4},{6... | collective-permute-start | bytes 983048 | tf_op jit(solution)/shard_map/ppermute | solution.py:454
  65.4 0.1 collective-permute-done.6.refs_10_
  65.5 5.0 %grads_three.1 = (f32[2,64,960]{2,1,0:T(8,128)S(1)}, f32[64,640]{1,0:T(8,128)S(1)}, bf16[1280,128]{1,0:T(8,128)(2,1)S(1)}) custom-call(bf16[1296,128]{1,0:T(8,128)(2,1)S(1)} %collective-permute-done.2.kv3.refs_0_, bf16[128,1408]{1,0:T(8,128)(2,1)S(1)} %get-tuple-element.72.refs_1_, bf16[2,960,960]{2,1,0:T(8,128)(2,1)S(1)} %get-tuple-element.73.refs_2_, ...), custom_call_target="tpu_custom_call" | custom-call | flops 6000000000 | bytes 1048576 | tf_op jit(solution)/shard_map/grads_three/pallas_call | solution.py:58
  70.5 0.0 collective-permute-done.5.dkv1
  70.5 1.1 %collective-permute-start.8 = (bf16[1280,128]{1,0:T(8,128)(2,1)S(1)}, bf16[1280,128]{1,0:T(8,128)(2,1)S(1)}, u32[]{:S(2)}, u32[]{:S(2)}) collective-permute-start(bf16[1280,128]{1,0:T(8,128)(2,1)S(1)} %get-tuple-element.86), channel_id=1, source_target_pairs={{0,1},{1,2},{2,3},{3,0},{8,11},{9,8},{10,9},{11,10},{4,5},{5,6},{6... | collective-permute-start | bytes 983048 | tf_op jit(solution)/shard_map/ppermute | solution.py:454
  71.5 5.0 %grads_own.1 = (f32[1280,128]{1,0:T(8,128)S(1)}, bf16[640,128]{1,0:T(8,128)(2,1)S(1)}, f32[1280,128]{1,0:T(8,128)S(1)}) custom-call(bf16[1296,128]{1,0:T(8,128)(2,1)S(1)} %get-tuple-element.46.kv.refs_0_, bf16[128,1408]{1,0:T(8,128)(2,1)S(1)} %get-tuple-element.48.refs_1_, bf16[2,960,960]{2,1,0:T(8,128)(2,1)S(1)} %get-tuple-element.49.refs_2_, ...), custom_call_target="tpu_custom_call" | custom-call | flops 6000000000 | bytes 1048576 | tf_op jit(solution)/shard_map/grads_own/pallas_call | solution.py:58
  76.6 0.1 collective-permute-start.7
  76.7 1.4 %collective-permute-done.7.far_dq = bf16[640,128]{1,0:T(8,128)(2,1)S(1)} collective-permute-done((bf16[640,128]{1,0:T(8,128)(2,1)S(1)}, bf16[640,128]{1,0:T(8,128)(2,1)S(1)}, u32[]{:S(2)}, u32[]{:S(2)}) %collective-permute-start.7) | collective-permute-done | bytes 163872 | tf_op jit(solution)/shard_map/ppermute | solution.py:458
  78.1 0.8 collective-permute-done.8.dkv3
  78.8 1.1 %merge.1 = bf16[16,128,128]{2,1,0:T(8,128)(2,1)S(1)} custom-call(s32[2]{0:T(128)S(1)} %get-tuple-element.45.at_ref, f32[1280,128]{1,0:T(8,128)S(1)} %get-tuple-element.82.own_dq, bf16[640,128]{1,0:T(8,128)(2,1)S(1)} %collective-permute-done.7.far_dq, f32[1280,128]{1,0:T(8,128)S(1)} %get-tuple-element.84.own_dkv, ...), custom_call_target="tpu_custom_call" | custom-call | flops 1048576 | bytes 1048576 | tf_op jit(solution)/shard_map/merge/pallas_call | solution.py:58
  80.0 14.0 %all_to_all.11.in_ref = bf16[16,128,128]{2,1,0:T(8,128)(2,1)S(1)} all-to-all(bf16[16,128,128]{2,1,0:T(8,128)(2,1)S(1)} %merge.1), channel_id=1, replica_groups=mesh['y'=4,'zl'=2,'c'=2,'zh'=2,'x'=4] {'y','zl','zh'}, dimensions={0} | all-to-all | bytes 1048576 | tf_op jit(solution)/shard_map/all_to_all | solution.py:550
  94.0 1.0 %join.1 = (bf16[80,1024]{1,0:T(8,128)(2,1)}, bf16[80,1024]{1,0:T(8,128)(2,1)}, bf16[80,1024]{1,0:T(8,128)(2,1)}) custom-call(bf16[16,128,128]{2,1,0:T(8,128)(2,1)S(1)} %all_to_all.11.in_ref), custom_call_target="tpu_custom_call" | custom-call | flops 1048576 | bytes 1048576 | tf_op jit(solution)/shard_map/join/pallas_call | solution.py:58
Async XLA Ops:
  26.6 2.9 %collective-permute-start = (bf16[1296,128]{1,0:T(8,128)(2,1)S(1)}, bf16[1296,128]{1,0:T(8,128)(2,1)S(1)}, u32[]{:S(2)}, u32[]{:S(2)}) collective-permute-start(bf16[1296,128]{1,0:T(8,128)(2,1)S(1)} %get-tuple-element.47.qg0.refs_5_), channel_id=1, source_target_pairs={{0,8},{8,0},{1,9},{9,1},{2,10},{10,2},{3,11},{11,3},{4,12},{12,4},... | collective-permute-start | bytes 995336 | tf_op jit(solution)/shard_map/ppermute | solution.py:458
  26.6 10.7 %collective-permute-start.2 = (bf16[1296,128]{1,0:T(8,128)(2,1)S(1)}, bf16[1296,128]{1,0:T(8,128)(2,1)S(1)}, u32[]{:S(2)}, u32[]{:S(2)}) collective-permute-start(bf16[1296,128]{1,0:T(8,128)(2,1)S(1)} %get-tuple-element.46.kv.refs_0_), channel_id=1, source_target_pairs={{0,3},{1,0},{2,1},{3,2},{8,9},{9,10},{10,11},{11,8},{4,7},{5,4},{6... | collective-permute-start | bytes 995336 | tf_op jit(solution)/shard_map/ppermute | solution.py:454
  29.5 8.6 %collective-permute-start.1 = (bf16[1296,128]{1,0:T(8,128)(2,1)S(1)}, bf16[1296,128]{1,0:T(8,128)(2,1)S(1)}, u32[]{:S(2)}, u32[]{:S(2)}) collective-permute-start(bf16[1296,128]{1,0:T(8,128)(2,1)S(1)} %get-tuple-element.46.kv.refs_0_), channel_id=1, source_target_pairs={{0,1},{1,2},{2,3},{3,0},{8,11},{9,8},{10,9},{11,10},{4,5},{5,6},{6... | collective-permute-start | bytes 995336 | tf_op jit(solution)/shard_map/ppermute | solution.py:454
  38.1 8.3 %collective-permute-start.3 = (bf16[1296,128]{1,0:T(8,128)(2,1)S(1)}, bf16[1296,128]{1,0:T(8,128)(2,1)S(1)}, u32[]{:S(2)}, u32[]{:S(2)}) collective-permute-start(bf16[1296,128]{1,0:T(8,128)(2,1)S(1)} %collective-permute-done.1.kv1.refs_0_), channel_id=1, source_target_pairs={{0,1},{1,2},{2,3},{3,0},{8,11},{9,8},{10,9},{11,10},{4,5},{5,6},{6... | collective-permute-start | bytes 995336 | tf_op jit(solution)/shard_map/ppermute | solution.py:454
  50.3 1.9 %collective-permute-start.4 = (f32[3,2,1024]{2,1,0:T(2,128)S(1)}, f32[3,2,1024]{2,1,0:T(2,128)S(1)}, u32[]{:S(2)}, u32[]{:S(2)}) collective-permute-start(f32[3,2,1024]{2,1,0:T(2,128)S(1)} %get-tuple-element.63.refs_7_), channel_id=1, source_target_pairs={{0,8},{8,0},{1,9},{9,1},{2,10},{10,2},{3,11},{11,3},{4,12},{12,4},... | collective-permute-start | bytes 73736 | tf_op jit(solution)/shard_map/ppermute | solution.py:458
  57.2 8.4 %collective-permute-start.6 = (bf16[1280,128]{1,0:T(8,128)(2,1)S(1)}, bf16[1280,128]{1,0:T(8,128)(2,1)S(1)}, u32[]{:S(2)}, u32[]{:S(2)}) collective-permute-start(bf16[1280,128]{1,0:T(8,128)(2,1)S(1)} %get-tuple-element.78), channel_id=1, source_target_pairs={{0,1},{1,2},{2,3},{3,0},{8,11},{9,8},{10,9},{11,10},{4,5},{5,6},{6... | collective-permute-start | bytes 983048 | tf_op jit(solution)/shard_map/ppermute | solution.py:454
  62.1 8.3 %collective-permute-start.5 = (bf16[1280,128]{1,0:T(8,128)(2,1)S(1)}, bf16[1280,128]{1,0:T(8,128)(2,1)S(1)}, u32[]{:S(2)}, u32[]{:S(2)}) collective-permute-start(bf16[1280,128]{1,0:T(8,128)(2,1)S(1)} %get-tuple-element.71), channel_id=1, source_target_pairs={{0,3},{1,0},{2,1},{3,2},{8,9},{9,10},{10,11},{11,8},{4,7},{5,4},{6... | collective-permute-start | bytes 983048 | tf_op jit(solution)/shard_map/ppermute | solution.py:454
  70.5 8.4 %collective-permute-start.8 = (bf16[1280,128]{1,0:T(8,128)(2,1)S(1)}, bf16[1280,128]{1,0:T(8,128)(2,1)S(1)}, u32[]{:S(2)}, u32[]{:S(2)}) collective-permute-start(bf16[1280,128]{1,0:T(8,128)(2,1)S(1)} %get-tuple-element.86), channel_id=1, source_target_pairs={{0,1},{1,2},{2,3},{3,0},{8,11},{9,8},{10,9},{11,10},{4,5},{5,6},{6... | collective-permute-start | bytes 983048 | tf_op jit(solution)/shard_map/ppermute | solution.py:454
  76.6 1.5 %collective-permute-start.7 = (bf16[640,128]{1,0:T(8,128)(2,1)S(1)}, bf16[640,128]{1,0:T(8,128)(2,1)S(1)}, u32[]{:S(2)}, u32[]{:S(2)}) collective-permute-start(bf16[640,128]{1,0:T(8,128)(2,1)S(1)} %get-tuple-element.83), channel_id=1, source_target_pairs={{0,8},{8,0},{1,9},{9,1},{2,10},{10,2},{3,11},{11,3},{4,12},{12,4},... | collective-permute-start | bytes 491528 | tf_op jit(solution)/shard_map/ppermute | solution.py:458

commit v6 on v5

--- a/solution.py
+++ b/solution.py
@@ -235,7 +235,8 @@
         stat_ref[n, 1:2, 0:LONG] = dot
         return 0
 
-    lax.fori_loop(0, 2, block, 0)
+    for n in range(2):
+        block(n, 0)
 
     def keep_rest(half, at, p, top):
         rest_refs[half][...] = p
@@ -309,7 +310,7 @@
     return jnp.where(low, dq[0 : OWN // 2, :], dq[OWN // 2 : OWN, :])
 
 
-def grads_kernel(names, *refs):
+def grads_kernel(blocks, with_rest, names, *refs):
     ref = dict(zip(names, refs))
     dq_ref, dq_rest_ref, dkv_ref, row_ref = ref["dq"], ref["dq_rest"], ref["dkv"], ref["row"]
     kv_ref, kvt_ref, qg_ref = ref["kv"], ref["kvt"], ref["qg"]
@@ -331,7 +332,7 @@
         qg_ref[n] = ref["qg", n][0:LONG, :]
     for out, known in ((dq_ref, "dq_in"), (dq_rest_ref, "dq_rest_in")):
         out[...] = ref[known][...] if known in ref else jnp.zeros_like(out)
-    dkv_ref[...] = jnp.zeros_like(dkv_ref)
+    dkv_ref[...] = ref["dkv_in"][...] if "dkv_in" in ref else jnp.zeros_like(dkv_ref)
 
     def block(n, _):
         lse = row_ref[n, 0:1, 0:LONG]
@@ -345,33 +346,35 @@
         dq_ref[n] += tile_grads(qg_ref[n], starts, weights_of, dot, kv_ref, kvt_ref, dkv_ref)
         return 0
 
-    lax.fori_loop(0, 2, block, 0)
-    both = slice(0, 2 * REST)
-    share = jnp.exp2(top_ref[2, 0, :, both] - row_ref[2, 0:1, both])
-    dq_rest_ref[...] += tile_grads(
-        rest_rows(ref["qg", 0], ref["qg", 1]),
-        [(LONG, REST)],
-        lambda at: rest_ref[...].astype(F32) * share,
-        row_ref[2, 1:2, both],
-        kv_ref,
-        kvt_ref,
-        dkv_ref,
-    )
+    for n in blocks:
+        block(n, 0)
+    if with_rest:
+        both = slice(0, 2 * REST)
+        share = jnp.exp2(top_ref[2, 0, :, both] - row_ref[2, 0:1, both])
+        dq_rest_ref[...] += tile_grads(
+            rest_rows(ref["qg", 0], ref["qg", 1]),
+            [(LONG, REST)],
+            lambda at: rest_ref[...].astype(F32) * share,
+            row_ref[2, 1:2, both],
+            kv_ref,
+            kvt_ref,
+            dkv_ref,
+        )
     if "dkv_out" in ref:
         ref["dkv_out"][...] = dkv_ref[...]
     if "dkv_send" in ref:
         relay = ref["relay"][...].astype(F32) if "relay" in ref else 0.0
         ref["dkv_send"][...] = (dkv_ref[...] + relay).astype(BF)
+    for n, (whole, name) in enumerate((("dq_out", "dq_out"), ("dq_send", "dq_rows"))):
+        if whole in ref:
+            rest = dq_rest_ref[:, n * REST : (n + 1) * REST] * SCALE
+            ref[name][0:LONG, :] = jnp.concatenate([dq_ref[n] * SCALE] * 2, axis=0).T
+            ref[name][LONG:OWN, :] = jnp.concatenate([rest] * 2, axis=0).T
     if "dq_send" in ref:
-        rows_ref = ref["dq_rows"]
-        rest = jnp.concatenate([dq_rest_ref[...] * SCALE] * 2, axis=0).T
-        for n, out in enumerate((ref["dq_out"], rows_ref)):
-            out[0:LONG, :] = jnp.concatenate([dq_ref[n] * SCALE] * 2, axis=0).T
-            out[LONG:OWN, :] = rest[n * REST : (n + 1) * REST, :]
-        ref["dq_send"][...] = packed_dq(rows_ref[...]).astype(BF)
-
-
-def grads(name, keys, arrays, takes, gives, flops=6_000_000_000):
+        ref["dq_send"][...] = packed_dq(ref["dq_rows"][...]).astype(BF)
+
+
+def grads(name, keys, arrays, takes, gives, blocks=(0, 1), with_rest=True):
     arrays.update(keys)
     ins = [*keys, ("qg", 0), ("qg", 1), *takes]
     shapes = {
@@ -386,17 +389,19 @@
         row=pltpu.VMEM((3, 2, 1024), F32),
         qg=pltpu.VMEM((2, LONG, 128), BF),
     )
+    if "dq" not in gives:
+        scratch["dq"] = pltpu.VMEM((2, HD, LONG), F32)
+    if "dq_rest" not in gives:
+        scratch["dq_rest"] = pltpu.VMEM((HD, 2 * REST), F32)
     if "dq_send" in gives:
-        scratch["dq"] = pltpu.VMEM((2, HD, LONG), F32)
-        scratch["dq_rest"] = pltpu.VMEM((HD, 2 * REST), F32)
         scratch["dq_rows"] = pltpu.VMEM((OWN, 128), F32)
     results = call(
-        functools.partial(grads_kernel, ins + list(gives) + list(scratch)),
+        functools.partial(grads_kernel, blocks, with_rest, ins + list(gives) + list(scratch)),
         name,
         [shapes[g] if g in shapes else shape(OWN, 128, dtype=F32) for g in gives],
         [arrays[n] for n in ins],
         scratch=scratch.values(),
-        flops=flops,
+        flops=3_000_000_000 * len(blocks),
     )
     arrays.update(zip(gives, results))
 
@@ -537,13 +542,20 @@
         if n == 1:
             arrays["relay"] = sent[2]
             takes = [*takes, "relay"]
+    takes = ["rows", "dq_in", "dq_rest_in"]
+    gives = ["dq_send", "dq_rest", "dkv_out"]
+    grads("grads_own_far", sets[0], arrays, takes, gives, blocks=(1,))
+    far_dq = crossed(arrays["dq_send"])
+    arrays["dkv_in"], arrays["dq_rest_in"] = arrays["dkv_out"], arrays["dq_rest"]
     sent[1], arrays["dq_in"] = lax.optimization_barrier((sent[1], arrays["dq_in"]))
-    grads("grads_own", sets[0], arrays, takes, ["dq_out", "dq_send", "dkv_out"])
+    grads(
+        "grads_own", sets[0], arrays, [*takes, "dkv_in"], ["dq_out", "dkv_out"], (0,), False
+    )
     merged = call(
         merge_kernel,
         "merge",
         [shape(16, 128, 128)],
-        [at, arrays["dq_out"], crossed(arrays["dq_send"]), arrays["dkv_out"], sent[1], sent[3]],
+        [at, arrays["dq_out"], far_dq, arrays["dkv_out"], sent[1], sent[3]],
         smem_in=1,
         scratch=[pltpu.VMEM((OWN, 128), F32), pltpu.VMEM((OWN, 128), F32)],
     )[0]

time: 95.8 us -> 92.8 us (0.969)
  Pallas kernels: 40.6 us -> 37.9 us
  waiting for transfers between devices: 9 us -> 10.5 us
    pallas_call x11 -> x12, Pallas kernels: 40.6 us -> 37.9 us  [call(): pl.pallas_call(kernel, out_shape=outs, in_specs=[sm] * smem_in + [vm] * (...]
    ppermute x6, waiting for transfers between devices: 6.77 us -> 9.46 us  [shifted(): return lax.ppermute(array, ('c', 'x'), pairs)]
    ppermute x3, waiting for transfers between devices: 2.23 us -> 1.05 us  [crossed(): return lax.ppermute(array, 'c', [(0, 1), (1, 0)])]
  transfers between devices with their start and end apart: 9 -> 9, of which waited for: 7 -> 6; matrix products, arithmetic and copies ran while one was open for 0% -> 0% of each run, Pallas kernels for 27% -> 26%
where the time goes in v6:
time: 92.8 us; the launch traced here: 92.5 us
  Pallas kernels  37.9 us (41%)
  blocking collectives  35.1 us (38%)
  waiting for transfers between devices  10.5 us (11%)
  starting transfers between devices  8.38 us (9%)
    pallas_call x12, Pallas kernels, call(): pl.pallas_call(kernel, out_shape=outs, in_specs=[sm] * smem_in + [vm] * (...  37.9 us
    all_to_all x1, blocking collectives, body(): packed = lax.all_to_all(packed, BY_HEAD, 0, 0, tiled=True)  21.9 us
    all_to_all x1, blocking collectives, body(): merged = lax.all_to_all(merged, BY_HEAD, 0, 0, tiled=True)  13.1 us
    ppermute x6, waiting for transfers between devices, shifted(): return lax.ppermute(array, ('c', 'x'), pairs)  9.46 us
    ppermute x6, starting transfers between devices, shifted(): return lax.ppermute(array, ('c', 'x'), pairs)  6.81 us
  transfers between devices with their start and end apart: 9, of which 6 were waited for; matrix products, arithmetic and copies ran while one was open for 0% of the time, Pallas kernels for 26%

profile of v6, /device:TPU:0, one launch (start us, length us, event | category | flops | bytes accessed | tf_op | source)
XLA Modules:
  0.0 92.5 jit_solution(10987862974751003276)
XLA Ops:
  0.6 2.3 %pack.1 = bf16[16,176,128]{2,1,0:T(8,128)(2,1)} custom-call(bf16[80,1024]{1,0:T(8,128)(2,1)} %q_ref.1, bf16[80,1024]{1,0:T(8,128)(2,1)} %k_ref.1, bf16[80,1024]{1,0:T(8,128)(2,1)} %v_ref.1, bf16[80,1024]{1,0:T(8,128)(2,1)} %g_ref.1, s32[640]{0:T(1024)} %doc_ref.1), custom_call_target="tpu_custom_call" | custom-call | flops 1048576 | bytes 1048576 | tf_op jit(solution)/shard_map/pack/pallas_call | solution.py:58
  2.9 21.9 %all_to_all.10.in_ref = bf16[16,176,128]{2,1,0:T(8,128)(2,1)S(1)} all-to-all(bf16[16,176,128]{2,1,0:T(8,128)(2,1)} %pack.1), channel_id=1, replica_groups=mesh['y'=4,'zl'=2,'c'=2,'zh'=2,'x'=4] {'y','zl','zh'}, dimensions={0} | all-to-all | bytes 1441792 | tf_op jit(solution)/shard_map/all_to_all | solution.py:474
  24.9 1.7 %order.1 = (s32[2]{0:T(128)S(1)}, bf16[1296,128]{1,0:T(8,128)(2,1)S(1)}, bf16[1296,128]{1,0:T(8,128)(2,1)S(1)}) custom-call(bf16[16,176,128]{2,1,0:T(8,128)(2,1)S(1)} %all_to_all.10.in_ref), custom_call_target="tpu_custom_call" | custom-call | flops 1048576 | bytes 1048576 | tf_op jit(solution)/shard_map/order/pallas_call | solution.py:58
  26.6 0.1 collective-permute-start
  26.7 2.8 %collective-permute-start.2 = (bf16[1296,128]{1,0:T(8,128)(2,1)S(1)}, bf16[1296,128]{1,0:T(8,128)(2,1)S(1)}, u32[]{:S(2)}, u32[]{:S(2)}) collective-permute-start(bf16[1296,128]{1,0:T(8,128)(2,1)S(1)} %get-tuple-element.48.kv.refs_0_), channel_id=1, source_target_pairs={{0,3},{1,0},{2,1},{3,2},{8,9},{9,10},{10,11},{11,8},{4,7},{5,4},{6... | collective-permute-start | bytes 995336 | tf_op jit(solution)/shard_map/ppermute | solution.py:459
  29.5 0.0 collective-permute-start.1
  29.5 0.0 collective-permute-done.qg1.refs_6_
  29.5 3.4 %totals_own.1 = (f32[3,2,1024]{2,1,0:T(2,128)S(1)}, bf16[2,64,960]{2,1,0:T(8,128)(2,1)S(1)}, bf16[64,640]{1,0:T(8,128)(2,1)S(1)}, bf16[128,1408]{1,0:T(8,128)(2,...) custom-call(bf16[1296,128]{1,0:T(8,128)(2,1)S(1)} %get-tuple-element.48.kv.ref, ...), custom_call_target="tpu_custom_call" | custom-call | flops 2500000000 | bytes 1048576 | tf_op jit(solution)/shard_map/totals_own/pallas_call | solution.py:58
  32.9 4.4 %collective-permute-done.2.kv3.refs_0_ = bf16[1296,128]{1,0:T(8,128)(2,1)S(1)} collective-permute-done((bf16[1296,128]{1,0:T(8,128)(2,1)S(1)}, bf16[1296,128]{1,0:T(8,128)(2,1)S(1)}, u32[]{:S(2)}, u32[]{:S(2)}) %collective-permute-start.2) | collective-permute-done | bytes 331808 | tf_op jit(solution)/shard_map/ppermute | solution.py:459
  37.3 0.7 collective-permute-done.1.kv1.refs_0_
  38.1 0.3 collective-permute-start.3
  38.3 6.0 %totals_near.1 = (f32[3,2,1024]{2,1,0:T(2,128)S(1)}, bf16[128,1408]{1,0:T(8,128)(2,1)S(1)}, bf16[128,1408]{1,0:T(8,128)(2,1)S(1)}, bf16[2,960,960]{2,1,0:T(8,128...) custom-call(bf16[1296,128]{1,0:T(8,128)(2,1)S(1)} %collective-permut, ...), custom_call_target="tpu_custom_call" | custom-call | flops 5000000000 | bytes 1048576 | tf_op jit(solution)/shard_map/totals_near/pallas_call | solution.py:58
  44.4 2.0 %collective-permute-done.3.kv.refs_0_ = bf16[1296,128]{1,0:T(8,128)(2,1)S(1)} collective-permute-done((bf16[1296,128]{1,0:T(8,128)(2,1)S(1)}, bf16[1296,128]{1,0:T(8,128)(2,1)S(1)}, u32[]{:S(2)}, u32[]{:S(2)}) %collective-permute-start.3) | collective-permute-done | bytes 331808 | tf_op jit(solution)/shard_map/ppermute | solution.py:459
  46.4 3.4 %totals_far.1 = (f32[3,2,1024]{2,1,0:T(2,128)S(1)}, bf16[128,1408]{1,0:T(8,128)(2,1)S(1)}, bf16[2,960,960]{2,1,0:T(8,128)(2,1)S(1)}, bf16[320,640]{1,0:T(8,128)(2,1)S(1)}, f32[3,4,1,1024]{3,2,1,0:T(1,128)S(1)}) custom-call(bf16[1296,128]{1,0:T(8,128)(2,1)S(1)} %collective-permute-done.3.kv.refs_0_, bf16[1296,128]{1,0:T(8,128)(2,1)S(1)} %get-tuple-element.49.qg0.refs_5_, ...), custom_call_target="tpu_custom_call" | custom-call | flops 2500000000 | bytes 1048576 | tf_op jit(solution)/shard_map/totals_far/pallas_call | solution.py:58
  49.8 0.4 collective-permute-start.4
  50.2 1.0 %collective-permute-done.4.refs_8_ = f32[3,2,1024]{2,1,0:T(2,128)S(1)} collective-permute-done((f32[3,2,1024]{2,1,0:T(2,128)S(1)}, f32[3,2,1024]{2,1,0:T(2,128)S(1)}, u32[]{:S(2)}, u32[]{:S(2)}) %collective-permute-start.4) | collective-permute-done | bytes 24608 | tf_op jit(solution)/shard_map/ppermute | solution.py:463
  51.3 4.6 %grads_far.1 = (f32[3,2,1024]{2,1,0:T(2,128)S(1)}, f32[2,64,960]{2,1,0:T(8,128)S(1)}, f32[64,640]{1,0:T(8,128)S(1)}, bf16[1280,128]{1,0:T(8,128)(2,1)S(1)}) custom-call(bf16[1296,128]{1,0:T(8,128)(2,1)S(1)} %collective-permute-done.3.kv.refs_0_, bf16[128,1408]{1,0:T(8,128)(2,1)S(1)} %get-tuple-element.61.refs_1_, ...), custom_call_target="tpu_custom_call" | custom-call | flops 6000000000 | bytes 1048576 | tf_op jit(solution)/shard_map/grads_far/pallas_call | solution.py:58
  55.8 0.1 collective-permute-start.6
  55.9 4.6 %grads_one.1 = (f32[2,64,960]{2,1,0:T(8,128)S(1)}, f32[64,640]{1,0:T(8,128)S(1)}, bf16[1280,128]{1,0:T(8,128)(2,1)S(1)}) custom-call(bf16[1296,128]{1,0:T(8,128)(2,1)S(1)} %collective-permute-done.1.kv1.refs_0_, bf16[128,1408]{1,0:T(8,128)(2,1)S(1)} %get-tuple-element.67.refs_1_, bf16[2,960,960]{2,1,0:T(8,128)(2,1)S(1)} %get-tuple-element.68.refs_2_, ...), custom_call_target="tpu_custom_call" | custom-call | flops 6000000000 | bytes 1048576 | tf_op jit(solution)/shard_map/grads_one/pallas_call | solution.py:58
  60.5 3.6 %collective-permute-start.5 = (bf16[1280,128]{1,0:T(8,128)(2,1)S(1)}, bf16[1280,128]{1,0:T(8,128)(2,1)S(1)}, u32[]{:S(2)}, u32[]{:S(2)}) collective-permute-start(bf16[1280,128]{1,0:T(8,128)(2,1)S(1)} %get-tuple-element.73), channel_id=1, source_target_pairs={{0,3},{1,0},{2,1},{3,2},{8,9},{9,10},{10,11},{11,8},{4,7},{5,4},{6... | collective-permute-start | bytes 983048 | tf_op jit(solution)/shard_map/ppermute | solution.py:459
  64.1 0.1 collective-permute-done.6.refs_10_
  64.2 4.7 %grads_three.1 = (f32[2,64,960]{2,1,0:T(8,128)S(1)}, f32[64,640]{1,0:T(8,128)S(1)}, bf16[1280,128]{1,0:T(8,128)(2,1)S(1)}) custom-call(bf16[1296,128]{1,0:T(8,128)(2,1)S(1)} %collective-permute-done.2.kv3.refs_0_, bf16[128,1408]{1,0:T(8,128)(2,1)S(1)} %get-tuple-element.74.refs_1_, bf16[2,960,960]{2,1,0:T(8,128)(2,1)S(1)} %get-tuple-element.75.refs_2_, ...), custom_call_target="tpu_custom_call" | custom-call | flops 6000000000 | bytes 1048576 | tf_op jit(solution)/shard_map/grads_three/pallas_call | solution.py:58
  68.9 0.1 collective-permute-start.8
  69.0 2.8 %grads_own_far.1 = (bf16[640,128]{1,0:T(8,128)(2,1)S(1)}, f32[64,640]{1,0:T(8,128)S(1)}, f32[1280,128]{1,0:T(8,128)S(1)}) custom-call(bf16[1296,128]{1,0:T(8,128)(2,1)S(1)} %get-tuple-element.48.kv.refs_0_, bf16[128,1408]{1,0:T(8,128)(2,1)S(1)} %get-tuple-element.50.refs_1_, bf16[2,960,960]{2,1,0:T(8,128)(2,1)S(1)} %get-tuple-element.51.refs_2_, ...), custom_call_target="tpu_custom_call" | custom-call | flops 3000000000 | bytes 1048576 | tf_op jit(solution)/shard_map/grads_own_far/pallas_call | solution.py:58
  71.7 0.0 collective-permute-done.5.dkv1
  71.8 1.0 %collective-permute-start.7 = (bf16[640,128]{1,0:T(8,128)(2,1)S(1)}, bf16[640,128]{1,0:T(8,128)(2,1)S(1)}, u32[]{:S(2)}, u32[]{:S(2)}) collective-permute-start(bf16[640,128]{1,0:T(8,128)(2,1)S(1)} %get-tuple-element.87), channel_id=1, source_target_pairs={{0,8},{8,0},{1,9},{9,1},{2,10},{10,2},{3,11},{11,3},{4,12},{12,4},... | collective-permute-start | bytes 491528 | tf_op jit(solution)/shard_map/ppermute | solution.py:463
  72.8 2.3 %grads_own.1 = (f32[1280,128]{1,0:T(8,128)S(1)}, f32[1280,128]{1,0:T(8,128)S(1)}) custom-call(bf16[1296,128]{1,0:T(8,128)(2,1)S(1)} %get-tuple-element.48.kv.refs_0_, bf16[128,1408]{1,0:T(8,128)(2,1)S(1)} %get-tuple-element.50.refs_1_, bf16[2,960,960]{2,1,0:T(8,128)(2,1)S(1)} %get-tuple-element.51.refs_2_, bf16[320,640]{1,0:T(8,128)(2,1)S(1)} %get-tuple-element.52.refs_3_, ...), custom_call_target="tpu_custom_call" | custom-call | flops 3000000000 | bytes 1048576 | tf_op jit(solution)/shard_map/grads_own/pallas_call | solution.py:58
  75.1 0.0 collective-permute-done.7.far_dq
  75.1 2.2 %collective-permute-done.8.dkv3 = bf16[1280,128]{1,0:T(8,128)(2,1)S(1)} collective-permute-done((bf16[1280,128]{1,0:T(8,128)(2,1)S(1)}, bf16[1280,128]{1,0:T(8,128)(2,1)S(1)}, u32[]{:S(2)}, u32[]{:S(2)}) %collective-permute-start.8) | collective-permute-done | bytes 327712 | tf_op jit(solution)/shard_map/ppermute | solution.py:459
  77.3 1.2 %merge.1 = bf16[16,128,128]{2,1,0:T(8,128)(2,1)S(1)} custom-call(s32[2]{0:T(128)S(1)} %get-tuple-element.47.at_ref, f32[1280,128]{1,0:T(8,128)S(1)} %get-tuple-element.86.own_dq, bf16[640,128]{1,0:T(8,128)(2,1)S(1)} %collective-permute-done.7.far_dq, f32[1280,128]{1,0:T(8,128)S(1)} %get-tuple-element.88.own_dkv, ...), custom_call_target="tpu_custom_call" | custom-call | flops 1048576 | bytes 1048576 | tf_op jit(solution)/shard_map/merge/pallas_call | solution.py:58
  78.4 13.1 %all_to_all.11.in_ref = bf16[16,128,128]{2,1,0:T(8,128)(2,1)S(1)} all-to-all(bf16[16,128,128]{2,1,0:T(8,128)(2,1)S(1)} %merge.1), channel_id=1, replica_groups=mesh['y'=4,'zl'=2,'c'=2,'zh'=2,'x'=4] {'y','zl','zh'}, dimensions={0} | all-to-all | bytes 1048576 | tf_op jit(solution)/shard_map/all_to_all | solution.py:562
  91.5 1.0 %join.1 = (bf16[80,1024]{1,0:T(8,128)(2,1)}, bf16[80,1024]{1,0:T(8,128)(2,1)}, bf16[80,1024]{1,0:T(8,128)(2,1)}) custom-call(bf16[16,128,128]{2,1,0:T(8,128)(2,1)S(1)} %all_to_all.11.in_ref), custom_call_target="tpu_custom_call" | custom-call | flops 1048576 | bytes 1048576 | tf_op jit(solution)/shard_map/join/pallas_call | solution.py:58
Async XLA Ops:
  26.6 2.9 %collective-permute-start = (bf16[1296,128]{1,0:T(8,128)(2,1)S(1)}, bf16[1296,128]{1,0:T(8,128)(2,1)S(1)}, u32[]{:S(2)}, u32[]{:S(2)}) collective-permute-start(bf16[1296,128]{1,0:T(8,128)(2,1)S(1)} %get-tuple-element.49.qg0.refs_5_), channel_id=1, source_target_pairs={{0,8},{8,0},{1,9},{9,1},{2,10},{10,2},{3,11},{11,3},{4,12},{12,4},... | collective-permute-start | bytes 995336 | tf_op jit(solution)/shard_map/ppermute | solution.py:463
  26.7 10.7 %collective-permute-start.2 = (bf16[1296,128]{1,0:T(8,128)(2,1)S(1)}, bf16[1296,128]{1,0:T(8,128)(2,1)S(1)}, u32[]{:S(2)}, u32[]{:S(2)}) collective-permute-start(bf16[1296,128]{1,0:T(8,128)(2,1)S(1)} %get-tuple-element.48.kv.refs_0_), channel_id=1, source_target_pairs={{0,3},{1,0},{2,1},{3,2},{8,9},{9,10},{10,11},{11,8},{4,7},{5,4},{6... | collective-permute-start | bytes 995336 | tf_op jit(solution)/shard_map/ppermute | solution.py:459
  29.5 8.6 %collective-permute-start.1 = (bf16[1296,128]{1,0:T(8,128)(2,1)S(1)}, bf16[1296,128]{1,0:T(8,128)(2,1)S(1)}, u32[]{:S(2)}, u32[]{:S(2)}) collective-permute-start(bf16[1296,128]{1,0:T(8,128)(2,1)S(1)} %get-tuple-element.48.kv.refs_0_), channel_id=1, source_target_pairs={{0,1},{1,2},{2,3},{3,0},{8,11},{9,8},{10,9},{11,10},{4,5},{5,6},{6... | collective-permute-start | bytes 995336 | tf_op jit(solution)/shard_map/ppermute | solution.py:459
  38.1 8.3 %collective-permute-start.3 = (bf16[1296,128]{1,0:T(8,128)(2,1)S(1)}, bf16[1296,128]{1,0:T(8,128)(2,1)S(1)}, u32[]{:S(2)}, u32[]{:S(2)}) collective-permute-start(bf16[1296,128]{1,0:T(8,128)(2,1)S(1)} %collective-permute-done.1.kv1.refs_0_), channel_id=1, source_target_pairs={{0,1},{1,2},{2,3},{3,0},{8,11},{9,8},{10,9},{11,10},{4,5},{5,6},{6... | collective-permute-start | bytes 995336 | tf_op jit(solution)/shard_map/ppermute | solution.py:459
  49.8 1.5 %collective-permute-start.4 = (f32[3,2,1024]{2,1,0:T(2,128)S(1)}, f32[3,2,1024]{2,1,0:T(2,128)S(1)}, u32[]{:S(2)}, u32[]{:S(2)}) collective-permute-start(f32[3,2,1024]{2,1,0:T(2,128)S(1)} %get-tuple-element.65.refs_7_), channel_id=1, source_target_pairs={{0,8},{8,0},{1,9},{9,1},{2,10},{10,2},{3,11},{11,3},{4,12},{12,4},... | collective-permute-start | bytes 73736 | tf_op jit(solution)/shard_map/ppermute | solution.py:463
  55.8 8.4 %collective-permute-start.6 = (bf16[1280,128]{1,0:T(8,128)(2,1)S(1)}, bf16[1280,128]{1,0:T(8,128)(2,1)S(1)}, u32[]{:S(2)}, u32[]{:S(2)}) collective-permute-start(bf16[1280,128]{1,0:T(8,128)(2,1)S(1)} %get-tuple-element.80), channel_id=1, source_target_pairs={{0,1},{1,2},{2,3},{3,0},{8,11},{9,8},{10,9},{11,10},{4,5},{5,6},{6... | collective-permute-start | bytes 983048 | tf_op jit(solution)/shard_map/ppermute | solution.py:459
  60.5 11.2 %collective-permute-start.5 = (bf16[1280,128]{1,0:T(8,128)(2,1)S(1)}, bf16[1280,128]{1,0:T(8,128)(2,1)S(1)}, u32[]{:S(2)}, u32[]{:S(2)}) collective-permute-start(bf16[1280,128]{1,0:T(8,128)(2,1)S(1)} %get-tuple-element.73), channel_id=1, source_target_pairs={{0,3},{1,0},{2,1},{3,2},{8,9},{9,10},{10,11},{11,8},{4,7},{5,4},{6... | collective-permute-start | bytes 983048 | tf_op jit(solution)/shard_map/ppermute | solution.py:459
  68.9 8.4 %collective-permute-start.8 = (bf16[1280,128]{1,0:T(8,128)(2,1)S(1)}, bf16[1280,128]{1,0:T(8,128)(2,1)S(1)}, u32[]{:S(2)}, u32[]{:S(2)}) collective-permute-start(bf16[1280,128]{1,0:T(8,128)(2,1)S(1)} %get-tuple-element.90), channel_id=1, source_target_pairs={{0,1},{1,2},{2,3},{3,0},{8,11},{9,8},{10,9},{11,10},{4,5},{5,6},{6... | collective-permute-start | bytes 983048 | tf_op jit(solution)/shard_map/ppermute | solution.py:459
  71.8 3.3 %collective-permute-start.7 = (bf16[640,128]{1,0:T(8,128)(2,1)S(1)}, bf16[640,128]{1,0:T(8,128)(2,1)S(1)}, u32[]{:S(2)}, u32[]{:S(2)}) collective-permute-start(bf16[640,128]{1,0:T(8,128)(2,1)S(1)} %get-tuple-element.87), channel_id=1, source_target_pairs={{0,8},{8,0},{1,9},{9,1},{2,10},{10,2},{3,11},{11,3},{4,12},{12,4},... | collective-permute-start | bytes 491528 | tf_op jit(solution)/shard_map/ppermute | solution.py:463

commit v7 on v6

--- a/solution.py
+++ b/solution.py
@@ -123,7 +123,7 @@
         kv_ref[rows, :] = in_ref[chunk, pl.ds(pl.multiple_of(ROWS + part, 16), 16), :]
         return 0
 
-    lax.fori_loop(0, OWN // 16, move, 0, unroll=8)
+    lax.fori_loop(0, OWN // 16, move, 0, unroll=20)
 
     def move_docs(i, _):
         at = place(i) * 16
@@ -435,7 +435,7 @@
         out_ref[c, 112:128, :] = groups[4].astype(BF)
         return 0
 
-    lax.fori_loop(0, 16, chunk, 0)
+    lax.fori_loop(0, 16, chunk, 0, unroll=8)
 
 
 def join_kernel(in_ref, q_out, k_out, v_out):
@@ -502,7 +502,7 @@
         scratch=side(1),
         flops=2_500_000_000,
     )
-    kv1, kv3, first = lax.optimization_barrier((kv1, kv3, first))
+    kv1, first = lax.optimization_barrier((kv1, first))
     kv2 = shifted(kv1, 1)
     near, kvt1, kvt3, p1, p3, rest1, rest3, top1, top3 = call(
         near_totals_kernel,

time: 92.8 us -> 91.6 us (0.987)
  waiting for transfers between devices: 10.5 us -> 7.2 us
  starting transfers between devices: 8.38 us -> 10.7 us
    ppermute x6, waiting for transfers between devices: 9.46 us -> 6.35 us  [shifted(): return lax.ppermute(array, ('c', 'x'), pairs)]
    ppermute x6, starting transfers between devices: 6.81 us -> 8.61 us  [shifted(): return lax.ppermute(array, ('c', 'x'), pairs)]
  transfers between devices with their start and end apart: 9 -> 9, of which waited for: 6 -> 5; matrix products, arithmetic and copies ran while one was open for 0% -> 0% of each run, Pallas kernels for 26% -> 26%
where the time goes in v7:
time: 91.6 us; the launch traced here: 91.3 us
  Pallas kernels  37.7 us (41%)
  blocking collectives  35.1 us (38%)
  starting transfers between devices  10.7 us (12%)
  waiting for transfers between devices  7.2 us (8%)
    pallas_call x12, Pallas kernels, call(): pl.pallas_call(kernel, out_shape=outs, in_specs=[sm] * smem_in + [vm] * (...  37.7 us
    all_to_all x1, blocking collectives, body(): packed = lax.all_to_all(packed, BY_HEAD, 0, 0, tiled=True)  21.9 us
    all_to_all x1, blocking collectives, body(): merged = lax.all_to_all(merged, BY_HEAD, 0, 0, tiled=True)  13.1 us
    ppermute x6, starting transfers between devices, shifted(): return lax.ppermute(array, ('c', 'x'), pairs)  8.61 us
    ppermute x6, waiting for transfers between devices, shifted(): return lax.ppermute(array, ('c', 'x'), pairs)  6.35 us
    ppermute x3, starting transfers between devices, crossed(): return lax.ppermute(array, 'c', [(0, 1), (1, 0)])  2.04 us
  transfers between devices with their start and end apart: 9, of which 5 were waited for; matrix products, arithmetic and copies ran while one was open for 0% of the time, Pallas kernels for 26%

profile of v7, /device:TPU:0, one launch (start us, length us, event | category | flops | bytes accessed | tf_op | source)
XLA Modules:
  0.0 91.3 jit_solution(16919030945428340154)
XLA Ops:
  0.6 2.3 %pack.1 = bf16[16,176,128]{2,1,0:T(8,128)(2,1)} custom-call(bf16[80,1024]{1,0:T(8,128)(2,1)} %q_ref.1, bf16[80,1024]{1,0:T(8,128)(2,1)} %k_ref.1, bf16[80,1024]{1,0:T(8,128)(2,1)} %v_ref.1, bf16[80,1024]{1,0:T(8,128)(2,1)} %g_ref.1, s32[640]{0:T(1024)} %doc_ref.1), custom_call_target="tpu_custom_call" | custom-call | flops 1048576 | bytes 1048576 | tf_op jit(solution)/shard_map/pack/pallas_call | solution.py:58
  2.9 21.9 %all_to_all.10.in_ref = bf16[16,176,128]{2,1,0:T(8,128)(2,1)S(1)} all-to-all(bf16[16,176,128]{2,1,0:T(8,128)(2,1)} %pack.1), channel_id=1, replica_groups=mesh['y'=4,'zl'=2,'c'=2,'zh'=2,'x'=4] {'y','zl','zh'}, dimensions={0} | all-to-all | bytes 1441792 | tf_op jit(solution)/shard_map/all_to_all | solution.py:474
  24.9 1.6 %order.1 = (s32[2]{0:T(128)S(1)}, bf16[1296,128]{1,0:T(8,128)(2,1)S(1)}, bf16[1296,128]{1,0:T(8,128)(2,1)S(1)}) custom-call(bf16[16,176,128]{2,1,0:T(8,128)(2,1)S(1)} %all_to_all.10.in_ref), custom_call_target="tpu_custom_call" | custom-call | flops 1048576 | bytes 1048576 | tf_op jit(solution)/shard_map/order/pallas_call | solution.py:58
  26.5 0.1 collective-permute-start
  26.6 1.6 %collective-permute-start.1 = (bf16[1296,128]{1,0:T(8,128)(2,1)S(1)}, bf16[1296,128]{1,0:T(8,128)(2,1)S(1)}, u32[]{:S(2)}, u32[]{:S(2)}) collective-permute-start(bf16[1296,128]{1,0:T(8,128)(2,1)S(1)} %get-tuple-element.47.kv.refs_0_), channel_id=1, source_target_pairs={{0,1},{1,2},{2,3},{3,0},{8,11},{9,8},{10,9},{11,10},{4,5},{5,6},{6... | collective-permute-start | bytes 995336 | tf_op jit(solution)/shard_map/ppermute | solution.py:459
  28.2 1.7 %collective-permute-start.3 = (bf16[1296,128]{1,0:T(8,128)(2,1)S(1)}, bf16[1296,128]{1,0:T(8,128)(2,1)S(1)}, u32[]{:S(2)}, u32[]{:S(2)}) collective-permute-start(bf16[1296,128]{1,0:T(8,128)(2,1)S(1)} %get-tuple-element.47.kv.refs_0_), channel_id=1, source_target_pairs={{0,3},{1,0},{2,1},{3,2},{8,9},{9,10},{10,11},{11,8},{4,7},{5,4},{6... | collective-permute-start | bytes 995336 | tf_op jit(solution)/shard_map/ppermute | solution.py:459
  29.9 0.0 collective-permute-done.qg1.refs_6_
  29.9 3.4 %totals_own.1 = (f32[3,2,1024]{2,1,0:T(2,128)S(1)}, bf16[2,64,960]{2,1,0:T(8,128)(2,1)S(1)}, bf16[64,640]{1,0:T(8,128)(2,1)S(1)}, bf16[128,1408]{1,0:T(8,128)(2,...) custom-call(bf16[1296,128]{1,0:T(8,128)(2,1)S(1)} %get-tuple-element.47.kv.ref, ...), custom_call_target="tpu_custom_call" | custom-call | flops 2500000000 | bytes 1048576 | tf_op jit(solution)/shard_map/totals_own/pallas_call | solution.py:58
  33.3 3.2 %collective-permute-done.1.kv1.refs_0_ = bf16[1296,128]{1,0:T(8,128)(2,1)S(1)} collective-permute-done((bf16[1296,128]{1,0:T(8,128)(2,1)S(1)}, bf16[1296,128]{1,0:T(8,128)(2,1)S(1)}, u32[]{:S(2)}, u32[]{:S(2)}) %collective-permute-start.1) | collective-permute-done | bytes 331808 | tf_op jit(solution)/shard_map/ppermute | solution.py:459
  36.6 1.6 %collective-permute-start.2 = (bf16[1296,128]{1,0:T(8,128)(2,1)S(1)}, bf16[1296,128]{1,0:T(8,128)(2,1)S(1)}, u32[]{:S(2)}, u32[]{:S(2)}) collective-permute-start(bf16[1296,128]{1,0:T(8,128)(2,1)S(1)} %collective-permute-done.1.kv1.refs_0_), channel_id=1, source_target_pairs={{0,1},{1,2},{2,3},{3,0},{8,11},{9,8},{10,9},{11,10},{4,5},{5,6},{6... | collective-permute-start | bytes 995336 | tf_op jit(solution)/shard_map/ppermute | solution.py:459
  38.2 0.0 collective-permute-done.3.kv3.refs_0_
  38.2 6.0 %totals_near.1 = (f32[3,2,1024]{2,1,0:T(2,128)S(1)}, bf16[128,1408]{1,0:T(8,128)(2,1)S(1)}, bf16[128,1408]{1,0:T(8,128)(2,1)S(1)}, bf16[2,960,960]{2,1,0:T(8,128...) custom-call(bf16[1296,128]{1,0:T(8,128)(2,1)S(1)} %collective-permut, ...), custom_call_target="tpu_custom_call" | custom-call | flops 5000000000 | bytes 1048576 | tf_op jit(solution)/shard_map/totals_near/pallas_call | solution.py:58
  44.2 1.0 %collective-permute-done.2.kv.refs_0_ = bf16[1296,128]{1,0:T(8,128)(2,1)S(1)} collective-permute-done((bf16[1296,128]{1,0:T(8,128)(2,1)S(1)}, bf16[1296,128]{1,0:T(8,128)(2,1)S(1)}, u32[]{:S(2)}, u32[]{:S(2)}) %collective-permute-start.2) | collective-permute-done | bytes 331808 | tf_op jit(solution)/shard_map/ppermute | solution.py:459
  45.2 3.4 %totals_far.1 = (f32[3,2,1024]{2,1,0:T(2,128)S(1)}, bf16[128,1408]{1,0:T(8,128)(2,1)S(1)}, bf16[2,960,960]{2,1,0:T(8,128)(2,1)S(1)}, bf16[320,640]{1,0:T(8,128)(2,1)S(1)}, f32[3,4,1,1024]{3,2,1,0:T(1,128)S(1)}) custom-call(bf16[1296,128]{1,0:T(8,128)(2,1)S(1)} %collective-permute-done.2.kv.refs_0_, bf16[1296,128]{1,0:T(8,128)(2,1)S(1)} %get-tuple-element.48.qg0.refs_5_, ...), custom_call_target="tpu_custom_call" | custom-call | flops 2500000000 | bytes 1048576 | tf_op jit(solution)/shard_map/totals_far/pallas_call | solution.py:58
  48.6 0.7 collective-permute-start.4
  49.3 0.8 collective-permute-done.4.refs_8_
  50.1 4.6 %grads_far.1 = (f32[3,2,1024]{2,1,0:T(2,128)S(1)}, f32[2,64,960]{2,1,0:T(8,128)S(1)}, f32[64,640]{1,0:T(8,128)S(1)}, bf16[1280,128]{1,0:T(8,128)(2,1)S(1)}) custom-call(bf16[1296,128]{1,0:T(8,128)(2,1)S(1)} %collective-permute-done.2.kv.refs_0_, bf16[128,1408]{1,0:T(8,128)(2,1)S(1)} %get-tuple-element.59.refs_1_, ...), custom_call_target="tpu_custom_call" | custom-call | flops 6000000000 | bytes 1048576 | tf_op jit(solution)/shard_map/grads_far/pallas_call | solution.py:58
  54.7 0.9 collective-permute-start.6
  55.6 4.6 %grads_one.1 = (f32[2,64,960]{2,1,0:T(8,128)S(1)}, f32[64,640]{1,0:T(8,128)S(1)}, bf16[1280,128]{1,0:T(8,128)(2,1)S(1)}) custom-call(bf16[1296,128]{1,0:T(8,128)(2,1)S(1)} %collective-permute-done.1.kv1.refs_0_, bf16[128,1408]{1,0:T(8,128)(2,1)S(1)} %get-tuple-element.65.refs_1_, bf16[2,960,960]{2,1,0:T(8,128)(2,1)S(1)} %get-tuple-element.66.refs_2_, ...), custom_call_target="tpu_custom_call" | custom-call | flops 6000000000 | bytes 1048576 | tf_op jit(solution)/shard_map/grads_one/pallas_call | solution.py:58
  60.2 2.8 %collective-permute-start.5 = (bf16[1280,128]{1,0:T(8,128)(2,1)S(1)}, bf16[1280,128]{1,0:T(8,128)(2,1)S(1)}, u32[]{:S(2)}, u32[]{:S(2)}) collective-permute-start(bf16[1280,128]{1,0:T(8,128)(2,1)S(1)} %get-tuple-element.71), channel_id=1, source_target_pairs={{0,3},{1,0},{2,1},{3,2},{8,9},{9,10},{10,11},{11,8},{4,7},{5,4},{6... | collective-permute-start | bytes 983048 | tf_op jit(solution)/shard_map/ppermute | solution.py:459
  63.0 0.1 collective-permute-done.6.refs_10_
  63.1 4.7 %grads_three.1 = (f32[2,64,960]{2,1,0:T(8,128)S(1)}, f32[64,640]{1,0:T(8,128)S(1)}, bf16[1280,128]{1,0:T(8,128)(2,1)S(1)}) custom-call(bf16[1296,128]{1,0:T(8,128)(2,1)S(1)} %collective-permute-done.3.kv3.refs_0_, bf16[128,1408]{1,0:T(8,128)(2,1)S(1)} %get-tuple-element.72.refs_1_, bf16[2,960,960]{2,1,0:T(8,128)(2,1)S(1)} %get-tuple-element.73.refs_2_, ...), custom_call_target="tpu_custom_call" | custom-call | flops 6000000000 | bytes 1048576 | tf_op jit(solution)/shard_map/grads_three/pallas_call | solution.py:58
  67.8 0.1 collective-permute-start.8
  67.8 2.8 %grads_own_far.1 = (bf16[640,128]{1,0:T(8,128)(2,1)S(1)}, f32[64,640]{1,0:T(8,128)S(1)}, f32[1280,128]{1,0:T(8,128)S(1)}) custom-call(bf16[1296,128]{1,0:T(8,128)(2,1)S(1)} %get-tuple-element.47.kv.refs_0_, bf16[128,1408]{1,0:T(8,128)(2,1)S(1)} %get-tuple-element.49.refs_1_, bf16[2,960,960]{2,1,0:T(8,128)(2,1)S(1)} %get-tuple-element.50.refs_2_, ...), custom_call_target="tpu_custom_call" | custom-call | flops 3000000000 | bytes 1048576 | tf_op jit(solution)/shard_map/grads_own_far/pallas_call | solution.py:58
  70.6 0.0 collective-permute-done.5.dkv1
  70.6 1.2 %collective-permute-start.7 = (bf16[640,128]{1,0:T(8,128)(2,1)S(1)}, bf16[640,128]{1,0:T(8,128)(2,1)S(1)}, u32[]{:S(2)}, u32[]{:S(2)}) collective-permute-start(bf16[640,128]{1,0:T(8,128)(2,1)S(1)} %get-tuple-element.85), channel_id=1, source_target_pairs={{0,8},{8,0},{1,9},{9,1},{2,10},{10,2},{3,11},{11,3},{4,12},{12,4},... | collective-permute-start | bytes 491528 | tf_op jit(solution)/shard_map/ppermute | solution.py:463
  71.8 2.3 %grads_own.1 = (f32[1280,128]{1,0:T(8,128)S(1)}, f32[1280,128]{1,0:T(8,128)S(1)}) custom-call(bf16[1296,128]{1,0:T(8,128)(2,1)S(1)} %get-tuple-element.47.kv.refs_0_, bf16[128,1408]{1,0:T(8,128)(2,1)S(1)} %get-tuple-element.49.refs_1_, bf16[2,960,960]{2,1,0:T(8,128)(2,1)S(1)} %get-tuple-element.50.refs_2_, bf16[320,640]{1,0:T(8,128)(2,1)S(1)} %get-tuple-element.51.refs_3_, ...), custom_call_target="tpu_custom_call" | custom-call | flops 3000000000 | bytes 1048576 | tf_op jit(solution)/shard_map/grads_own/pallas_call | solution.py:58
  74.1 0.0 collective-permute-done.7.far_dq
  74.1 2.0 %collective-permute-done.8.dkv3 = bf16[1280,128]{1,0:T(8,128)(2,1)S(1)} collective-permute-done((bf16[1280,128]{1,0:T(8,128)(2,1)S(1)}, bf16[1280,128]{1,0:T(8,128)(2,1)S(1)}, u32[]{:S(2)}, u32[]{:S(2)}) %collective-permute-start.8) | collective-permute-done | bytes 327712 | tf_op jit(solution)/shard_map/ppermute | solution.py:459
  76.1 1.1 %merge.1 = bf16[16,128,128]{2,1,0:T(8,128)(2,1)S(1)} custom-call(s32[2]{0:T(128)S(1)} %get-tuple-element.46.at_ref, f32[1280,128]{1,0:T(8,128)S(1)} %get-tuple-element.84.own_dq, bf16[640,128]{1,0:T(8,128)(2,1)S(1)} %collective-permute-done.7.far_dq, f32[1280,128]{1,0:T(8,128)S(1)} %get-tuple-element.86.own_dkv, ...), custom_call_target="tpu_custom_call" | custom-call | flops 1048576 | bytes 1048576 | tf_op jit(solution)/shard_map/merge/pallas_call | solution.py:58
  77.2 13.1 %all_to_all.11.in_ref = bf16[16,128,128]{2,1,0:T(8,128)(2,1)S(1)} all-to-all(bf16[16,128,128]{2,1,0:T(8,128)(2,1)S(1)} %merge.1), channel_id=1, replica_groups=mesh['y'=4,'zl'=2,'c'=2,'zh'=2,'x'=4] {'y','zl','zh'}, dimensions={0} | all-to-all | bytes 1048576 | tf_op jit(solution)/shard_map/all_to_all | solution.py:562
  90.3 1.0 %join.1 = (bf16[80,1024]{1,0:T(8,128)(2,1)}, bf16[80,1024]{1,0:T(8,128)(2,1)}, bf16[80,1024]{1,0:T(8,128)(2,1)}) custom-call(bf16[16,128,128]{2,1,0:T(8,128)(2,1)S(1)} %all_to_all.11.in_ref), custom_call_target="tpu_custom_call" | custom-call | flops 1048576 | bytes 1048576 | tf_op jit(solution)/shard_map/join/pallas_call | solution.py:58
Async XLA Ops:
  26.5 3.4 %collective-permute-start = (bf16[1296,128]{1,0:T(8,128)(2,1)S(1)}, bf16[1296,128]{1,0:T(8,128)(2,1)S(1)}, u32[]{:S(2)}, u32[]{:S(2)}) collective-permute-start(bf16[1296,128]{1,0:T(8,128)(2,1)S(1)} %get-tuple-element.48.qg0.refs_5_), channel_id=1, source_target_pairs={{0,8},{8,0},{1,9},{9,1},{2,10},{10,2},{3,11},{11,3},{4,12},{12,4},... | collective-permute-start | bytes 995336 | tf_op jit(solution)/shard_map/ppermute | solution.py:463
  26.6 9.9 %collective-permute-start.1 = (bf16[1296,128]{1,0:T(8,128)(2,1)S(1)}, bf16[1296,128]{1,0:T(8,128)(2,1)S(1)}, u32[]{:S(2)}, u32[]{:S(2)}) collective-permute-start(bf16[1296,128]{1,0:T(8,128)(2,1)S(1)} %get-tuple-element.47.kv.refs_0_), channel_id=1, source_target_pairs={{0,1},{1,2},{2,3},{3,0},{8,11},{9,8},{10,9},{11,10},{4,5},{5,6},{6... | collective-permute-start | bytes 995336 | tf_op jit(solution)/shard_map/ppermute | solution.py:459
  28.2 10.0 %collective-permute-start.3 = (bf16[1296,128]{1,0:T(8,128)(2,1)S(1)}, bf16[1296,128]{1,0:T(8,128)(2,1)S(1)}, u32[]{:S(2)}, u32[]{:S(2)}) collective-permute-start(bf16[1296,128]{1,0:T(8,128)(2,1)S(1)} %get-tuple-element.47.kv.refs_0_), channel_id=1, source_target_pairs={{0,3},{1,0},{2,1},{3,2},{8,9},{9,10},{10,11},{11,8},{4,7},{5,4},{6... | collective-permute-start | bytes 995336 | tf_op jit(solution)/shard_map/ppermute | solution.py:459
  36.6 8.6 %collective-permute-start.2 = (bf16[1296,128]{1,0:T(8,128)(2,1)S(1)}, bf16[1296,128]{1,0:T(8,128)(2,1)S(1)}, u32[]{:S(2)}, u32[]{:S(2)}) collective-permute-start(bf16[1296,128]{1,0:T(8,128)(2,1)S(1)} %collective-permute-done.1.kv1.refs_0_), channel_id=1, source_target_pairs={{0,1},{1,2},{2,3},{3,0},{8,11},{9,8},{10,9},{11,10},{4,5},{5,6},{6... | collective-permute-start | bytes 995336 | tf_op jit(solution)/shard_map/ppermute | solution.py:459
  48.6 1.6 %collective-permute-start.4 = (f32[3,2,1024]{2,1,0:T(2,128)S(1)}, f32[3,2,1024]{2,1,0:T(2,128)S(1)}, u32[]{:S(2)}, u32[]{:S(2)}) collective-permute-start(f32[3,2,1024]{2,1,0:T(2,128)S(1)} %get-tuple-element.63.refs_7_), channel_id=1, source_target_pairs={{0,8},{8,0},{1,9},{9,1},{2,10},{10,2},{3,11},{11,3},{4,12},{12,4},... | collective-permute-start | bytes 73736 | tf_op jit(solution)/shard_map/ppermute | solution.py:463
  54.7 8.4 %collective-permute-start.6 = (bf16[1280,128]{1,0:T(8,128)(2,1)S(1)}, bf16[1280,128]{1,0:T(8,128)(2,1)S(1)}, u32[]{:S(2)}, u32[]{:S(2)}) collective-permute-start(bf16[1280,128]{1,0:T(8,128)(2,1)S(1)} %get-tuple-element.78), channel_id=1, source_target_pairs={{0,1},{1,2},{2,3},{3,0},{8,11},{9,8},{10,9},{11,10},{4,5},{5,6},{6... | collective-permute-start | bytes 983048 | tf_op jit(solution)/shard_map/ppermute | solution.py:459
  60.2 10.4 %collective-permute-start.5 = (bf16[1280,128]{1,0:T(8,128)(2,1)S(1)}, bf16[1280,128]{1,0:T(8,128)(2,1)S(1)}, u32[]{:S(2)}, u32[]{:S(2)}) collective-permute-start(bf16[1280,128]{1,0:T(8,128)(2,1)S(1)} %get-tuple-element.71), channel_id=1, source_target_pairs={{0,3},{1,0},{2,1},{3,2},{8,9},{9,10},{10,11},{11,8},{4,7},{5,4},{6... | collective-permute-start | bytes 983048 | tf_op jit(solution)/shard_map/ppermute | solution.py:459
  67.8 8.4 %collective-permute-start.8 = (bf16[1280,128]{1,0:T(8,128)(2,1)S(1)}, bf16[1280,128]{1,0:T(8,128)(2,1)S(1)}, u32[]{:S(2)}, u32[]{:S(2)}) collective-permute-start(bf16[1280,128]{1,0:T(8,128)(2,1)S(1)} %get-tuple-element.88), channel_id=1, source_target_pairs={{0,1},{1,2},{2,3},{3,0},{8,11},{9,8},{10,9},{11,10},{4,5},{5,6},{6... | collective-permute-start | bytes 983048 | tf_op jit(solution)/shard_map/ppermute | solution.py:459
  70.6 3.5 %collective-permute-start.7 = (bf16[640,128]{1,0:T(8,128)(2,1)S(1)}, bf16[640,128]{1,0:T(8,128)(2,1)S(1)}, u32[]{:S(2)}, u32[]{:S(2)}) collective-permute-start(bf16[640,128]{1,0:T(8,128)(2,1)S(1)} %get-tuple-element.85), channel_id=1, source_target_pairs={{0,8},{8,0},{1,9},{9,1},{2,10},{10,2},{3,11},{11,3},{4,12},{12,4},... | collective-permute-start | bytes 491528 | tf_op jit(solution)/shard_map/ppermute | solution.py:463

commit v8 on v7

--- a/solution.py
+++ b/solution.py
@@ -264,10 +264,13 @@
 
 
 def own_totals_kernel(
-    kv, qg0, qg1, stat_ref, gt_ref, gt_rest_ref, kvt, p, rest, top, *scratch
+    kv, qg0, qg1, stat_ref, gt_ref, gt_rest_ref, kvt, p, rest, top, prob_grad_ref, *scratch
 ):
     for n, ref in enumerate((qg0, qg1)):
         gt_ref[n] = ref[0:LONG, :].T[HD:, :]
+        _, g0 = halves(ref[0:LONG, :])
+        for at in range(0, LONG, STEP):
+            prob_grad_ref[n, at : at + STEP, :] = dot_nt(kv[at : at + STEP, :], g0)
     gt_rest_ref[...] = rest_rows(qg0, qg1).T[HD:, :]
     totals([kv], qg0, qg1, gt_ref, gt_rest_ref, stat_ref, [kvt], [p], [rest], [top], *scratch)
 
@@ -292,13 +295,14 @@
         stat_ref[n, 0:1, :], stat_ref[n, 1:2, :] = added(parts)
 
 
-def tile_grads(qg, starts, weights_of, dot, kv_ref, kvt_ref, dkv_ref):
+def tile_grads(qg, starts, weights_of, dot, kv_ref, kvt_ref, dkv_ref, prob_grad_of=None):
     q0, g0 = halves(qg)
     acc = None
     for at, width in starts:
         kv = kv_ref[at : at + width, :]
         p = weights_of(at)
-        ds = (p * (dot_nt(kv, g0) - dot)).astype(BF)
+        prob_grad = prob_grad_of(at) if prob_grad_of else dot_nt(kv, g0)
+        ds = (p * (prob_grad - dot)).astype(BF)
         dkv_ref[at : at + width, :] += dot_nn(p.astype(BF), g0) + dot_nn(ds, q0)
         part = dot_nn(kvt_ref[0:HD, lane_at(at) : lane_at(at) + width], ds)
         acc = part if acc is None else acc + part
@@ -343,7 +347,12 @@
 
         starts = [(at, STEP) for at in range(0, LONG, STEP)]
         dot = row_ref[n, 1:2, 0:LONG]
-        dq_ref[n] += tile_grads(qg_ref[n], starts, weights_of, dot, kv_ref, kvt_ref, dkv_ref)
+        prob_grad_of = None
+        if "prob_grad" in ref:
+            prob_grad_of = lambda at: ref["prob_grad"][n, at : at + STEP, :]
+        dq_ref[n] += tile_grads(
+            qg_ref[n], starts, weights_of, dot, kv_ref, kvt_ref, dkv_ref, prob_grad_of
+        )
         return 0
 
     for n in blocks:
@@ -494,10 +503,10 @@
     kept, kept_rest = shape(2, LONG, LONG), shape(REST, 2 * REST)
     kept_top = shape(3, LONG // STEP, 1, 1024, dtype=F32)
     grad_t = [shape(2, HD, LONG), shape(HD, 2 * REST)]
-    first, *grad_t, kvt0, p0, rest0, top0 = call(
+    first, *grad_t, kvt0, p0, rest0, top0, prob_grad = call(
         own_totals_kernel,
         "totals_own",
-        [stat, *grad_t, turned, kept, kept_rest, kept_top],
+        [stat, *grad_t, turned, kept, kept_rest, kept_top, shape(2, LONG, LONG, dtype=F32)],
         [kv, qg, qg_far],
         scratch=side(1),
         flops=2_500_000_000,
@@ -542,7 +551,8 @@
         if n == 1:
             arrays["relay"] = sent[2]
             takes = [*takes, "relay"]
-    takes = ["rows", "dq_in", "dq_rest_in"]
+    arrays["prob_grad"] = prob_grad
+    takes = ["rows", "dq_in", "dq_rest_in", "prob_grad"]
     gives = ["dq_send", "dq_rest", "dkv_out"]
     grads("grads_own_far", sets[0], arrays, takes, gives, blocks=(1,))
     far_dq = crossed(arrays["dq_send"])

time: 91.6 us -> 91.7 us (level)
  no operation moved by 1% of the time
where the time goes in v8:
time: 91.7 us; the launch traced here: 91.4 us
  Pallas kernels  37.8 us (41%)
  blocking collectives  35.1 us (38%)
  starting transfers between devices  10.6 us (12%)
  waiting for transfers between devices  7.19 us (8%)
    pallas_call x12, Pallas kernels, call(): pl.pallas_call(kernel, out_shape=outs, in_specs=[sm] * smem_in + [vm] * (...  37.8 us
    all_to_all x1, blocking collectives, body(): packed = lax.all_to_all(packed, BY_HEAD, 0, 0, tiled=True)  21.9 us
    all_to_all x1, blocking collectives, body(): merged = lax.all_to_all(merged, BY_HEAD, 0, 0, tiled=True)  13.1 us
    ppermute x6, starting transfers between devices, shifted(): return lax.ppermute(array, ('c', 'x'), pairs)  8.61 us
    ppermute x6, waiting for transfers between devices, shifted(): return lax.ppermute(array, ('c', 'x'), pairs)  6.33 us
    ppermute x3, starting transfers between devices, crossed(): return lax.ppermute(array, 'c', [(0, 1), (1, 0)])  2.03 us
  transfers between devices with their start and end apart: 9, of which 5 were waited for; matrix products, arithmetic and copies ran while one was open for 0% of the time, Pallas kernels for 26%

profile of v8, /device:TPU:0, one launch (start us, length us, event | category | flops | bytes accessed | tf_op | source)
XLA Modules:
  0.0 91.4 jit_solution(1066060870693821639)
XLA Ops:
  0.6 2.3 %pack.1 = bf16[16,176,128]{2,1,0:T(8,128)(2,1)} custom-call(bf16[80,1024]{1,0:T(8,128)(2,1)} %q_ref.1, bf16[80,1024]{1,0:T(8,128)(2,1)} %k_ref.1, bf16[80,1024]{1,0:T(8,128)(2,1)} %v_ref.1, bf16[80,1024]{1,0:T(8,128)(2,1)} %g_ref.1, s32[640]{0:T(1024)} %doc_ref.1), custom_call_target="tpu_custom_call" | custom-call | flops 1048576 | bytes 1048576 | tf_op jit(solution)/shard_map/pack/pallas_call | solution.py:58
  2.9 21.9 %all_to_all.10.in_ref = bf16[16,176,128]{2,1,0:T(8,128)(2,1)S(1)} all-to-all(bf16[16,176,128]{2,1,0:T(8,128)(2,1)} %pack.1), channel_id=1, replica_groups=mesh['y'=4,'zl'=2,'c'=2,'zh'=2,'x'=4] {'y','zl','zh'}, dimensions={0} | all-to-all | bytes 1441792 | tf_op jit(solution)/shard_map/all_to_all | solution.py:483
  24.9 1.6 %order.1 = (s32[2]{0:T(128)S(1)}, bf16[1296,128]{1,0:T(8,128)(2,1)S(1)}, bf16[1296,128]{1,0:T(8,128)(2,1)S(1)}) custom-call(bf16[16,176,128]{2,1,0:T(8,128)(2,1)S(1)} %all_to_all.10.in_ref), custom_call_target="tpu_custom_call" | custom-call | flops 1048576 | bytes 1048576 | tf_op jit(solution)/shard_map/order/pallas_call | solution.py:58
  26.5 0.1 collective-permute-start
  26.6 1.6 %collective-permute-start.1 = (bf16[1296,128]{1,0:T(8,128)(2,1)S(1)}, bf16[1296,128]{1,0:T(8,128)(2,1)S(1)}, u32[]{:S(2)}, u32[]{:S(2)}) collective-permute-start(bf16[1296,128]{1,0:T(8,128)(2,1)S(1)} %get-tuple-element.48.kv.refs_0_), channel_id=1, source_target_pairs={{0,1},{1,2},{2,3},{3,0},{8,11},{9,8},{10,9},{11,10},{4,5},{5,6},{6... | collective-permute-start | bytes 995336 | tf_op jit(solution)/shard_map/ppermute | solution.py:468
  28.2 1.7 %collective-permute-start.3 = (bf16[1296,128]{1,0:T(8,128)(2,1)S(1)}, bf16[1296,128]{1,0:T(8,128)(2,1)S(1)}, u32[]{:S(2)}, u32[]{:S(2)}) collective-permute-start(bf16[1296,128]{1,0:T(8,128)(2,1)S(1)} %get-tuple-element.48.kv.refs_0_), channel_id=1, source_target_pairs={{0,3},{1,0},{2,1},{3,2},{8,9},{9,10},{10,11},{11,8},{4,7},{5,4},{6... | collective-permute-start | bytes 995336 | tf_op jit(solution)/shard_map/ppermute | solution.py:468
  29.9 0.0 collective-permute-done.qg1.refs_6_
  29.9 4.4 %totals_own.1 = (f32[3,2,1024]{2,1,0:T(2,128)S(1)}, bf16[2,64,960]{2,1,0:T(8,128)(2,1)S(1)}, bf16[64,640]{1,0:T(8,128)(2,1)S(1)}, bf16[128,1408]{1,0:T(8,128)(2,...) custom-call(bf16[1296,128]{1,0:T(8,128)(2,1)S(1)} %get-tuple-element, ...), custom_call_target="tpu_custom_call" | custom-call | flops 2500000000 | bytes 1048576 | tf_op jit(solution)/shard_map/totals_own/pallas_call | solution.py:58
  34.4 2.2 %collective-permute-done.1.kv1.refs_0_ = bf16[1296,128]{1,0:T(8,128)(2,1)S(1)} collective-permute-done((bf16[1296,128]{1,0:T(8,128)(2,1)S(1)}, bf16[1296,128]{1,0:T(8,128)(2,1)S(1)}, u32[]{:S(2)}, u32[]{:S(2)}) %collective-permute-start.1) | collective-permute-done | bytes 331808 | tf_op jit(solution)/shard_map/ppermute | solution.py:468
  36.6 1.6 %collective-permute-start.2 = (bf16[1296,128]{1,0:T(8,128)(2,1)S(1)}, bf16[1296,128]{1,0:T(8,128)(2,1)S(1)}, u32[]{:S(2)}, u32[]{:S(2)}) collective-permute-start(bf16[1296,128]{1,0:T(8,128)(2,1)S(1)} %collective-permute-done.1.kv1.refs_0_), channel_id=1, source_target_pairs={{0,1},{1,2},{2,3},{3,0},{8,11},{9,8},{10,9},{11,10},{4,5},{5,6},{6... | collective-permute-start | bytes 995336 | tf_op jit(solution)/shard_map/ppermute | solution.py:468
  38.2 0.0 collective-permute-done.3.kv3.refs_0_
  38.2 6.0 %totals_near.1 = (f32[3,2,1024]{2,1,0:T(2,128)S(1)}, bf16[128,1408]{1,0:T(8,128)(2,1)S(1)}, bf16[128,1408]{1,0:T(8,128)(2,1)S(1)}, bf16[2,960,960]{2,1,0:T(8,128...) custom-call(bf16[1296,128]{1,0:T(8,128)(2,1)S(1)} %collective-permut, ...), custom_call_target="tpu_custom_call" | custom-call | flops 5000000000 | bytes 1048576 | tf_op jit(solution)/shard_map/totals_near/pallas_call | solution.py:58
  44.2 1.0 %collective-permute-done.2.kv.refs_0_ = bf16[1296,128]{1,0:T(8,128)(2,1)S(1)} collective-permute-done((bf16[1296,128]{1,0:T(8,128)(2,1)S(1)}, bf16[1296,128]{1,0:T(8,128)(2,1)S(1)}, u32[]{:S(2)}, u32[]{:S(2)}) %collective-permute-start.2) | collective-permute-done | bytes 331808 | tf_op jit(solution)/shard_map/ppermute | solution.py:468
  45.2 3.3 %totals_far.1 = (f32[3,2,1024]{2,1,0:T(2,128)S(1)}, bf16[128,1408]{1,0:T(8,128)(2,1)S(1)}, bf16[2,960,960]{2,1,0:T(8,128)(2,1)S(1)}, bf16[320,640]{1,0:T(8,128)(2,1)S(1)}, f32[3,4,1,1024]{3,2,1,0:T(1,128)S(1)}) custom-call(bf16[1296,128]{1,0:T(8,128)(2,1)S(1)} %collective-permute-done.2.kv.refs_0_, bf16[1296,128]{1,0:T(8,128)(2,1)S(1)} %get-tuple-element.49.qg0.refs_5_, ...), custom_call_target="tpu_custom_call" | custom-call | flops 2500000000 | bytes 1048576 | tf_op jit(solution)/shard_map/totals_far/pallas_call | solution.py:58
  48.6 0.7 collective-permute-start.4
  49.3 0.8 collective-permute-done.4.refs_8_
  50.1 4.7 %grads_far.1 = (f32[3,2,1024]{2,1,0:T(2,128)S(1)}, f32[2,64,960]{2,1,0:T(8,128)S(1)}, f32[64,640]{1,0:T(8,128)S(1)}, bf16[1280,128]{1,0:T(8,128)(2,1)S(1)}) custom-call(bf16[1296,128]{1,0:T(8,128)(2,1)S(1)} %collective-permute-done.2.kv.refs_0_, bf16[128,1408]{1,0:T(8,128)(2,1)S(1)} %get-tuple-element.60.refs_1_, ...), custom_call_target="tpu_custom_call" | custom-call | flops 6000000000 | bytes 1048576 | tf_op jit(solution)/shard_map/grads_far/pallas_call | solution.py:58
  54.8 0.9 collective-permute-start.6
  55.7 4.6 %grads_one.1 = (f32[2,64,960]{2,1,0:T(8,128)S(1)}, f32[64,640]{1,0:T(8,128)S(1)}, bf16[1280,128]{1,0:T(8,128)(2,1)S(1)}) custom-call(bf16[1296,128]{1,0:T(8,128)(2,1)S(1)} %collective-permute-done.1.kv1.refs_0_, bf16[128,1408]{1,0:T(8,128)(2,1)S(1)} %get-tuple-element.66.refs_1_, bf16[2,960,960]{2,1,0:T(8,128)(2,1)S(1)} %get-tuple-element.67.refs_2_, ...), custom_call_target="tpu_custom_call" | custom-call | flops 6000000000 | bytes 1048576 | tf_op jit(solution)/shard_map/grads_one/pallas_call | solution.py:58
  60.3 2.8 %collective-permute-start.5 = (bf16[1280,128]{1,0:T(8,128)(2,1)S(1)}, bf16[1280,128]{1,0:T(8,128)(2,1)S(1)}, u32[]{:S(2)}, u32[]{:S(2)}) collective-permute-start(bf16[1280,128]{1,0:T(8,128)(2,1)S(1)} %get-tuple-element.72), channel_id=1, source_target_pairs={{0,3},{1,0},{2,1},{3,2},{8,9},{9,10},{10,11},{11,8},{4,7},{5,4},{6... | collective-permute-start | bytes 983048 | tf_op jit(solution)/shard_map/ppermute | solution.py:468
  63.0 0.1 collective-permute-done.6.refs_10_
  63.2 4.7 %grads_three.1 = (f32[2,64,960]{2,1,0:T(8,128)S(1)}, f32[64,640]{1,0:T(8,128)S(1)}, bf16[1280,128]{1,0:T(8,128)(2,1)S(1)}) custom-call(bf16[1296,128]{1,0:T(8,128)(2,1)S(1)} %collective-permute-done.3.kv3.refs_0_, bf16[128,1408]{1,0:T(8,128)(2,1)S(1)} %get-tuple-element.73.refs_1_, bf16[2,960,960]{2,1,0:T(8,128)(2,1)S(1)} %get-tuple-element.74.refs_2_, ...), custom_call_target="tpu_custom_call" | custom-call | flops 6000000000 | bytes 1048576 | tf_op jit(solution)/shard_map/grads_three/pallas_call | solution.py:58
  67.9 0.1 collective-permute-start.8
  67.9 2.3 %grads_own_far.1 = (bf16[640,128]{1,0:T(8,128)(2,1)S(1)}, f32[64,640]{1,0:T(8,128)S(1)}, f32[1280,128]{1,0:T(8,128)S(1)}) custom-call(bf16[1296,128]{1,0:T(8,128)(2,1)S(1)} %get-tuple-element.48.kv.refs_0_, bf16[128,1408]{1,0:T(8,128)(2,1)S(1)} %get-tuple-element.50.refs_1_, bf16[2,960,960]{2,1,0:T(8,128)(2,1)S(1)} %get-tuple-element.51.refs_2_, ...), custom_call_target="tpu_custom_call" | custom-call | flops 3000000000 | bytes 1048576 | tf_op jit(solution)/shard_map/grads_own_far/pallas_call | solution.py:58
  70.2 0.0 collective-permute-done.5.dkv1
  70.2 1.2 %collective-permute-start.7 = (bf16[640,128]{1,0:T(8,128)(2,1)S(1)}, bf16[640,128]{1,0:T(8,128)(2,1)S(1)}, u32[]{:S(2)}, u32[]{:S(2)}) collective-permute-start(bf16[640,128]{1,0:T(8,128)(2,1)S(1)} %get-tuple-element.87), channel_id=1, source_target_pairs={{0,8},{8,0},{1,9},{9,1},{2,10},{10,2},{3,11},{11,3},{4,12},{12,4},... | collective-permute-start | bytes 491528 | tf_op jit(solution)/shard_map/ppermute | solution.py:472
  71.4 1.8 %grads_own.1 = (f32[1280,128]{1,0:T(8,128)S(1)}, f32[1280,128]{1,0:T(8,128)S(1)}) custom-call(bf16[1296,128]{1,0:T(8,128)(2,1)S(1)} %get-tuple-element.48.kv.refs_0_, bf16[128,1408]{1,0:T(8,128)(2,1)S(1)} %get-tuple-element.50.refs_1_, bf16[2,960,960]{2,1,0:T(8,128)(2,1)S(1)} %get-tuple-element.51.refs_2_, bf16[320,640]{1,0:T(8,128)(2,1)S(1)} %get-tuple-element.52.refs_3_, ...), custom_call_target="tpu_custom_call" | custom-call | flops 3000000000 | bytes 1048576 | tf_op jit(solution)/shard_map/grads_own/pallas_call | solution.py:58
  73.2 0.0 collective-permute-done.7.far_dq
  73.2 3.0 %collective-permute-done.8.dkv3 = bf16[1280,128]{1,0:T(8,128)(2,1)S(1)} collective-permute-done((bf16[1280,128]{1,0:T(8,128)(2,1)S(1)}, bf16[1280,128]{1,0:T(8,128)(2,1)S(1)}, u32[]{:S(2)}, u32[]{:S(2)}) %collective-permute-start.8) | collective-permute-done | bytes 327712 | tf_op jit(solution)/shard_map/ppermute | solution.py:468
  76.2 1.1 %merge.1 = bf16[16,128,128]{2,1,0:T(8,128)(2,1)S(1)} custom-call(s32[2]{0:T(128)S(1)} %get-tuple-element.47.at_ref, f32[1280,128]{1,0:T(8,128)S(1)} %get-tuple-element.86.own_dq, bf16[640,128]{1,0:T(8,128)(2,1)S(1)} %collective-permute-done.7.far_dq, f32[1280,128]{1,0:T(8,128)S(1)} %get-tuple-element.88.own_dkv, ...), custom_call_target="tpu_custom_call" | custom-call | flops 1048576 | bytes 1048576 | tf_op jit(solution)/shard_map/merge/pallas_call | solution.py:58
  77.3 13.1 %all_to_all.11.in_ref = bf16[16,128,128]{2,1,0:T(8,128)(2,1)S(1)} all-to-all(bf16[16,128,128]{2,1,0:T(8,128)(2,1)S(1)} %merge.1), channel_id=1, replica_groups=mesh['y'=4,'zl'=2,'c'=2,'zh'=2,'x'=4] {'y','zl','zh'}, dimensions={0} | all-to-all | bytes 1048576 | tf_op jit(solution)/shard_map/all_to_all | solution.py:572
  90.4 1.0 %join.1 = (bf16[80,1024]{1,0:T(8,128)(2,1)}, bf16[80,1024]{1,0:T(8,128)(2,1)}, bf16[80,1024]{1,0:T(8,128)(2,1)}) custom-call(bf16[16,128,128]{2,1,0:T(8,128)(2,1)S(1)} %all_to_all.11.in_ref), custom_call_target="tpu_custom_call" | custom-call | flops 1048576 | bytes 1048576 | tf_op jit(solution)/shard_map/join/pallas_call | solution.py:58
Async XLA Ops:
  26.5 3.4 %collective-permute-start = (bf16[1296,128]{1,0:T(8,128)(2,1)S(1)}, bf16[1296,128]{1,0:T(8,128)(2,1)S(1)}, u32[]{:S(2)}, u32[]{:S(2)}) collective-permute-start(bf16[1296,128]{1,0:T(8,128)(2,1)S(1)} %get-tuple-element.49.qg0.refs_5_), channel_id=1, source_target_pairs={{0,8},{8,0},{1,9},{9,1},{2,10},{10,2},{3,11},{11,3},{4,12},{12,4},... | collective-permute-start | bytes 995336 | tf_op jit(solution)/shard_map/ppermute | solution.py:472
  26.6 9.9 %collective-permute-start.1 = (bf16[1296,128]{1,0:T(8,128)(2,1)S(1)}, bf16[1296,128]{1,0:T(8,128)(2,1)S(1)}, u32[]{:S(2)}, u32[]{:S(2)}) collective-permute-start(bf16[1296,128]{1,0:T(8,128)(2,1)S(1)} %get-tuple-element.48.kv.refs_0_), channel_id=1, source_target_pairs={{0,1},{1,2},{2,3},{3,0},{8,11},{9,8},{10,9},{11,10},{4,5},{5,6},{6... | collective-permute-start | bytes 995336 | tf_op jit(solution)/shard_map/ppermute | solution.py:468
  28.2 10.0 %collective-permute-start.3 = (bf16[1296,128]{1,0:T(8,128)(2,1)S(1)}, bf16[1296,128]{1,0:T(8,128)(2,1)S(1)}, u32[]{:S(2)}, u32[]{:S(2)}) collective-permute-start(bf16[1296,128]{1,0:T(8,128)(2,1)S(1)} %get-tuple-element.48.kv.refs_0_), channel_id=1, source_target_pairs={{0,3},{1,0},{2,1},{3,2},{8,9},{9,10},{10,11},{11,8},{4,7},{5,4},{6... | collective-permute-start | bytes 995336 | tf_op jit(solution)/shard_map/ppermute | solution.py:468
  36.6 8.6 %collective-permute-start.2 = (bf16[1296,128]{1,0:T(8,128)(2,1)S(1)}, bf16[1296,128]{1,0:T(8,128)(2,1)S(1)}, u32[]{:S(2)}, u32[]{:S(2)}) collective-permute-start(bf16[1296,128]{1,0:T(8,128)(2,1)S(1)} %collective-permute-done.1.kv1.refs_0_), channel_id=1, source_target_pairs={{0,1},{1,2},{2,3},{3,0},{8,11},{9,8},{10,9},{11,10},{4,5},{5,6},{6... | collective-permute-start | bytes 995336 | tf_op jit(solution)/shard_map/ppermute | solution.py:468
  48.6 1.6 %collective-permute-start.4 = (f32[3,2,1024]{2,1,0:T(2,128)S(1)}, f32[3,2,1024]{2,1,0:T(2,128)S(1)}, u32[]{:S(2)}, u32[]{:S(2)}) collective-permute-start(f32[3,2,1024]{2,1,0:T(2,128)S(1)} %get-tuple-element.64.refs_7_), channel_id=1, source_target_pairs={{0,8},{8,0},{1,9},{9,1},{2,10},{10,2},{3,11},{11,3},{4,12},{12,4},... | collective-permute-start | bytes 73736 | tf_op jit(solution)/shard_map/ppermute | solution.py:472
  54.8 8.4 %collective-permute-start.6 = (bf16[1280,128]{1,0:T(8,128)(2,1)S(1)}, bf16[1280,128]{1,0:T(8,128)(2,1)S(1)}, u32[]{:S(2)}, u32[]{:S(2)}) collective-permute-start(bf16[1280,128]{1,0:T(8,128)(2,1)S(1)} %get-tuple-element.79), channel_id=1, source_target_pairs={{0,1},{1,2},{2,3},{3,0},{8,11},{9,8},{10,9},{11,10},{4,5},{5,6},{6... | collective-permute-start | bytes 983048 | tf_op jit(solution)/shard_map/ppermute | solution.py:468
  60.3 9.9 %collective-permute-start.5 = (bf16[1280,128]{1,0:T(8,128)(2,1)S(1)}, bf16[1280,128]{1,0:T(8,128)(2,1)S(1)}, u32[]{:S(2)}, u32[]{:S(2)}) collective-permute-start(bf16[1280,128]{1,0:T(8,128)(2,1)S(1)} %get-tuple-element.72), channel_id=1, source_target_pairs={{0,3},{1,0},{2,1},{3,2},{8,9},{9,10},{10,11},{11,8},{4,7},{5,4},{6... | collective-permute-start | bytes 983048 | tf_op jit(solution)/shard_map/ppermute | solution.py:468
  67.9 8.4 %collective-permute-start.8 = (bf16[1280,128]{1,0:T(8,128)(2,1)S(1)}, bf16[1280,128]{1,0:T(8,128)(2,1)S(1)}, u32[]{:S(2)}, u32[]{:S(2)}) collective-permute-start(bf16[1280,128]{1,0:T(8,128)(2,1)S(1)} %get-tuple-element.90), channel_id=1, source_target_pairs={{0,1},{1,2},{2,3},{3,0},{8,11},{9,8},{10,9},{11,10},{4,5},{5,6},{6... | collective-permute-start | bytes 983048 | tf_op jit(solution)/shard_map/ppermute | solution.py:468
  70.2 3.0 %collective-permute-start.7 = (bf16[640,128]{1,0:T(8,128)(2,1)S(1)}, bf16[640,128]{1,0:T(8,128)(2,1)S(1)}, u32[]{:S(2)}, u32[]{:S(2)}) collective-permute-start(bf16[640,128]{1,0:T(8,128)(2,1)S(1)} %get-tuple-element.87), channel_id=1, source_target_pairs={{0,8},{8,0},{1,9},{9,1},{2,10},{10,2},{3,11},{11,3},{4,12},{12,4},... | collective-permute-start | bytes 491528 | tf_op jit(solution)/shard_map/ppermute | solution.py:472
